TPU v7x, 32 devices: a whole 2x2x4 slice. The times are simulated.
32 devices in a mesh: blk: 4 (over y, x), grp: 8 (over z, core).
Axes of the slice: x: 2, y: 2, z: 4, core: 2. Of those that a mesh axis runs over, the one named last changes fastest.
Arguments:
- images: bfloat16 [2048, 1152], P(('blk', 'grp')), may hold values from -6 to 6
- captions: bfloat16 [2048, 1152], P(('blk', 'grp')), may hold values from -6 to 6
- image_head: bfloat16 [1152, 1152], replicated, may hold values from -0.1875 to 0.1875
- text_head: bfloat16 [1152, 1152], replicated, may hold values from -0.1875 to 0.1875
Outputs:
- grad_images: bfloat16 [2048, 1152], P(('blk', 'grp'))
- grad_captions: bfloat16 [2048, 1152], P(('blk', 'grp'))
- grad_image_head: float32 [1152, 1152], P('grp')
- grad_text_head: float32 [1152, 1152], P('grp')
All inputs are finite; a program needn't handle non-finite values.
Results may differ from a plain program's by a relative error of at most 0.013.
Values may be sent and summed in bfloat16 or wider, within the bound.
No kernel may reach another device: no remote copies, remote signals or barrier semaphores. Data moves between devices by JAX's collectives and lax.ppermute only.
A program may use at most 128 MiB of HBM per device.

v0:
```python
import jax
import jax.numpy as jnp
from jax import lax
from jax.sharding import PartitionSpec as P

logit_scale = 32.0
logit_bias = -3.0
epsilon = 1e-06


def shifted(array, axis, by):
    count = lax.axis_size(axis)
    return lax.ppermute(array, axis, [(i, (i + by) % count) for i in range(count)])


def project(features, weight):
    before = jnp.dot(features, weight, preferred_element_type=jnp.float32)
    inverse = lax.rsqrt(jnp.sum(before * before, axis=1, keepdims=True) + epsilon)
    return (before * inverse, inverse)


def unproject(grad_unit, unit, inverse):
    inner_sum = jnp.sum(unit * grad_unit, axis=1, keepdims=True)
    return (inverse * (grad_unit - unit * inner_sum)).astype(jnp.bfloat16)


def pair_weights(rows_low, row_ids, cols_low, col_ids):
    logits = (
        logit_scale
        * lax.dot_general(
            rows_low, cols_low, (((1,), (1,)), ((), ())), preferred_element_type=jnp.float32
        )
        + logit_bias
    )
    label_sign = jnp.where(
        row_ids[:, None] == col_ids[None, :], jnp.float32(1.0), jnp.float32(-1.0)
    )
    return (-label_sign * jax.nn.sigmoid(-label_sign * logits)).astype(jnp.bfloat16)


def tile(image_block, image_ids, text_block, text_ids):
    weights_low = pair_weights(image_block, image_ids, text_block, text_ids)
    image_part = logit_scale * jnp.dot(weights_low, text_block, preferred_element_type=jnp.float32)
    text_part = logit_scale * lax.dot_general(
        weights_low, image_block, (((0,), (0,)), ((), ())), preferred_element_type=jnp.float32
    )
    return (image_part, text_part)


def per_device(images, captions, image_head, text_head):
    members = lax.axis_size("grp")
    groups = lax.axis_size("blk")
    blk_pos = lax.axis_index("blk")
    grp_pos = lax.axis_index("grp")
    local_rows = images.shape[0]
    width = images.shape[1]
    image_unit, image_inverse = project(images, image_head)
    text_unit, text_inverse = project(captions, text_head)
    image_low = image_unit.astype(jnp.bfloat16)
    text_low = text_unit.astype(jnp.bfloat16)

    def column_ids(local_index):
        return (
            local_index // local_rows * members + grp_pos
        ) * local_rows + local_index % local_rows

    text_block = lax.all_gather(text_low, "grp", axis=0, tiled=True)
    group_rows = text_block.shape[0]
    text_ids = blk_pos * group_rows + lax.iota(jnp.int32, group_rows)
    zero_text = jnp.zeros((group_rows, width), jnp.float32)

    def block_ids(section_index):
        anchor = (blk_pos - section_index) % groups
        return (anchor, column_ids(anchor * local_rows + lax.iota(jnp.int32, local_rows)))

    def collect_step(section_index, current, buffer, text_total):
        anchor, ids = block_ids(section_index)
        image_part, text_part = tile(current, ids, text_block, text_ids)
        buffer = lax.dynamic_update_slice_in_dim(buffer, image_part, anchor * local_rows, 0)
        return (buffer, text_total + text_part)

    def advance_collect(section_index, loop_carry):
        current, buffer, text_total = loop_carry
        buffer, text_total = collect_step(section_index, current, buffer, text_total)
        current = shifted(current, "blk", 1)
        return (current, buffer, text_total)

    zero_buffer = jnp.zeros((groups * local_rows, width), jnp.float32)
    current, buffer, text_total = lax.fori_loop(
        0, groups - 1, advance_collect, (image_low, zero_buffer, zero_text)
    )
    buffer, text_total = collect_step(groups - 1, current, buffer, text_total)
    grad_image_unit = lax.psum_scatter(buffer, "blk", scatter_dimension=0, tiled=True)
    grad_text_unit = lax.psum_scatter(text_total, "grp", scatter_dimension=0, tiled=True)
    image_back = unproject(grad_image_unit, image_unit, image_inverse)
    text_back = unproject(grad_text_unit, text_unit, text_inverse)
    grad_images = lax.dot_general(
        image_back, image_head, (((1,), (1,)), ((), ())), preferred_element_type=jnp.float32
    ).astype(jnp.bfloat16)
    grad_captions = lax.dot_general(
        text_back, text_head, (((1,), (1,)), ((), ())), preferred_element_type=jnp.float32
    ).astype(jnp.bfloat16)
    image_terms = lax.dot_general(
        images, image_back, (((0,), (0,)), ((), ())), preferred_element_type=jnp.float32
    )
    text_terms = lax.dot_general(
        captions, text_back, (((0,), (0,)), ((), ())), preferred_element_type=jnp.float32
    )
    image_share, text_share = (
        lax.psum_scatter(
            image_terms.astype(jnp.bfloat16), "grp", scatter_dimension=0, tiled=True
        ).astype(jnp.float32),
        lax.psum_scatter(
            text_terms.astype(jnp.bfloat16), "grp", scatter_dimension=0, tiled=True
        ).astype(jnp.float32),
    )
    grad_image_head, grad_text_head = (
        lax.psum(image_share.astype(jnp.bfloat16), "blk").astype(jnp.float32),
        lax.psum(text_share.astype(jnp.bfloat16), "blk").astype(jnp.float32),
    )
    return (grad_images, grad_captions, grad_image_head, grad_text_head)


def solution(mesh):
    return jax.shard_map(
        per_device,
        mesh=mesh,
        in_specs=(P(("blk", "grp"), None), P(("blk", "grp"), None), P(), P()),
        out_specs=(
            P(("blk", "grp"), None),
            P(("blk", "grp"), None),
            P("grp", None),
            P("grp", None),
        ),
        check_vma=False,
    )
```

profile of v0, /device:TPU:0, one launch (start us, length us, event | category | flops | bytes accessed | tf_op | source)
XLA Modules:
  0.0 278.3 jit_solution(7320121568543798036)
XLA Ops:
  7.2 2.7 multiply_reduce_fusion.2
  12.2 24.1 %all-gather.2.cloned.1.call-done = bf16[512,1152]{1,0:T(8,128)(2,1)} async-done(((bf16[64,1152]{1,0:T(8,128)(2,1)}), bf16[512,1152]{1,0:T(8,128)(2,1)}) %all-gather.2.cloned.1.call-update) | async-done | bytes 1179664 | tf_op jit(solution)/shard_map/all_gather | solution.py:67
  37.3 24.1 %while.21 = (s32[]{:T(128)}, bf16[64,1152]{1,0:T(8,128)(2,1)S(1)}, f32[256,1152]{1,0:T(8,128)}, f32[512,1152]{1,0:T(8,128)}, s32[]{:T(128)}, /*index=5*/s32[]{:T...) while((s32[]{:T(128)}, bf16[64,1152]{1,0:T(8,128)(2,1)S(1)}, ...), condition=%wide.region_3.4_spmd.clone, body=%wide.region_2.3_spmd.clone.sunk | while | flops 228698128 | bytes 13472650 | solution.py:89
  39.4 1.8 fusion.67
  41.2 1.9 fusion.69
  46.3 1.8 fusion.67
  48.1 3.7 %fusion.69 = f32[512,1152]{1,0:T(8,128)} fusion(bf16[64,512]{1,0:T(8,128)(2,1)S(1)} %fusion.67, bf16[64,1152]{1,0:T(8,128)(2,1)S(1)} %copy.22, f32[512,1152]{1,0:T(8,128)} %get-tuple-element.367, pred[]{:T(512)S(6)} %compare.35), kind=kOutput, calls=%fused_computation.2.clone.1 | convolution fusion | flops 77266944 | bytes 4931585 | tf_op jit(solution)/shard_map/while/body/eval_jaxpr/dot_general | solution.py:44
  56.8 3.7 %fusion.69 = f32[512,1152]{1,0:T(8,128)} fusion(bf16[64,512]{1,0:T(8,128)(2,1)S(1)} %fusion.67, bf16[64,1152]{1,0:T(8,128)(2,1)S(1)} %copy.22, f32[512,1152]{1,0:T(8,128)} %get-tuple-element.367, pred[]{:T(512)S(6)} %compare.35), kind=kOutput, calls=%fused_computation.2.clone.1 | convolution fusion | flops 77266944 | bytes 4931585 | tf_op jit(solution)/shard_map/while/body/eval_jaxpr/dot_general | solution.py:44
  61.5 1.8 fusion.24
  63.3 2.3 fusion.16
  65.7 3.6 %fusion.15 = f32[512,1152]{1,0:T(8,128)} fusion(f32[512,1152]{1,0:T(8,128)} %get-tuple-element.240, bf16[64,512]{1,0:T(8,128)(2,1)S(1)} %fusion.24, bf16[64,1152]{1,0:T(8,128)(2,1)S(1)} %get-tuple-element.239), kind=kOutput, calls=%fused_computation.26 | convolution fusion | flops 76677120 | bytes 4931584 | tf_op jit(solution)/shard_map/dot_general | solution.py:44
  69.4 23.8 %reduce-scatter.9.cloned.1.call-done = f32[64,1152]{1,0:T(8,128)} async-done(((f32[256,1152]{1,0:T(8,128)}), f32[64,1152]{1,0:T(8,128)}) %reduce-scatter.9.cloned.1.call-update) | async-done | bytes 294928 | tf_op jit(solution)/shard_map/reduce_scatter | solution.py:93
  95.4 2.4 fusion.13
  97.8 5.2 %copy.12 = bf16[1152,1152]{1,0:T(8,128)(2,1)} copy(bf16[1152,1152]{0,1:T(8,128)(2,1)} %fusion.13) | data formatting | bytes 5308416
  103.1 28.6 %reduce-scatter.11.cloned.1.call-done = f32[64,1152]{1,0:T(8,128)} async-done(((f32[512,1152]{1,0:T(8,128)}), f32[64,1152]{1,0:T(8,128)}) %reduce-scatter.11.cloned.1.call-update) | async-done | bytes 294928 | tf_op jit(solution)/shard_map/reduce_scatter | solution.py:94
  134.0 2.4 fusion.14
  136.3 5.2 %copy.14 = bf16[1152,1152]{1,0:T(8,128)(2,1)} copy(bf16[1152,1152]{0,1:T(8,128)(2,1)} %fusion.14) | data formatting | bytes 5308416
  141.7 29.3 %reduce-scatter.13.cloned.1.call-done = bf16[144,1152]{1,0:T(8,128)(2,1)} async-done(((bf16[1152,1152]{1,0:T(8,128)(2,1)}), bf16[144,1152]{1,0:T(8,128)(2,1)}) %reduce-scatter.13.cloned.1.call-update) | async-done | bytes 331792
  170.9 2.0 copy.13
  172.9 37.0 %reduce-scatter.15.cloned.1.call-done = bf16[144,1152]{1,0:T(8,128)(2,1)} async-done(((bf16[1152,1152]{1,0:T(8,128)(2,1)}), bf16[144,1152]{1,0:T(8,128)(2,1)}) %reduce-scatter.15.cloned.1.call-update) | async-done | bytes 331792
  210.0 2.0 copy.15
  215.4 51.8 %all-reduce.3.cloned.1.call-done = (bf16[144,1152]{0,1:T(8,128)(2,1)}, bf16[144,1152]{0,1:T(8,128)(2,1)}) async-done(((bf16[144,1152]{0,1:T(8,128)(2,1)}, bf16[144,1152]{0,1:T(8,128)(2,1)}), (bf16[144,1152]{0,1:T(8,128)(2,1)}, bf16[144,1152]{0,1:T(8,128)(2,1)})) %all-reduce.3.cloned.1.call-update) | async-done | bytes 663568 | tf_op jit(solution)/shard_map/psum | solution.py:118
  267.2 2.1 copy.10
  269.3 2.1 copy.11
  (62 shorter events, 22.6 us)
Async XLA Ops:
  7.2 4.2 %copy-start = (bf16[1152,1152]{1,0:T(8,128)(2,1)S(1)}, bf16[1152,1152]{1,0:T(8,128)(2,1)}, u32[]{:S(2)}) copy-start(bf16[1152,1152]{1,0:T(8,128)(2,1)} %param.8) | copy-start | bytes 7962628
  7.2 4.2 %copy-start.3 = (bf16[64,1152]{1,0:T(8,128)(2,1)S(1)}, bf16[64,1152]{1,0:T(8,128)(2,1)}, u32[]{:S(2)}) copy-start(bf16[64,1152]{1,0:T(8,128)(2,1)} %param.6) | copy-start | bytes 442372
  7.2 29.0 %all-gather.2.cloned.1.call-start = ((), (), s32[]{:S(2)}) async-start(), calls=%async_computation.4 | async-start | bytes 1327104 | tf_op jit(solution)/shard_map/all_gather | solution.py:67
  10.7 82.4 %reduce-scatter.9.cloned.1.call-start = ((), (), s32[]{:S(2)}) async-start(), calls=%async_computation.5 | async-start | bytes 1474560 | tf_op jit(solution)/shard_map/reduce_scatter | solution.py:93
  37.3 6.9 %collective-permute-start = (bf16[64,1152]{1,0:T(8,128)(2,1)S(1)}, bf16[64,1152]{1,0:T(8,128)(2,1)S(1)}, u32[]{:S(2)}, u32[]{:S(2)}) collective-permute-start(bf16[64,1152]{1,0:T(8,128)(2,1)S(1)} %copy.22), channel_id=1, source_target_pairs={{0,8},{8,16},{16,24},{24,0},{1,9},{9,17},{17,25},{25,1},{2,10},{10... | collective-permute-start | bytes 442376 | tf_op jit(solution)/shard_map/while/body/eval_jaxpr/ppermute | solution.py:13
  41.2 1.9 copy-start.1
  44.3 8.5 %collective-permute-start = (bf16[64,1152]{1,0:T(8,128)(2,1)S(1)}, bf16[64,1152]{1,0:T(8,128)(2,1)S(1)}, u32[]{:S(2)}, u32[]{:S(2)}) collective-permute-start(bf16[64,1152]{1,0:T(8,128)(2,1)S(1)} %copy.22), channel_id=1, source_target_pairs={{0,8},{8,16},{16,24},{24,0},{1,9},{9,17},{17,25},{25,1},{2,10},{10... | collective-permute-start | bytes 442376 | tf_op jit(solution)/shard_map/while/body/eval_jaxpr/ppermute | solution.py:13
  48.1 3.7 %copy-start.1 = (bf16[512,1152]{1,0:T(8,128)(2,1)S(1)}, bf16[512,1152]{1,0:T(8,128)(2,1)}, u32[]{:S(2)}) copy-start(bf16[512,1152]{1,0:T(8,128)(2,1)} %get-tuple-element.384) | copy-start | bytes 3538948 | tf_op jit(solution)/shard_map/while
  52.8 8.6 %collective-permute-start = (bf16[64,1152]{1,0:T(8,128)(2,1)S(1)}, bf16[64,1152]{1,0:T(8,128)(2,1)S(1)}, u32[]{:S(2)}, u32[]{:S(2)}) collective-permute-start(bf16[64,1152]{1,0:T(8,128)(2,1)S(1)} %copy.22), channel_id=1, source_target_pairs={{0,8},{8,16},{16,24},{24,0},{1,9},{9,17},{17,25},{25,1},{2,10},{10... | collective-permute-start | bytes 442376 | tf_op jit(solution)/shard_map/while/body/eval_jaxpr/ppermute | solution.py:13
  56.7 3.7 %copy-start.1 = (bf16[512,1152]{1,0:T(8,128)(2,1)S(1)}, bf16[512,1152]{1,0:T(8,128)(2,1)}, u32[]{:S(2)}) copy-start(bf16[512,1152]{1,0:T(8,128)(2,1)} %get-tuple-element.384) | copy-start | bytes 3538948 | tf_op jit(solution)/shard_map/while
  65.6 66.1 %reduce-scatter.11.cloned.1.call-start = ((), (), s32[]{:S(2)}) async-start(), calls=%async_computation.6 | async-start | bytes 2654208 | tf_op jit(solution)/shard_map/reduce_scatter | solution.py:94
  69.3 26.1 %copy-start.4 = (bf16[64,1152]{1,0:T(8,128)(2,1)S(1)}, bf16[64,1152]{1,0:T(8,128)(2,1)}, u32[]{:S(2)}) copy-start(bf16[64,1152]{1,0:T(8,128)(2,1)} %param.6) | copy-start | bytes 442372
  69.3 101.6 %reduce-scatter.13.cloned.1.call-start = ((), (), s32[]{:S(2)}) async-start(), calls=%async_computation.7 | async-start | bytes 2985984
  103.0 30.9 %copy-start.5 = (bf16[64,1152]{1,0:T(8,128)(2,1)S(1)}, bf16[64,1152]{1,0:T(8,128)(2,1)}, u32[]{:S(2)}) copy-start(bf16[64,1152]{1,0:T(8,128)(2,1)} %param.7) | copy-start | bytes 442372
  103.1 106.9 %reduce-scatter.15.cloned.1.call-start = ((), (), s32[]{:S(2)}) async-start(), calls=%async_computation.8 | async-start | bytes 2985984
  141.6 125.6 %all-reduce.3.cloned.1.call-start = ((), (), s32[]{:S(2)}) async-start(), calls=%async_computation.9 | async-start | bytes 2359296 | tf_op jit(solution)/shard_map/psum | solution.py:118
  212.0 1.8 copy-start.2
Sparse Core Ops, SparseCore 0:
  10.8 25.3 all-gather.1
  65.8 27.3 reduce-scatter.8
  95.5 36.2 reduce-scatter.10
  133.9 37.0 reduce-scatter.12
  173.1 36.8 reduce-scatter.14
  213.5 53.6 all-reduce.2
where the time goes:
time: 279 us; the launch traced here: 278 us
  waiting for transfers between devices  195 us (70%)
  matrix products  36.8 us (13%)
  local copies, waits for them, and re-layouts  20.1 us (7%)
  between operations  14.3 us (5%)
  other arithmetic  7.52 us (3%)
  starting transfers between devices  4.81 us (2%)
    unnamed x8, waiting for transfers between devices  66.4 us
    psum x1, waiting for transfers between devices, per_device(): lax.psum(image_share.astype(jnp.bfloat16), 'blk').astype(jnp.float32)  51.8 us
    reduce_scatter x1, waiting for transfers between devices, per_device(): lax.psum_scatter(text_total, 'grp', scatter_dimension=0, tiled=True)  28.6 us
    all_gather x1, waiting for transfers between devices, per_device(): text_block = lax.all_gather(text_low, 'grp', axis=0, tiled=True)  24.1 us
    reduce_scatter x1, waiting for transfers between devices, per_device(): lax.psum_scatter(buffer, 'blk', scatter_dimension=0, tiled=True)  23.8 us
    unnamed x16, local copies, waits for them, and re-layouts  18.9 us
    dot_general x4, matrix products, tile(): lax.dot_general(weights_low, image_block, (((0,), (0,)), ((), ())), prefe...  12.9 us
    dot_general x4, matrix products, pair_weights(): lax.dot_general(rows_low, cols_low, (((1,), (1,)), ((), ())), preferred_e...  7.13 us
  transfers between devices with their start and end apart: 9, of which 7 were waited for; matrix products, arithmetic and copies ran while one was open for 18% of the time, Pallas kernels for 0%

commit v1 on v0

v1 whole, which is shorter than its diff:
```python
import jax
import jax.numpy as jnp
from jax import lax
from jax.sharding import PartitionSpec as P

logit_scale = 32.0
logit_bias = -3.0
epsilon = 1e-06
low = jnp.bfloat16
wide = jnp.float32


def dot(a, b, a_dim, b_dim):
    return lax.dot_general(a, b, (((a_dim,), (b_dim,)), ((), ())), preferred_element_type=wide)


def project(features, weight):
    before = dot(features, weight, 1, 0)
    inverse = lax.rsqrt(jnp.sum(before * before, axis=1, keepdims=True) + epsilon)
    return (before * inverse, inverse)


def unproject(grad_unit, unit, inverse):
    inner_sum = jnp.sum(unit * grad_unit, axis=1, keepdims=True)
    return (inverse * (grad_unit - unit * inner_sum)).astype(low)


def pair_weights(rows_low, cols_low, own):
    logits = logit_scale * dot(rows_low, cols_low, 1, 1) + logit_bias
    if not own:
        return jax.nn.sigmoid(logits).astype(low)
    row_ids = lax.broadcasted_iota(jnp.int32, logits.shape, 0)
    col_ids = lax.broadcasted_iota(jnp.int32, logits.shape, 1)
    label_sign = jnp.where(row_ids == col_ids, wide(1.0), wide(-1.0))
    return (-label_sign * jax.nn.sigmoid(-label_sign * logits)).astype(low)


def per_device(images, captions, image_head, text_head):
    groups = lax.axis_size("blk")
    members = lax.axis_size("grp")
    layers = members // 2
    rows, width = images.shape
    blk_pos = lax.axis_index("blk")
    grp_pos = lax.axis_index("grp")
    layer_pos, core_pos = grp_pos // 2, grp_pos % 2

    def over_blk(array, by):
        return lax.ppermute(array, "blk", [(i, i ^ by) for i in range(groups)])

    def over_layer(array, by):
        return lax.ppermute(array, "grp", [(i, i ^ (2 * by)) for i in range(members)])

    def over_core(array):
        return lax.ppermute(array, "grp", [(i, i ^ 1) for i in range(members)])

    def gather_plane(array):
        mine = jnp.concatenate([array] + [over_blk(array, k) for k in range(1, groups)])
        return jnp.concatenate([mine, over_core(mine)])

    image_blocks = [images] + [over_layer(images, k) for k in range(1, layers)]
    caption_plane = gather_plane(captions)
    image_plane = gather_plane(images)

    share = width // members
    part = -(-share // groups)
    padded = -(-part // 16) * 16
    slot = lax.broadcasted_iota(jnp.int32, (layers * padded, width), 0)
    column = lax.broadcasted_iota(jnp.int32, (layers * padded, width), 1)
    layer = (slot // padded) ^ layer_pos
    within = blk_pos * part + slot % padded
    wanted = (layer * 2 + core_pos) * share + within
    valid = (slot % padded < part) & (within < share)
    choose = ((column == wanted) & valid).astype(low)
    image_columns = dot(choose, image_plane, 1, 1).astype(low)
    caption_columns = dot(choose, caption_plane, 1, 1).astype(low)

    text_unit, text_inverse = project(caption_plane, text_head)
    text_low = text_unit.astype(low)
    weights, image_lows, image_total = [], [], None
    for k in range(layers):
        unit, inverse = project(image_blocks[k], image_head)
        unit_low = unit.astype(low)
        pair_weight = pair_weights(unit_low, text_low, k == 0)
        image_part = dot(pair_weight, text_low, 1, 0)
        if k == 0:
            image_unit, image_inverse = unit, inverse
            image_total = image_part
        else:
            image_total = image_total + over_layer(image_part.astype(low), k).astype(wide)
        weights.append(pair_weight)
        image_lows.append(unit_low)
    text_part = dot(jnp.concatenate(weights), jnp.concatenate(image_lows), 0, 0)
    half = groups * rows
    text_half = text_part[:half] + over_core(text_part[half:].astype(low)).astype(wide)
    text_total = text_half[:rows]
    for k in range(1, groups):
        block = text_half[k * rows : (k + 1) * rows]
        text_total = text_total + over_blk(block.astype(low), k).astype(wide)

    image_back = unproject(logit_scale * image_total, image_unit, image_inverse)
    text_back = unproject(logit_scale * text_total, text_unit[:rows], text_inverse[:rows])
    grad_images = dot(image_back, image_head, 1, 1).astype(low)
    grad_captions = dot(text_back, text_head, 1, 1).astype(low)

    row_of = lax.broadcasted_iota(jnp.int32, (share, groups * padded), 0)
    slot_of = lax.broadcasted_iota(jnp.int32, (share, groups * padded), 1)
    source = (slot_of // padded) ^ blk_pos
    place = ((row_of // part == source) & (row_of % part == slot_of % padded)).astype(low)

    def head_gradient(columns, back):
        terms = dot(columns, gather_plane(back), 1, 0)
        total = terms[:padded]
        for k in range(1, layers):
            block = terms[k * padded : (k + 1) * padded]
            total = total + over_layer(block.astype(low), k).astype(wide)
        total = total.astype(low)
        parts = jnp.concatenate([total] + [over_blk(total, k) for k in range(1, groups)])
        return dot(place, parts, 1, 0)

    grad_image_head = head_gradient(image_columns, image_back)
    grad_text_head = head_gradient(caption_columns, text_back)
    return (grad_images, grad_captions, grad_image_head, grad_text_head)


def solution(mesh):
    return jax.shard_map(
        per_device,
        mesh=mesh,
        in_specs=(P(("blk", "grp"), None), P(("blk", "grp"), None), P(), P()),
        out_specs=(
            P(("blk", "grp"), None),
            P(("blk", "grp"), None),
            P("grp", None),
            P("grp", None),
        ),
        check_vma=False,
    )
```

time: 279 us -> 124 us (0.44)
  waiting for transfers between devices: 195 us -> 34.9 us
  starting transfers between devices: 4.81 us -> 42.8 us
  between operations: 14.3 us -> 1.2 us
  matrix products: 36.8 us -> 25.3 us
  local copies, waits for them, and re-layouts: 20.1 us -> 11.1 us
    unnamed x8 -> x0, waiting for transfers between devices: 66.4 us -> none
    reduce_scatter x2 -> x0, waiting for transfers between devices: 52.4 us -> none  [the longest x1 28.6 us: per_device(): lax.psum_scatter(text_total, 'grp', scatter_dimension=0, tiled=True)]
    psum x1 -> x0, waiting for transfers between devices: 51.8 us -> none  [per_device(): lax.psum(image_share.astype(jnp.bfloat16), 'blk').astype(jnp.float32)]
    ppermute x3 -> x38, starting transfers between devices: 4.56 us -> 42.8 us  [the longest x21 26.3 us: over_blk(): return lax.ppermute(array, 'blk', [(i, i ^ by) for i in range(groups)])]
    ppermute x3 -> x38, waiting for transfers between devices: 0.1 us -> 34.9 us  [the longest x12 18.9 us: over_layer(): return lax.ppermute(array, 'grp', [(i, i ^ 2 * by) for i in range(members)])]
    all_gather x1 -> x0, waiting for transfers between devices: 24.1 us -> none  [per_device(): text_block = lax.all_gather(text_low, 'grp', axis=0, tiled=True)]
    dot_general x18 -> x20, matrix products: 36.8 us -> 25.3 us  [dot(): lax.dot_general(a, b, (((a_dim,), (b_dim,)), ((), ())), preferred_element...]
    unnamed x16 -> x54, local copies, waits for them, and re-layouts: 18.9 us -> 8.16 us
  transfers between devices with their start and end apart: 9 -> 38, of which waited for: 7 -> 13; matrix products, arithmetic and copies ran while one was open for 18% -> 34% of each run, Pallas kernels for 0% -> 0%
where the time goes in v1:
time: 124 us
  starting transfers between devices  42.8 us (35%)
  waiting for transfers between devices  34.9 us (28%)
  matrix products  25.3 us (20%)
  local copies, waits for them, and re-layouts  11.1 us (9%)
  other arithmetic  8.68 us (7%)
    ppermute x21, starting transfers between devices, over_blk(): return lax.ppermute(array, 'blk', [(i, i ^ by) for i in range(groups)])  26.3 us
    dot_general x20, matrix products, dot(): lax.dot_general(a, b, (((a_dim,), (b_dim,)), ((), ())), preferred_element...  25.3 us
    ppermute x12, waiting for transfers between devices, over_layer(): return lax.ppermute(array, 'grp', [(i, i ^ 2 * by) for i in range(members)])  18.9 us
    ppermute x21, waiting for transfers between devices, over_blk(): return lax.ppermute(array, 'blk', [(i, i ^ by) for i in range(groups)])  15.9 us
    ppermute x12, starting transfers between devices, over_layer(): return lax.ppermute(array, 'grp', [(i, i ^ 2 * by) for i in range(members)])  15.7 us
    unnamed x54, local copies, waits for them, and re-layouts  8.16 us
  transfers between devices with their start and end apart: 38, of which 13 were waited for; matrix products, arithmetic and copies ran while one was open for 34% of the time, Pallas kernels for 0%

profile of v1, /device:TPU:0, one launch (start us, length us, event | category | flops | bytes accessed | tf_op | source)
XLA Modules:
  0.0 124.0 jit_solution(17186509965100893599)
XLA Ops:
  0.6 4.0 %collective-permute-start.2 = (bf16[64,1152]{1,0:T(8,128)(2,1)}, bf16[64,1152]{1,0:T(8,128)(2,1)S(1)}, u32[]{:S(2)}, u32[]{:S(2)}) collective-permute-start(bf16[64,1152]{1,0:T(8,128)(2,1)} %param.5), channel_id=1, source_target_pairs={{0,24},{8,16},{16,8},{24,0},{1,25},{9,17},{17,9},{25,1},{2,26},{10... | collective-permute-start | bytes 442376 | tf_op jit(solution)/shard_map/ppermute | solution.py:48
  5.3 2.8 %collective-permute-start.16 = (bf16[64,1152]{1,0:T(8,128)(2,1)}, bf16[64,1152]{1,0:T(8,128)(2,1)S(1)}, u32[]{:S(2)}, u32[]{:S(2)}) collective-permute-start(bf16[64,1152]{1,0:T(8,128)(2,1)} %param.4), channel_id=1, source_target_pairs={{0,24},{8,16},{16,8},{24,0},{1,25},{9,17},{17,9},{25,1},{2,26},{10... | collective-permute-start | bytes 442376 | tf_op jit(solution)/shard_map/ppermute | solution.py:48
  8.1 3.6 %collective-permute-start.8 = (bf16[64,1152]{1,0:T(8,128)(2,1)}, bf16[64,1152]{1,0:T(8,128)(2,1)}, u32[]{:S(2)}, u32[]{:S(2)}) collective-permute-start(bf16[64,1152]{1,0:T(8,128)(2,1)} %param.4), channel_id=1, source_target_pairs={{0,6},{1,7},{2,4},{3,5},{4,2},{5,3},{6,0},{7,1},{8,14},{9,15},{10,... | collective-permute-start | bytes 442376 | tf_op jit(solution)/shard_map/ppermute | solution.py:51
  16.6 2.6 %multiply_reduce_fusion.6 = (f32[64]{0:T(128)S(1)}, f32[64,1152]{1,0:T(8,128)S(1)}) fusion(bf16[64,1152]{1,0:T(8,128)(2,1)} %param.4, bf16[1152,1152]{1,0:T(8,128)(2,1)} %param.6), kind=kOutput, calls=%fused_computation.93 | convolution fusion | flops 170016704 | bytes 3096832 | tf_op jit(solution)/shard_map/dot_general | solution.py:14
  21.6 2.7 %multiply_reduce_fusion.3 = (f32[64]{0:T(128)S(1)}, f32[64,1152]{1,0:T(8,128)S(1)}) fusion(bf16[64,1152]{1,0:T(8,128)(2,1)} %collective-permute-done.8, bf16[1152,1152]{1,0:T(8,128)(2,1)} %param.6), kind=kOutput, calls=%fused_computation.88 | convolution fusion | flops 170016704 | bytes 3096832 | tf_op jit(solution)/shard_map/dot_general | solution.py:14
  26.5 5.6 %collective-permute-done.6 = bf16[64,1152]{1,0:T(8,128)(2,1)S(1)} collective-permute-done((bf16[64,1152]{1,0:T(8,128)(2,1)S(1)}, bf16[64,1152]{1,0:T(8,128)(2,1)S(1)}, u32[]{:S(2)}, u32[]{:S(2)}) %collective-permute-start.6) | collective-permute-done | bytes 147488 | tf_op jit(solution)/shard_map/ppermute | solution.py:51
  36.1 1.9 %multiply_reduce_fusion = (f32[512]{0:T(512)S(1)}, f32[512,1152]{1,0:T(8,128)S(1)}) fusion(bf16[512,1152]{1,0:T(8,128)(2,1)S(1)} %constant_dynamic-update-slice_fusion, bf16[1152,1152]{1,0:T(8,128)(2,1)S(1)} %copy-done), kind=kOutput, calls=%fused_computation | convolution fusion | flops 1360133632 | bytes 6195200 | tf_op jit(solution)/shard_map/dot_general | solution.py:14
  42.3 3.4 %collective-permute-start.5 = (bf16[64,1152]{1,0:T(8,128)(2,1)S(1)}, bf16[64,1152]{1,0:T(8,128)(2,1)S(1)}, u32[]{:S(2)}, u32[]{:S(2)}) collective-permute-start(bf16[64,1152]{1,0:T(8,128)(2,1)S(1)} %convolution_convert_fusion.4), channel_id=1, source_target_pairs={{0,2},{1,3},{2,0},{3,1},{4,6},{5,7},{6,4},{7,5},{8,10},{9,11},{10,... | collective-permute-start | bytes 442376 | tf_op jit(solution)/shard_map/ppermute | solution.py:51
  47.0 2.5 %collective-permute-done.9 = bf16[64,1152]{1,0:T(8,128)(2,1)S(1)} collective-permute-done((bf16[64,1152]{1,0:T(8,128)(2,1)S(1)}, bf16[64,1152]{1,0:T(8,128)(2,1)S(1)}, u32[]{:S(2)}, u32[]{:S(2)}) %collective-permute-start.9) | collective-permute-done | bytes 147488 | tf_op jit(solution)/shard_map/ppermute | solution.py:51
  49.6 5.3 %collective-permute-done.7 = bf16[64,1152]{1,0:T(8,128)(2,1)S(1)} collective-permute-done((bf16[64,1152]{1,0:T(8,128)(2,1)S(1)}, bf16[64,1152]{1,0:T(8,128)(2,1)S(1)}, u32[]{:S(2)}, u32[]{:S(2)}) %collective-permute-start.7) | collective-permute-done | bytes 147488 | tf_op jit(solution)/shard_map/ppermute | solution.py:51
  55.4 2.5 %collective-permute-start.20 = (bf16[64,1152]{1,0:T(8,128)(2,1)S(1)}, bf16[64,1152]{1,0:T(8,128)(2,1)S(1)}, u32[]{:S(2)}, u32[]{:S(2)}) collective-permute-start(bf16[64,1152]{1,0:T(8,128)(2,1)S(1)} %get-tuple-element.7), channel_id=1, source_target_pairs={{0,24},{8,16},{16,8},{24,0},{1,25},{9,17},{17,9},{25,1},{2,26},{10... | collective-permute-start | bytes 442376 | tf_op jit(solution)/shard_map/ppermute | solution.py:48
  59.0 1.6 %convolution_convert_fusion.1 = bf16[64,1152]{1,0:T(8,128)(2,1)} fusion(bf16[64,1152]{1,0:T(8,128)(2,1)S(1)} %get-tuple-element.7, bf16[1152,1152]{1,0:T(8,128)(2,1)S(1)} %copy-done.1), kind=kOutput, calls=%fused_computation.2 | convolution fusion | flops 169943040 | bytes 2949120 | tf_op jit(solution)/shard_map/dot_general | solution.py:14
  60.6 2.2 %collective-permute-done.20 = bf16[64,1152]{1,0:T(8,128)(2,1)S(1)} collective-permute-done((bf16[64,1152]{1,0:T(8,128)(2,1)S(1)}, bf16[64,1152]{1,0:T(8,128)(2,1)S(1)}, u32[]{:S(2)}, u32[]{:S(2)}) %collective-permute-start.20) | collective-permute-done | bytes 147488 | tf_op jit(solution)/shard_map/ppermute | solution.py:48
  62.8 2.5 %collective-permute-done.19 = bf16[64,1152]{1,0:T(8,128)(2,1)S(1)} collective-permute-done((bf16[64,1152]{1,0:T(8,128)(2,1)S(1)}, bf16[64,1152]{1,0:T(8,128)(2,1)S(1)}, u32[]{:S(2)}, u32[]{:S(2)}) %collective-permute-start.19) | collective-permute-done | bytes 147488 | tf_op jit(solution)/shard_map/ppermute | solution.py:48
  69.4 3.1 %collective-permute-done.11 = bf16[64,1152]{1,0:T(8,128)(2,1)S(1)} collective-permute-done((bf16[64,1152]{1,0:T(8,128)(2,1)S(1)}, bf16[64,1152]{1,0:T(8,128)(2,1)S(1)}, u32[]{:S(2)}, u32[]{:S(2)}) %collective-permute-start.11) | collective-permute-done | bytes 147488 | tf_op jit(solution)/shard_map/ppermute | solution.py:48
  72.5 3.7 %collective-permute-done.13 = bf16[64,1152]{1,0:T(8,128)(2,1)S(1)} collective-permute-done((bf16[64,1152]{1,0:T(8,128)(2,1)S(1)}, bf16[64,1152]{1,0:T(8,128)(2,1)S(1)}, u32[]{:S(2)}, u32[]{:S(2)}) %collective-permute-start.13) | collective-permute-done | bytes 147488 | tf_op jit(solution)/shard_map/ppermute | solution.py:48
  82.1 1.6 %convolution_convert_fusion = bf16[64,1152]{1,0:T(8,128)(2,1)} fusion(bf16[64,1152]{1,0:T(8,128)(2,1)S(1)} %get-tuple-element.5, bf16[1152,1152]{1,0:T(8,128)(2,1)S(1)} %copy-done), kind=kOutput, calls=%fused_computation.1 | convolution fusion | flops 169943040 | bytes 2949120 | tf_op jit(solution)/shard_map/dot_general | solution.py:14
  84.8 3.7 %fusion.92 = (bf16[192,1152]{1,0:T(8,128)(2,1)}, f32[192,1152]{1,0:T(8,128)}) fusion(bf16[512,1152]{1,0:T(8,128)(2,1)} %copy-done.5, bf16[512,1152]{1,0:T(8,128)(2,1)} %copy-done.7, s32[192]{0:T(256)S(1)} %copy-done.15, s32[192]{0:T(256)S(1)} %get-tuple-element.41, s32[]{:T(128)S(6)} %mul.162, s32[]{:T(128)S(6)} %select_n.57, s32[]{:T(128)S(6)} %select_n.56, ...), kind=kOutput, calls=%fused_computation.163 | convolution fusion | flops 456179712 | bytes 3689868 | tf_op jit(solution)/shard_map/dot_general | solution.py:14
  88.5 1.7 %fusion.91 = (bf16[48,1152]{1,0:T(8,128)(2,1)}, bf16[48,1152]{1,0:T(8,128)(2,1)}, bf16[48,1152]{1,0:T(8,128)(2,1)S(1)}) fusion(bf16[192,1152]{1,0:T(8,128)(2,1)} %get-tuple-element.33), kind=kLoop, calls=%fused_computation.162 | loop fusion | bytes 663552 | tf_op jit(solution)/shard_map/slice | solution.py:114
  91.5 2.2 %collective-permute-start.23 = (bf16[48,1152]{1,0:T(8,128)(2,1)S(1)}, bf16[48,1152]{1,0:T(8,128)(2,1)}, u32[]{:S(2)}, u32[]{:S(2)}) collective-permute-start(bf16[48,1152]{1,0:T(8,128)(2,1)S(1)} %get-tuple-element.20), channel_id=1, source_target_pairs={{0,4},{1,5},{2,6},{3,7},{4,0},{5,1},{6,2},{7,3},{8,12},{9,13},{10,... | collective-permute-start | bytes 331784 | tf_op jit(solution)/shard_map/ppermute | solution.py:51
  96.7 3.5 %fusion.95 = (bf16[192,1152]{1,0:T(8,128)(2,1)S(1)}, f32[192,1152]{1,0:T(8,128)}) fusion(bf16[512,1152]{1,0:T(8,128)(2,1)} %constant_dynamic-update-slice_fusion.15, bf16[512,1152]{1,0:T(8,128)(2,1)} %copy-done.9, s32[192]{0:T(256)S(1)} %copy-done.15, s32[192]{0:T(256)S(1)} %get-tuple-element.41, s32[]{:T(128)S(6)} %mul.162, s32[]{:T(128)S(6)} %select_n.57, ...), kind=kOutput, calls=%fused_computation.164 | convolution fusion | flops 456179712 | bytes 3689868 | tf_op jit(solution)/shard_map/dot_general | solution.py:14
  109.1 5.1 %collective-permute-done.33 = bf16[48,1152]{1,0:T(8,128)(2,1)S(1)} collective-permute-done((bf16[48,1152]{1,0:T(8,128)(2,1)S(1)}, bf16[48,1152]{1,0:T(8,128)(2,1)S(1)}, u32[]{:S(2)}, u32[]{:S(2)}) %collective-permute-start.33) | collective-permute-done | bytes 110624 | tf_op jit(solution)/shard_map/ppermute | solution.py:51
  115.1 1.6 %collective-permute-start.37 = (bf16[48,1152]{1,0:T(8,128)(2,1)S(1)}, bf16[48,1152]{1,0:T(8,128)(2,1)S(1)}, u32[]{:S(2)}, u32[]{:S(2)}) collective-permute-start(bf16[48,1152]{1,0:T(8,128)(2,1)S(1)} %fusion.69), channel_id=1, source_target_pairs={{0,24},{8,16},{16,8},{24,0},{1,25},{9,17},{17,9},{25,1},{2,26},{10... | collective-permute-start | bytes 331784 | tf_op jit(solution)/shard_map/ppermute | solution.py:48
  119.9 2.0 %collective-permute-done.37 = bf16[48,1152]{1,0:T(8,128)(2,1)S(1)} collective-permute-done((bf16[48,1152]{1,0:T(8,128)(2,1)S(1)}, bf16[48,1152]{1,0:T(8,128)(2,1)S(1)}, u32[]{:S(2)}, u32[]{:S(2)}) %collective-permute-start.37) | collective-permute-done | bytes 110624 | tf_op jit(solution)/shard_map/ppermute | solution.py:48
  (162 shorter events, 51.5 us)
Async XLA Ops:
  0.6 23.6 %collective-permute-start.2 = (bf16[64,1152]{1,0:T(8,128)(2,1)}, bf16[64,1152]{1,0:T(8,128)(2,1)S(1)}, u32[]{:S(2)}, u32[]{:S(2)}) collective-permute-start(bf16[64,1152]{1,0:T(8,128)(2,1)} %param.5), channel_id=1, source_target_pairs={{0,24},{8,16},{16,8},{24,0},{1,25},{9,17},{17,9},{25,1},{2,26},{10... | collective-permute-start | bytes 442376 | tf_op jit(solution)/shard_map/ppermute | solution.py:48
  4.6 20.3 %collective-permute-start.1 = (bf16[64,1152]{1,0:T(8,128)(2,1)}, bf16[64,1152]{1,0:T(8,128)(2,1)S(1)}, u32[]{:S(2)}, u32[]{:S(2)}) collective-permute-start(bf16[64,1152]{1,0:T(8,128)(2,1)} %param.5), channel_id=1, source_target_pairs={{0,16},{8,24},{16,0},{24,8},{1,17},{9,25},{17,1},{25,9},{2,18},{10... | collective-permute-start | bytes 442376 | tf_op jit(solution)/shard_map/ppermute | solution.py:48
  5.1 19.8 %collective-permute-start = (bf16[64,1152]{1,0:T(8,128)(2,1)}, bf16[64,1152]{1,0:T(8,128)(2,1)}, u32[]{:S(2)}, u32[]{:S(2)}) collective-permute-start(bf16[64,1152]{1,0:T(8,128)(2,1)} %param.5), channel_id=1, source_target_pairs={{0,8},{8,0},{16,24},{24,16},{1,9},{9,1},{17,25},{25,17},{2,10},{10... | collective-permute-start | bytes 442376 | tf_op jit(solution)/shard_map/ppermute | solution.py:48
  5.3 27.5 %collective-permute-start.16 = (bf16[64,1152]{1,0:T(8,128)(2,1)}, bf16[64,1152]{1,0:T(8,128)(2,1)S(1)}, u32[]{:S(2)}, u32[]{:S(2)}) collective-permute-start(bf16[64,1152]{1,0:T(8,128)(2,1)} %param.4), channel_id=1, source_target_pairs={{0,24},{8,16},{16,8},{24,0},{1,25},{9,17},{17,9},{25,1},{2,26},{10... | collective-permute-start | bytes 442376 | tf_op jit(solution)/shard_map/ppermute | solution.py:48
  8.1 13.0 %collective-permute-start.8 = (bf16[64,1152]{1,0:T(8,128)(2,1)}, bf16[64,1152]{1,0:T(8,128)(2,1)}, u32[]{:S(2)}, u32[]{:S(2)}) collective-permute-start(bf16[64,1152]{1,0:T(8,128)(2,1)} %param.4), channel_id=1, source_target_pairs={{0,6},{1,7},{2,4},{3,5},{4,2},{5,3},{6,0},{7,1},{8,14},{9,15},{10,... | collective-permute-start | bytes 442376 | tf_op jit(solution)/shard_map/ppermute | solution.py:51
  21.1 11.7 %collective-permute-start.15 = (bf16[64,1152]{1,0:T(8,128)(2,1)S(1)}, bf16[64,1152]{1,0:T(8,128)(2,1)S(1)}, u32[]{:S(2)}, u32[]{:S(2)}) collective-permute-start(bf16[64,1152]{1,0:T(8,128)(2,1)S(1)} %copy-done.2), channel_id=1, source_target_pairs={{0,16},{8,24},{16,0},{24,8},{1,17},{9,25},{17,1},{25,9},{2,18},{10... | collective-permute-start | bytes 442376 | tf_op jit(solution)/shard_map/ppermute | solution.py:48
  32.8 14.1 %collective-permute-start.17 = (bf16[256,1152]{1,0:T(8,128)(2,1)S(1)}, bf16[256,1152]{1,0:T(8,128)(2,1)S(1)}, u32[]{:S(2)}, u32[]{:S(2)}) collective-permute-start(bf16[256,1152]{1,0:T(8,128)(2,1)S(1)} %pad_maximum_fusion.1), channel_id=1, source_target_pairs={{0,1},{1,0},{2,3},{3,2},{4,5},{5,4},{6,7},{7,6},{8,9},{9,8},{10,11... | collective-permute-start | bytes 1769480 | tf_op jit(solution)/shard_map/ppermute | solution.py:54
  40.9 8.7 %collective-permute-start.9 = (bf16[64,1152]{1,0:T(8,128)(2,1)S(1)}, bf16[64,1152]{1,0:T(8,128)(2,1)S(1)}, u32[]{:S(2)}, u32[]{:S(2)}) collective-permute-start(bf16[64,1152]{1,0:T(8,128)(2,1)S(1)} %convolution_convert_fusion.2), channel_id=1, source_target_pairs={{0,6},{1,7},{2,4},{3,5},{4,2},{5,3},{6,0},{7,1},{8,14},{9,15},{10,... | collective-permute-start | bytes 442376 | tf_op jit(solution)/shard_map/ppermute | solution.py:51
  42.0 12.9 %collective-permute-start.7 = (bf16[64,1152]{1,0:T(8,128)(2,1)S(1)}, bf16[64,1152]{1,0:T(8,128)(2,1)S(1)}, u32[]{:S(2)}, u32[]{:S(2)}) collective-permute-start(bf16[64,1152]{1,0:T(8,128)(2,1)S(1)} %convolution_convert_fusion.3), channel_id=1, source_target_pairs={{0,4},{1,5},{2,6},{3,7},{4,0},{5,1},{6,2},{7,3},{8,12},{9,13},{10,... | collective-permute-start | bytes 442376 | tf_op jit(solution)/shard_map/ppermute | solution.py:51
  42.3 12.5 %collective-permute-start.5 = (bf16[64,1152]{1,0:T(8,128)(2,1)S(1)}, bf16[64,1152]{1,0:T(8,128)(2,1)S(1)}, u32[]{:S(2)}, u32[]{:S(2)}) collective-permute-start(bf16[64,1152]{1,0:T(8,128)(2,1)S(1)} %convolution_convert_fusion.4), channel_id=1, source_target_pairs={{0,2},{1,3},{2,0},{3,1},{4,6},{5,7},{6,4},{7,5},{8,10},{9,11},{10,... | collective-permute-start | bytes 442376 | tf_op jit(solution)/shard_map/ppermute | solution.py:51
  46.9 18.7 %collective-permute-start.10 = (bf16[256,1152]{1,0:T(8,128)(2,1)S(1)}, bf16[256,1152]{1,0:T(8,128)(2,1)S(1)}, u32[]{:S(2)}, u32[]{:S(2)}) collective-permute-start(bf16[256,1152]{1,0:T(8,128)(2,1)S(1)} %slice.119), channel_id=1, source_target_pairs={{0,1},{1,0},{2,3},{3,2},{4,5},{5,4},{6,7},{7,6},{8,9},{9,8},{10,11... | collective-permute-start | bytes 1769480 | tf_op jit(solution)/shard_map/ppermute | solution.py:54
  65.4 18.2 %collective-permute-start.21 = (bf16[256,1152]{1,0:T(8,128)(2,1)S(1)}, bf16[256,1152]{1,0:T(8,128)(2,1)S(1)}, u32[]{:S(2)}, u32[]{:S(2)}) collective-permute-start(bf16[256,1152]{1,0:T(8,128)(2,1)S(1)} %pad_maximum_fusion.2), channel_id=1, source_target_pairs={{0,1},{1,0},{2,3},{3,2},{4,5},{5,4},{6,7},{7,6},{8,9},{9,8},{10,11... | collective-permute-start | bytes 1769480 | tf_op jit(solution)/shard_map/ppermute | solution.py:54
  67.3 8.9 %collective-permute-start.13 = (bf16[64,1152]{1,0:T(8,128)(2,1)S(1)}, bf16[64,1152]{1,0:T(8,128)(2,1)S(1)}, u32[]{:S(2)}, u32[]{:S(2)}) collective-permute-start(bf16[64,1152]{1,0:T(8,128)(2,1)S(1)} %get-tuple-element.13), channel_id=1, source_target_pairs={{0,24},{8,16},{16,8},{24,0},{1,25},{9,17},{17,9},{25,1},{2,26},{10... | collective-permute-start | bytes 442376 | tf_op jit(solution)/shard_map/ppermute | solution.py:48
  68.7 8.8 %collective-permute-start.12 = (bf16[64,1152]{1,0:T(8,128)(2,1)S(1)}, bf16[64,1152]{1,0:T(8,128)(2,1)S(1)}, u32[]{:S(2)}, u32[]{:S(2)}) collective-permute-start(bf16[64,1152]{1,0:T(8,128)(2,1)S(1)} %get-tuple-element.14), channel_id=1, source_target_pairs={{0,16},{8,24},{16,0},{24,8},{1,17},{9,25},{17,1},{25,9},{2,18},{10... | collective-permute-start | bytes 442376 | tf_op jit(solution)/shard_map/ppermute | solution.py:48
  78.6 13.0 %collective-permute-start.30 = (bf16[64,1152]{1,0:T(8,128)(2,1)S(1)}, bf16[64,1152]{1,0:T(8,128)(2,1)S(1)}, u32[]{:S(2)}, u32[]{:S(2)}) collective-permute-start(bf16[64,1152]{1,0:T(8,128)(2,1)S(1)} %get-tuple-element.5), channel_id=1, source_target_pairs={{0,24},{8,16},{16,8},{24,0},{1,25},{9,17},{17,9},{25,1},{2,26},{10... | collective-permute-start | bytes 442376 | tf_op jit(solution)/shard_map/ppermute | solution.py:48
  80.1 13.6 %collective-permute-start.29 = (bf16[64,1152]{1,0:T(8,128)(2,1)S(1)}, bf16[64,1152]{1,0:T(8,128)(2,1)S(1)}, u32[]{:S(2)}, u32[]{:S(2)}) collective-permute-start(bf16[64,1152]{1,0:T(8,128)(2,1)S(1)} %get-tuple-element.5), channel_id=1, source_target_pairs={{0,16},{8,24},{16,0},{24,8},{1,17},{9,25},{17,1},{25,9},{2,18},{10... | collective-permute-start | bytes 442376 | tf_op jit(solution)/shard_map/ppermute | solution.py:48
  80.8 12.9 %collective-permute-start.28 = (bf16[64,1152]{1,0:T(8,128)(2,1)S(1)}, bf16[64,1152]{1,0:T(8,128)(2,1)S(1)}, u32[]{:S(2)}, u32[]{:S(2)}) collective-permute-start(bf16[64,1152]{1,0:T(8,128)(2,1)S(1)} %get-tuple-element.5), channel_id=1, source_target_pairs={{0,8},{8,0},{16,24},{24,16},{1,9},{9,1},{17,25},{25,17},{2,10},{10... | collective-permute-start | bytes 442376 | tf_op jit(solution)/shard_map/ppermute | solution.py:48
  90.2 12.4 %collective-permute-start.22 = (bf16[48,1152]{1,0:T(8,128)(2,1)}, bf16[48,1152]{1,0:T(8,128)(2,1)S(1)}, u32[]{:S(2)}, u32[]{:S(2)}) collective-permute-start(bf16[48,1152]{1,0:T(8,128)(2,1)} %get-tuple-element.18), channel_id=1, source_target_pairs={{0,2},{1,3},{2,0},{3,1},{4,6},{5,7},{6,4},{7,5},{8,10},{9,11},{10,... | collective-permute-start | bytes 331784 | tf_op jit(solution)/shard_map/ppermute | solution.py:51
  90.2 13.6 %collective-permute-start.24 = (bf16[48,1152]{1,0:T(8,128)(2,1)}, bf16[48,1152]{1,0:T(8,128)(2,1)}, u32[]{:S(2)}, u32[]{:S(2)}) collective-permute-start(bf16[48,1152]{1,0:T(8,128)(2,1)} %get-tuple-element.19), channel_id=1, source_target_pairs={{0,6},{1,7},{2,4},{3,5},{4,2},{5,3},{6,0},{7,1},{8,14},{9,15},{10,... | collective-permute-start | bytes 331784 | tf_op jit(solution)/shard_map/ppermute | solution.py:51
  91.5 12.3 %collective-permute-start.23 = (bf16[48,1152]{1,0:T(8,128)(2,1)S(1)}, bf16[48,1152]{1,0:T(8,128)(2,1)}, u32[]{:S(2)}, u32[]{:S(2)}) collective-permute-start(bf16[48,1152]{1,0:T(8,128)(2,1)S(1)} %get-tuple-element.20), channel_id=1, source_target_pairs={{0,4},{1,5},{2,6},{3,7},{4,0},{5,1},{6,2},{7,3},{8,12},{9,13},{10,... | collective-permute-start | bytes 331784 | tf_op jit(solution)/shard_map/ppermute | solution.py:51
  102.6 11.5 %collective-permute-start.33 = (bf16[48,1152]{1,0:T(8,128)(2,1)S(1)}, bf16[48,1152]{1,0:T(8,128)(2,1)S(1)}, u32[]{:S(2)}, u32[]{:S(2)}) collective-permute-start(bf16[48,1152]{1,0:T(8,128)(2,1)S(1)} %get-tuple-element.17), channel_id=1, source_target_pairs={{0,4},{1,5},{2,6},{3,7},{4,0},{5,1},{6,2},{7,3},{8,12},{9,13},{10,... | collective-permute-start | bytes 331784 | tf_op jit(solution)/shard_map/ppermute | solution.py:51
  105.0 12.5 %collective-permute-start.27 = (bf16[48,1152]{1,0:T(8,128)(2,1)S(1)}, bf16[48,1152]{1,0:T(8,128)(2,1)S(1)}, u32[]{:S(2)}, u32[]{:S(2)}) collective-permute-start(bf16[48,1152]{1,0:T(8,128)(2,1)S(1)} %fusion.72), channel_id=1, source_target_pairs={{0,24},{8,16},{16,8},{24,0},{1,25},{9,17},{17,9},{25,1},{2,26},{10... | collective-permute-start | bytes 331784 | tf_op jit(solution)/shard_map/ppermute | solution.py:48
  106.6 12.1 %collective-permute-start.26 = (bf16[48,1152]{1,0:T(8,128)(2,1)S(1)}, bf16[48,1152]{1,0:T(8,128)(2,1)S(1)}, u32[]{:S(2)}, u32[]{:S(2)}) collective-permute-start(bf16[48,1152]{1,0:T(8,128)(2,1)S(1)} %fusion.72), channel_id=1, source_target_pairs={{0,16},{8,24},{16,0},{24,8},{1,17},{9,25},{17,1},{25,9},{2,18},{10... | collective-permute-start | bytes 331784 | tf_op jit(solution)/shard_map/ppermute | solution.py:48
  107.3 11.4 %collective-permute-start.25 = (bf16[48,1152]{1,0:T(8,128)(2,1)S(1)}, bf16[48,1152]{1,0:T(8,128)(2,1)S(1)}, u32[]{:S(2)}, u32[]{:S(2)}) collective-permute-start(bf16[48,1152]{1,0:T(8,128)(2,1)S(1)} %fusion.72), channel_id=1, source_target_pairs={{0,8},{8,0},{16,24},{24,16},{1,9},{9,1},{17,25},{25,17},{2,10},{10... | collective-permute-start | bytes 331784 | tf_op jit(solution)/shard_map/ppermute | solution.py:48
  (35 other events, 276.3 us)

commit v2 on v1

v2 whole, which is shorter than its diff:
```python
import functools

import jax
import jax.numpy as jnp
from jax import lax
from jax.experimental import pallas as pl
from jax.experimental.pallas import tpu as pltpu
from jax.sharding import Mesh
from jax.sharding import PartitionSpec as P

logit_scale = 32.0
logit_bias = -3.0
epsilon = 1e-06
low = jnp.bfloat16
wide = jnp.float32


def dot(a, b, a_dim, b_dim):
    return lax.dot_general(a, b, (((a_dim,), (b_dim,)), ((), ())), preferred_element_type=wide)


def project(features, weight):
    before = dot(features, weight, 1, 0)
    inverse = lax.rsqrt(jnp.sum(before * before, axis=1, keepdims=True) + epsilon)
    return (before * inverse, inverse)


def unproject(grad_unit, unit, inverse):
    inner_sum = jnp.sum(unit * grad_unit, axis=1, keepdims=True)
    return (inverse * (grad_unit - unit * inner_sum)).astype(low)


def pair_weights(rows_low, cols_low, own):
    logits = logit_scale * dot(rows_low, cols_low, 1, 1) + logit_bias
    if not own:
        return jax.nn.sigmoid(logits).astype(low)
    row_ids = lax.broadcasted_iota(jnp.int32, logits.shape, 0)
    col_ids = lax.broadcasted_iota(jnp.int32, logits.shape, 1)
    label_sign = jnp.where(row_ids == col_ids, wide(1.0), wide(-1.0))
    return (-label_sign * jax.nn.sigmoid(-label_sign * logits)).astype(low)


def after(array, *others):
    return lax.optimization_barrier((array, *others))[0]


def selectors_kernel(sizes, place_ref, choose_ref, order_ref):
    groups, layers, cores, share, part, padded = sizes
    blk_pos, layer_pos, core_pos = place_ref[0], place_ref[1], place_ref[2]
    width = choose_ref.shape[1]
    row = lax.broadcasted_iota(jnp.int32, (padded, width), 0)
    column = lax.broadcasted_iota(jnp.int32, (padded, width), 1)
    kept = (row < part) & (row < share - blk_pos * part)
    pieces = []
    for core in range(cores):
        for layer in range(layers):
            first = ((layer ^ layer_pos) * cores + (core ^ core_pos)) * share + blk_pos * part
            pieces.append(jnp.where(kept & (column == row + first), wide(1.0), wide(0.0)))
    choose_ref[...] = jnp.concatenate(pieces).astype(low)
    row = lax.broadcasted_iota(jnp.int32, order_ref.shape, 0)
    column = lax.broadcasted_iota(jnp.int32, order_ref.shape, 1)
    found = jnp.zeros(order_ref.shape, wide)
    for k in range(groups):
        at = column - k * padded
        match = (at >= 0) & (at < part) & (row == (k ^ blk_pos) * part + at)
        found = jnp.where(match, wide(1.0), found)
    order_ref[...] = found.astype(low)


def selectors(position, sizes, width):
    groups, layers, cores, share, part, padded = sizes
    return pl.pallas_call(
        functools.partial(selectors_kernel, sizes),
        out_shape=(
            jax.ShapeDtypeStruct((cores * layers * padded, width), low),
            jax.ShapeDtypeStruct((share, groups * padded), low),
        ),
        in_specs=[pl.BlockSpec(memory_space=pltpu.SMEM)],
        out_specs=(pl.BlockSpec(memory_space=pltpu.VMEM),) * 2,
        compiler_params=pltpu.CompilerParams(vmem_limit_bytes=16 * 2**20),
    )(position)


def per_device(images, captions, image_head, text_head):
    groups = lax.axis_size("blk")
    layers = lax.axis_size("layer")
    cores = lax.axis_size("core")
    rows, width = images.shape
    position = jnp.stack([lax.axis_index("blk"), lax.axis_index("layer"), lax.axis_index("core")])

    def over(array, axis, by):
        return lax.ppermute(array, axis, [(i, i ^ by) for i in range(lax.axis_size(axis))])

    def over_blk(array):
        return [array] + [over(array, "blk", k) for k in range(1, groups)]

    def over_core(array):
        return over(array, "core", 1)

    share = width // (layers * cores)
    part = -(-share // groups)
    padded = -(-part // 8) * 8
    sent = layers * padded
    sizes = (groups, layers, cores, share, part, padded)

    caption_blocks = over_blk(captions)
    image_blocks = [images, over(after(images, *caption_blocks), "layer", 1)]
    image_blocks += [over(images, "layer", k) for k in range(2, layers)]
    image_group = [images, over(after(images, image_blocks[-1]), "blk", 1)]
    image_group += [over(after(images, *caption_blocks), "blk", k) for k in range(2, groups)]
    choose, order = selectors(position.astype(jnp.int32), sizes, width)

    text_unit, text_inverse = project(jnp.concatenate(caption_blocks), text_head)
    near_low = text_unit.astype(low)
    text_low = jnp.concatenate([near_low, over_core(near_low)])
    weights, image_lows, image_parts = [None] * layers, [None] * layers, [None] * layers
    for k in (*range(layers - 1, 0, -1), 0):
        unit, inverse = project(image_blocks[k], image_head)
        unit_low = unit.astype(low)
        pair_weight = pair_weights(unit_low, text_low, k == 0)
        image_part = dot(pair_weight, text_low, 1, 0)
        if k == 0:
            image_unit, image_inverse, image_total = unit, inverse, image_part
        else:
            image_parts[k] = over(image_part.astype(low), "layer", k)
        weights[k] = pair_weight
        image_lows[k] = unit_low
    weight, image_low = jnp.concatenate(weights), jnp.concatenate(image_lows)
    half = groups * rows
    far_part = dot(weight[:, half:], image_low, 0, 0).astype(low)
    near_part = dot(weight[:, :half], image_low, 0, 0)
    text_half = near_part + over_core(far_part).astype(wide)
    text_total = text_half[:rows]
    text_out = [text_half[k * rows : (k + 1) * rows].astype(low) for k in range(1, groups)]
    text_out, image_group = lax.optimization_barrier((text_out, image_group))
    text_out[0] = after(text_out[0], image_parts[1])
    text_parts = [over(block, "blk", k + 1) for k, block in enumerate(text_out)]

    image_columns = [dot(choose, after(block, *text_out), 1, 1).astype(low) for block in image_group]
    caption_columns = [dot(choose, after(block, *text_out), 1, 1).astype(low) for block in caption_blocks]
    image_columns, caption_columns = lax.optimization_barrier((image_columns, caption_columns))

    for block in text_parts:
        text_total = text_total + block.astype(wide)
    text_back = unproject(logit_scale * text_total, text_unit[:rows], text_inverse[:rows])
    text_backs = over_blk(text_back)
    for block in image_parts[1:]:
        image_total = image_total + after(block, text_back).astype(wide)
    image_back = unproject(logit_scale * image_total, image_unit, image_inverse)
    image_backs = [image_back] + [None] + [over(image_back, "blk", k) for k in range(2, groups)]
    image_backs[1] = over(after(image_back, *text_backs), "blk", 1)
    grad_images = dot(after(image_back, *image_backs[2:]), image_head, 1, 1).astype(low)
    grad_captions = dot(after(text_back, image_back), text_head, 1, 1).astype(low)

    def head_terms(columns, backs):
        terms = sum(dot(c, b, 1, 0) for c, b in zip(columns, backs))
        terms = terms[:sent] + over_core(terms[sent:].astype(low)).astype(wide)
        out = [terms[k * padded : (k + 1) * padded].astype(low) for k in range(1, layers)]
        return terms[:padded], out

    def over_layers(out):
        return [over(block, "layer", k + 1) for k, block in enumerate(out)]

    def add_up(total, parts):
        for block in parts:
            total = total + block.astype(wide)
        return total.astype(low)

    text_total, text_out = head_terms(caption_columns, text_backs)
    text_parts = over_layers(text_out)
    image_backs = [image_back] + [after(block, *text_out) for block in image_backs[1:]]
    image_total, image_out = head_terms(image_columns, image_backs)
    image_parts = over_layers(image_out)
    text_sum = add_up(text_total, [after(block, *image_out) for block in text_parts])
    text_sums = over_blk(text_sum)
    image_sum = add_up(image_total, [after(block, text_sum) for block in image_parts])
    image_sums = over_blk(image_sum)
    text_sums = [text_sum] + [after(block, image_sum) for block in text_sums[1:]]
    grad_text_head = dot(order, jnp.concatenate(text_sums), 1, 0)
    grad_image_head = dot(order, jnp.concatenate(image_sums), 1, 0)
    return (grad_images, grad_captions, grad_image_head, grad_text_head)


def solution(mesh):
    groups, members = mesh.devices.shape
    fine = Mesh(mesh.devices.reshape(groups, members // 2, 2), ("blk", "layer", "core"))
    pairs, share = P(("blk", "layer", "core"), None), P(("layer", "core"), None)
    return jax.shard_map(
        per_device,
        mesh=fine,
        in_specs=(pairs, pairs, P(), P()),
        out_specs=(pairs, pairs, share, share),
        check_vma=False,
    )
```

time: 124 us -> 99 us (0.80)
  waiting for transfers between devices: 34.9 us -> 23.1 us
  local copies, waits for them, and re-layouts: 11.1 us -> 2.14 us
  other arithmetic: 8.68 us -> 1.97 us
  starting transfers between devices: 42.8 us -> 44.7 us
    ppermute x38 -> x37, waiting for transfers between devices: 34.9 us -> 23.1 us  [over(): lax.ppermute(array, axis, [(i, i ^ by) for i in range(lax.axis_size(axis))])]
    unnamed x54 -> x12, local copies, waits for them, and re-layouts: 8.16 us -> 1.96 us
    convert_element_type x3 -> x5, other arithmetic: 2.41 us -> 0.52 us  [the longest x2 0.23 us: unproject(): return (inverse * (grad_unit - unit * inner_sum)).astype(low)]
    ppermute x38 -> x37, starting transfers between devices: 42.8 us -> 44.7 us  [over(): lax.ppermute(array, axis, [(i, i ^ by) for i in range(lax.axis_size(axis))])]
    slice x4 -> x5, local copies, waits for them, and re-layouts: 1.84 us -> 0.17 us  [the longest x2 0.09 us: head_terms(): terms = terms[:sent] + over_core(terms[sent:].astype(low)).astype(wide)]
    dot_general x20 -> x35, matrix products: 25.3 us -> 24.9 us  [dot(): lax.dot_general(a, b, (((a_dim,), (b_dim,)), ((), ())), preferred_element...]
  transfers between devices with their start and end apart: 38 -> 37, of which waited for: 13 -> 12; matrix products, arithmetic and copies ran while one was open for 34% -> 25% of each run, Pallas kernels for 0% -> 1%
where the time goes in v2:
time: 99 us; the launch traced here: 98.7 us
  starting transfers between devices  44.7 us (45%)
  matrix products  24.9 us (25%)
  waiting for transfers between devices  23.1 us (23%)
  local copies, waits for them, and re-layouts  2.14 us (2%)
  other arithmetic  1.97 us (2%)
  between operations  1.17 us (1%)
    ppermute x37, starting transfers between devices, over(): lax.ppermute(array, axis, [(i, i ^ by) for i in range(lax.axis_size(axis))])  44.7 us
    dot_general x35, matrix products, dot(): lax.dot_general(a, b, (((a_dim,), (b_dim,)), ((), ())), preferred_element...  24.9 us
    ppermute x37, waiting for transfers between devices, over(): lax.ppermute(array, axis, [(i, i ^ by) for i in range(lax.axis_size(axis))])  23.1 us
  transfers between devices with their start and end apart: 37, of which 12 were waited for; matrix products, arithmetic and copies ran while one was open for 25% of the time, Pallas kernels for 1%

profile of v2, /device:TPU:0, one launch (start us, length us, event | category | flops | bytes accessed | tf_op | source)
XLA Modules:
  0.0 98.7 jit_solution(16994869872948956363)
XLA Ops:
  0.7 3.0 %collective-permute-start = (bf16[64,1152]{1,0:T(8,128)(2,1)}, bf16[64,1152]{1,0:T(8,128)(2,1)}, u32[]{:S(2)}, u32[]{:S(2)}) collective-permute-start(bf16[64,1152]{1,0:T(8,128)(2,1)} %param.5), channel_id=1, source_target_pairs={{0,8},{8,0},{16,24},{24,16},{1,9},{9,1},{17,25},{25,17},{2,10},{10... | collective-permute-start | bytes 442376 | tf_op jit(solution)/shard_map/ppermute | solution.py:92
  3.7 1.5 %collective-permute-start.1 = (bf16[64,1152]{1,0:T(8,128)(2,1)}, bf16[64,1152]{1,0:T(8,128)(2,1)}, u32[]{:S(2)}, u32[]{:S(2)}) collective-permute-start(bf16[64,1152]{1,0:T(8,128)(2,1)} %param.5), channel_id=1, source_target_pairs={{0,16},{8,24},{16,0},{24,8},{1,17},{9,25},{17,1},{25,9},{2,18},{10... | collective-permute-start | bytes 442376 | tf_op jit(solution)/shard_map/ppermute | solution.py:92
  5.2 4.1 %collective-permute-start.7 = (bf16[64,1152]{1,0:T(8,128)(2,1)}, bf16[64,1152]{1,0:T(8,128)(2,1)S(1)}, u32[]{:S(2)}, u32[]{:S(2)}) collective-permute-start(bf16[64,1152]{1,0:T(8,128)(2,1)} %param.4), channel_id=1, source_target_pairs={{0,6},{2,4},{4,2},{6,0},{1,7},{3,5},{5,3},{7,1},{8,14},{10,12},{12... | collective-permute-start | bytes 442376 | tf_op jit(solution)/shard_map/ppermute | solution.py:92
  9.3 2.5 %multiply_reduce_fusion.6 = (f32[64]{0:T(128)S(1)}, f32[64,1152]{1,0:T(8,128)S(1)}) fusion(bf16[64,1152]{1,0:T(8,128)(2,1)} %param.4, bf16[1152,1152]{1,0:T(8,128)(2,1)} %param.6), kind=kOutput, calls=%fused_computation.101 | convolution fusion | flops 170016704 | bytes 3096832 | tf_op jit(solution)/shard_map/dot_general | solution.py:19
  14.1 1.7 %collective-permute-start.10 = (bf16[64,1152]{1,0:T(8,128)(2,1)S(1)}, bf16[64,1152]{1,0:T(8,128)(2,1)S(1)}, u32[]{:S(2)}, u32[]{:S(2)}) collective-permute-start(bf16[64,1152]{1,0:T(8,128)(2,1)S(1)} %copy-done.2), channel_id=1, source_target_pairs={{0,16},{8,24},{16,0},{24,8},{1,17},{9,25},{17,1},{25,9},{2,18},{10... | collective-permute-start | bytes 442376 | tf_op jit(solution)/shard_map/ppermute | solution.py:92
  15.8 1.4 %collective-permute-start.11 = (bf16[64,1152]{1,0:T(8,128)(2,1)S(1)}, bf16[64,1152]{1,0:T(8,128)(2,1)S(1)}, u32[]{:S(2)}, u32[]{:S(2)}) collective-permute-start(bf16[64,1152]{1,0:T(8,128)(2,1)S(1)} %copy-done.2), channel_id=1, source_target_pairs={{0,24},{8,16},{16,8},{24,0},{1,25},{9,17},{17,9},{25,1},{2,26},{10... | collective-permute-start | bytes 442376 | tf_op jit(solution)/shard_map/ppermute | solution.py:92
  17.3 2.1 %multiply_reduce_fusion = (f32[256]{0:T(256)S(1)}, f32[256,1152]{1,0:T(8,128)S(1)}) fusion(bf16[1152,1152]{1,0:T(8,128)(2,1)S(1)} %copy-done, bf16[64,1152]{1,0:T(8,128)(2,1)} %collective-permute-done.2, bf16[64,1152]{1,0:T(8,128)(2,1)} %collective-permute-done.1, bf16[64,1152]{1,0:T(8,128)(2,1)} %collective-permute-done, bf16[64,1152]{1,0:T(8,128)(2,1)S(1)} %copy-done.3), kind=kOutput, calls=%fused_computation.18 | convolution fusion | flops 682426112 | bytes 4424704 | tf_op jit(solution)/shard_map/dot_general | solution.py:19
  29.4 3.0 %collective-permute-start.15 = (bf16[64,1152]{1,0:T(8,128)(2,1)S(1)}, bf16[64,1152]{1,0:T(8,128)(2,1)S(1)}, u32[]{:S(2)}, u32[]{:S(2)}) collective-permute-start(bf16[64,1152]{1,0:T(8,128)(2,1)S(1)} %convolution_convert_fusion.4), channel_id=1, source_target_pairs={{0,4},{2,6},{4,0},{6,2},{1,5},{3,7},{5,1},{7,3},{8,12},{10,14},{12... | collective-permute-start | bytes 442376 | tf_op jit(solution)/shard_map/ppermute | solution.py:92
  33.4 2.8 %collective-permute-done.5 = bf16[64,1152]{1,0:T(8,128)(2,1)S(1)} collective-permute-done((bf16[64,1152]{1,0:T(8,128)(2,1)S(1)}, bf16[64,1152]{1,0:T(8,128)(2,1)S(1)}, u32[]{:S(2)}, u32[]{:S(2)}) %collective-permute-start.5) | collective-permute-done | bytes 147488 | tf_op jit(solution)/shard_map/ppermute | solution.py:92
  37.3 1.5 %collective-permute-start.13 = (bf16[64,1152]{1,0:T(8,128)(2,1)S(1)}, bf16[64,1152]{1,0:T(8,128)(2,1)S(1)}, u32[]{:S(2)}, u32[]{:S(2)}) collective-permute-start(bf16[64,1152]{1,0:T(8,128)(2,1)S(1)} %get-tuple-element.54), channel_id=1, source_target_pairs={{0,16},{8,24},{16,0},{24,8},{1,17},{9,25},{17,1},{25,9},{2,18},{10... | collective-permute-start | bytes 442376 | tf_op jit(solution)/shard_map/ppermute | solution.py:92
  46.9 1.8 %collective-permute-start.21 = (bf16[64,1152]{1,0:T(8,128)(2,1)S(1)}, bf16[64,1152]{1,0:T(8,128)(2,1)S(1)}, u32[]{:S(2)}, u32[]{:S(2)}) collective-permute-start(bf16[64,1152]{1,0:T(8,128)(2,1)S(1)} %multiply_convert_fusion.1), channel_id=1, source_target_pairs={{0,24},{8,16},{16,8},{24,0},{1,25},{9,17},{17,9},{25,1},{2,26},{10... | collective-permute-start | bytes 442376 | tf_op jit(solution)/shard_map/ppermute | solution.py:92
  50.3 1.5 %collective-permute-done.19 = bf16[64,1152]{1,0:T(8,128)(2,1)S(1)} collective-permute-done((bf16[64,1152]{1,0:T(8,128)(2,1)S(1)}, bf16[64,1152]{1,0:T(8,128)(2,1)S(1)}, u32[]{:S(2)}, u32[]{:S(2)}) %collective-permute-start.19) | collective-permute-done | bytes 147488 | tf_op jit(solution)/shard_map/ppermute | solution.py:92
  52.2 2.1 %collective-permute-done.21 = bf16[64,1152]{1,0:T(8,128)(2,1)S(1)} collective-permute-done((bf16[64,1152]{1,0:T(8,128)(2,1)S(1)}, bf16[64,1152]{1,0:T(8,128)(2,1)S(1)}, u32[]{:S(2)}, u32[]{:S(2)}) %collective-permute-start.21) | collective-permute-done | bytes 147488 | tf_op jit(solution)/shard_map/ppermute | solution.py:92
  58.8 1.6 %collective-permute-start.22 = (bf16[64,1152]{1,0:T(8,128)(2,1)S(1)}, bf16[64,1152]{1,0:T(8,128)(2,1)S(1)}, u32[]{:S(2)}, u32[]{:S(2)}) collective-permute-start(bf16[64,1152]{1,0:T(8,128)(2,1)S(1)} %multiply_convert_fusion), channel_id=1, source_target_pairs={{0,8},{8,0},{16,24},{24,16},{1,9},{9,1},{17,25},{25,17},{2,10},{10... | collective-permute-start | bytes 442376 | tf_op jit(solution)/shard_map/ppermute | solution.py:92
  60.5 5.3 %collective-permute-done.17 = bf16[64,1152]{1,0:T(8,128)(2,1)S(1)} collective-permute-done((bf16[64,1152]{1,0:T(8,128)(2,1)S(1)}, bf16[64,1152]{1,0:T(8,128)(2,1)S(1)}, u32[]{:S(2)}, u32[]{:S(2)}) %collective-permute-start.17) | collective-permute-done | bytes 147488 | tf_op jit(solution)/shard_map/ppermute | solution.py:92
  68.3 1.6 %convolution_convert_fusion.1 = bf16[64,1152]{1,0:T(8,128)(2,1)} fusion(bf16[64,1152]{1,0:T(8,128)(2,1)S(1)} %multiply_convert_fusion.1, bf16[1152,1152]{1,0:T(8,128)(2,1)S(1)} %copy-done), kind=kOutput, calls=%fused_computation.11 | convolution fusion | flops 169943040 | bytes 2949120 | tf_op jit(solution)/shard_map/dot_general | solution.py:19
  69.9 1.6 %convolution_convert_fusion.2 = bf16[64,1152]{1,0:T(8,128)(2,1)} fusion(bf16[64,1152]{1,0:T(8,128)(2,1)S(1)} %multiply_convert_fusion, bf16[1152,1152]{1,0:T(8,128)(2,1)S(1)} %copy-done.1), kind=kOutput, calls=%fused_computation.12 | convolution fusion | flops 169943040 | bytes 2949120 | tf_op jit(solution)/shard_map/dot_general | solution.py:19
  71.5 2.9 %collective-permute-start.27 = (bf16[40,1152]{1,0:T(8,128)(2,1)S(1)}, bf16[40,1152]{1,0:T(8,128)(2,1)S(1)}, u32[]{:S(2)}, u32[]{:S(2)}) collective-permute-start(bf16[40,1152]{1,0:T(8,128)(2,1)S(1)} %get-tuple-element.109), channel_id=1, source_target_pairs={{0,4},{2,6},{4,0},{6,2},{1,5},{3,7},{5,1},{7,3},{8,12},{10,14},{12... | collective-permute-start | bytes 276488 | tf_op jit(solution)/shard_map/ppermute | solution.py:92
  74.4 1.5 %collective-permute-start.28 = (bf16[40,1152]{1,0:T(8,128)(2,1)S(1)}, bf16[40,1152]{1,0:T(8,128)(2,1)S(1)}, u32[]{:S(2)}, u32[]{:S(2)}) collective-permute-start(bf16[40,1152]{1,0:T(8,128)(2,1)S(1)} %get-tuple-element.108), channel_id=1, source_target_pairs={{0,6},{2,4},{4,2},{6,0},{1,7},{3,5},{5,3},{7,1},{8,14},{10,12},{12... | collective-permute-start | bytes 276488 | tf_op jit(solution)/shard_map/ppermute | solution.py:92
  76.1 2.9 %collective-permute-start.29 = (bf16[40,1152]{1,0:T(8,128)(2,1)S(1)}, bf16[40,1152]{1,0:T(8,128)(2,1)S(1)}, u32[]{:S(2)}, u32[]{:S(2)}) collective-permute-start(bf16[40,1152]{1,0:T(8,128)(2,1)S(1)} %get-tuple-element.105), channel_id=1, source_target_pairs={{0,4},{2,6},{4,0},{6,2},{1,5},{3,7},{5,1},{7,3},{8,12},{10,14},{12... | collective-permute-start | bytes 276488 | tf_op jit(solution)/shard_map/ppermute | solution.py:92
  79.0 1.5 %collective-permute-start.30 = (bf16[40,1152]{1,0:T(8,128)(2,1)S(1)}, bf16[40,1152]{1,0:T(8,128)(2,1)S(1)}, u32[]{:S(2)}, u32[]{:S(2)}) collective-permute-start(bf16[40,1152]{1,0:T(8,128)(2,1)S(1)} %get-tuple-element.106), channel_id=1, source_target_pairs={{0,6},{2,4},{4,2},{6,0},{1,7},{3,5},{5,3},{7,1},{8,14},{10,12},{12... | collective-permute-start | bytes 276488 | tf_op jit(solution)/shard_map/ppermute | solution.py:92
  80.5 1.4 %collective-permute-done.27 = bf16[40,1152]{1,0:T(8,128)(2,1)S(1)} collective-permute-done((bf16[40,1152]{1,0:T(8,128)(2,1)S(1)}, bf16[40,1152]{1,0:T(8,128)(2,1)S(1)}, u32[]{:S(2)}, u32[]{:S(2)}) %collective-permute-start.27) | collective-permute-done | bytes 92192 | tf_op jit(solution)/shard_map/ppermute | solution.py:92
  85.6 4.3 %collective-permute-done.29 = bf16[40,1152]{1,0:T(8,128)(2,1)S(1)} collective-permute-done((bf16[40,1152]{1,0:T(8,128)(2,1)S(1)}, bf16[40,1152]{1,0:T(8,128)(2,1)S(1)}, u32[]{:S(2)}, u32[]{:S(2)}) %collective-permute-start.29) | collective-permute-done | bytes 92192 | tf_op jit(solution)/shard_map/ppermute | solution.py:92
  95.0 1.6 %collective-permute-done.32 = bf16[40,1152]{1,0:T(8,128)(2,1)S(1)} collective-permute-done((bf16[40,1152]{1,0:T(8,128)(2,1)S(1)}, bf16[40,1152]{1,0:T(8,128)(2,1)S(1)}, u32[]{:S(2)}, u32[]{:S(2)}) %collective-permute-start.32) | collective-permute-done | bytes 92192 | tf_op jit(solution)/shard_map/ppermute | solution.py:92
  (123 shorter events, 42.2 us)
Async XLA Ops:
  0.7 12.8 %collective-permute-start = (bf16[64,1152]{1,0:T(8,128)(2,1)}, bf16[64,1152]{1,0:T(8,128)(2,1)}, u32[]{:S(2)}, u32[]{:S(2)}) collective-permute-start(bf16[64,1152]{1,0:T(8,128)(2,1)} %param.5), channel_id=1, source_target_pairs={{0,8},{8,0},{16,24},{24,16},{1,9},{9,1},{17,25},{25,17},{2,10},{10... | collective-permute-start | bytes 442376 | tf_op jit(solution)/shard_map/ppermute | solution.py:92
  3.7 9.8 %collective-permute-start.1 = (bf16[64,1152]{1,0:T(8,128)(2,1)}, bf16[64,1152]{1,0:T(8,128)(2,1)}, u32[]{:S(2)}, u32[]{:S(2)}) collective-permute-start(bf16[64,1152]{1,0:T(8,128)(2,1)} %param.5), channel_id=1, source_target_pairs={{0,16},{8,24},{16,0},{24,8},{1,17},{9,25},{17,1},{25,9},{2,18},{10... | collective-permute-start | bytes 442376 | tf_op jit(solution)/shard_map/ppermute | solution.py:92
  5.2 8.3 %collective-permute-start.2 = (bf16[64,1152]{1,0:T(8,128)(2,1)}, bf16[64,1152]{1,0:T(8,128)(2,1)}, u32[]{:S(2)}, u32[]{:S(2)}) collective-permute-start(bf16[64,1152]{1,0:T(8,128)(2,1)} %param.5), channel_id=1, source_target_pairs={{0,24},{8,16},{16,8},{24,0},{1,25},{9,17},{17,9},{25,1},{2,26},{10... | collective-permute-start | bytes 442376 | tf_op jit(solution)/shard_map/ppermute | solution.py:92
  5.2 14.8 %collective-permute-start.7 = (bf16[64,1152]{1,0:T(8,128)(2,1)}, bf16[64,1152]{1,0:T(8,128)(2,1)S(1)}, u32[]{:S(2)}, u32[]{:S(2)}) collective-permute-start(bf16[64,1152]{1,0:T(8,128)(2,1)} %param.4), channel_id=1, source_target_pairs={{0,6},{2,4},{4,2},{6,0},{1,7},{3,5},{5,3},{7,1},{8,14},{10,12},{12... | collective-permute-start | bytes 442376 | tf_op jit(solution)/shard_map/ppermute | solution.py:92
  9.3 12.6 %collective-permute-start.6 = (bf16[64,1152]{1,0:T(8,128)(2,1)}, bf16[64,1152]{1,0:T(8,128)(2,1)S(1)}, u32[]{:S(2)}, u32[]{:S(2)}) collective-permute-start(bf16[64,1152]{1,0:T(8,128)(2,1)} %param.4), channel_id=1, source_target_pairs={{0,4},{2,6},{4,0},{6,2},{1,5},{3,7},{5,1},{7,3},{8,12},{10,14},{12... | collective-permute-start | bytes 442376 | tf_op jit(solution)/shard_map/ppermute | solution.py:92
  13.5 10.1 %collective-permute-start.4 = (bf16[64,1152]{1,0:T(8,128)(2,1)S(1)}, bf16[64,1152]{1,0:T(8,128)(2,1)S(1)}, u32[]{:S(2)}, u32[]{:S(2)}) collective-permute-start(bf16[64,1152]{1,0:T(8,128)(2,1)S(1)} %copy-done.2), channel_id=1, source_target_pairs={{0,2},{2,0},{4,6},{6,4},{1,3},{3,1},{5,7},{7,5},{8,10},{10,8},{12,... | collective-permute-start | bytes 442376 | tf_op jit(solution)/shard_map/ppermute | solution.py:92
  14.1 18.7 %collective-permute-start.10 = (bf16[64,1152]{1,0:T(8,128)(2,1)S(1)}, bf16[64,1152]{1,0:T(8,128)(2,1)S(1)}, u32[]{:S(2)}, u32[]{:S(2)}) collective-permute-start(bf16[64,1152]{1,0:T(8,128)(2,1)S(1)} %copy-done.2), channel_id=1, source_target_pairs={{0,16},{8,24},{16,0},{24,8},{1,17},{9,25},{17,1},{25,9},{2,18},{10... | collective-permute-start | bytes 442376 | tf_op jit(solution)/shard_map/ppermute | solution.py:92
  15.8 17.6 %collective-permute-start.11 = (bf16[64,1152]{1,0:T(8,128)(2,1)S(1)}, bf16[64,1152]{1,0:T(8,128)(2,1)S(1)}, u32[]{:S(2)}, u32[]{:S(2)}) collective-permute-start(bf16[64,1152]{1,0:T(8,128)(2,1)S(1)} %copy-done.2), channel_id=1, source_target_pairs={{0,24},{8,16},{16,8},{24,0},{1,25},{9,17},{17,9},{25,1},{2,26},{10... | collective-permute-start | bytes 442376 | tf_op jit(solution)/shard_map/ppermute | solution.py:92
  22.6 10.8 %collective-permute-start.9 = (bf16[64,1152]{1,0:T(8,128)(2,1)S(1)}, bf16[64,1152]{1,0:T(8,128)(2,1)S(1)}, u32[]{:S(2)}, u32[]{:S(2)}) collective-permute-start(bf16[64,1152]{1,0:T(8,128)(2,1)S(1)} %copy-done.2), channel_id=1, source_target_pairs={{0,8},{8,0},{16,24},{24,16},{1,9},{9,1},{17,25},{25,17},{2,10},{10... | collective-permute-start | bytes 442376 | tf_op jit(solution)/shard_map/ppermute | solution.py:92
  27.7 8.5 %collective-permute-start.5 = (bf16[64,1152]{1,0:T(8,128)(2,1)S(1)}, bf16[64,1152]{1,0:T(8,128)(2,1)S(1)}, u32[]{:S(2)}, u32[]{:S(2)}) collective-permute-start(bf16[64,1152]{1,0:T(8,128)(2,1)S(1)} %convolution_convert_fusion.5), channel_id=1, source_target_pairs={{0,2},{2,0},{4,6},{6,4},{1,3},{3,1},{5,7},{7,5},{8,10},{10,8},{12,... | collective-permute-start | bytes 442376 | tf_op jit(solution)/shard_map/ppermute | solution.py:92
  29.4 20.1 %collective-permute-start.15 = (bf16[64,1152]{1,0:T(8,128)(2,1)S(1)}, bf16[64,1152]{1,0:T(8,128)(2,1)S(1)}, u32[]{:S(2)}, u32[]{:S(2)}) collective-permute-start(bf16[64,1152]{1,0:T(8,128)(2,1)S(1)} %convolution_convert_fusion.4), channel_id=1, source_target_pairs={{0,4},{2,6},{4,0},{6,2},{1,5},{3,7},{5,1},{7,3},{8,12},{10,14},{12... | collective-permute-start | bytes 442376 | tf_op jit(solution)/shard_map/ppermute | solution.py:92
  32.8 17.0 %collective-permute-start.16 = (bf16[64,1152]{1,0:T(8,128)(2,1)S(1)}, bf16[64,1152]{1,0:T(8,128)(2,1)S(1)}, u32[]{:S(2)}, u32[]{:S(2)}) collective-permute-start(bf16[64,1152]{1,0:T(8,128)(2,1)S(1)} %convolution_convert_fusion.3), channel_id=1, source_target_pairs={{0,6},{2,4},{4,2},{6,0},{1,7},{3,5},{5,3},{7,1},{8,14},{10,12},{12... | collective-permute-start | bytes 442376 | tf_op jit(solution)/shard_map/ppermute | solution.py:92
  36.2 9.1 %collective-permute-start.12 = (bf16[64,1152]{1,0:T(8,128)(2,1)S(1)}, bf16[64,1152]{1,0:T(8,128)(2,1)S(1)}, u32[]{:S(2)}, u32[]{:S(2)}) collective-permute-start(bf16[64,1152]{1,0:T(8,128)(2,1)S(1)} %get-tuple-element.53), channel_id=1, source_target_pairs={{0,8},{8,0},{16,24},{24,16},{1,9},{9,1},{17,25},{25,17},{2,10},{10... | collective-permute-start | bytes 442376 | tf_op jit(solution)/shard_map/ppermute | solution.py:92
  37.3 8.0 %collective-permute-start.13 = (bf16[64,1152]{1,0:T(8,128)(2,1)S(1)}, bf16[64,1152]{1,0:T(8,128)(2,1)S(1)}, u32[]{:S(2)}, u32[]{:S(2)}) collective-permute-start(bf16[64,1152]{1,0:T(8,128)(2,1)S(1)} %get-tuple-element.54), channel_id=1, source_target_pairs={{0,16},{8,24},{16,0},{24,8},{1,17},{9,25},{17,1},{25,9},{2,18},{10... | collective-permute-start | bytes 442376 | tf_op jit(solution)/shard_map/ppermute | solution.py:92
  56.3 9.5 %collective-permute-start.17 = (bf16[64,1152]{1,0:T(8,128)(2,1)S(1)}, bf16[64,1152]{1,0:T(8,128)(2,1)S(1)}, u32[]{:S(2)}, u32[]{:S(2)}) collective-permute-start(bf16[64,1152]{1,0:T(8,128)(2,1)S(1)} %multiply_convert_fusion), channel_id=1, source_target_pairs={{0,16},{8,24},{16,0},{24,8},{1,17},{9,25},{17,1},{25,9},{2,18},{10... | collective-permute-start | bytes 442376 | tf_op jit(solution)/shard_map/ppermute | solution.py:92
  57.1 10.0 %collective-permute-start.18 = (bf16[64,1152]{1,0:T(8,128)(2,1)S(1)}, bf16[64,1152]{1,0:T(8,128)(2,1)S(1)}, u32[]{:S(2)}, u32[]{:S(2)}) collective-permute-start(bf16[64,1152]{1,0:T(8,128)(2,1)S(1)} %multiply_convert_fusion), channel_id=1, source_target_pairs={{0,24},{8,16},{16,8},{24,0},{1,25},{9,17},{17,9},{25,1},{2,26},{10... | collective-permute-start | bytes 442376 | tf_op jit(solution)/shard_map/ppermute | solution.py:92
  58.8 8.3 %collective-permute-start.22 = (bf16[64,1152]{1,0:T(8,128)(2,1)S(1)}, bf16[64,1152]{1,0:T(8,128)(2,1)S(1)}, u32[]{:S(2)}, u32[]{:S(2)}) collective-permute-start(bf16[64,1152]{1,0:T(8,128)(2,1)S(1)} %multiply_convert_fusion), channel_id=1, source_target_pairs={{0,8},{8,0},{16,24},{24,16},{1,9},{9,1},{17,25},{25,17},{2,10},{10... | collective-permute-start | bytes 442376 | tf_op jit(solution)/shard_map/ppermute | solution.py:92
  71.5 10.4 %collective-permute-start.27 = (bf16[40,1152]{1,0:T(8,128)(2,1)S(1)}, bf16[40,1152]{1,0:T(8,128)(2,1)S(1)}, u32[]{:S(2)}, u32[]{:S(2)}) collective-permute-start(bf16[40,1152]{1,0:T(8,128)(2,1)S(1)} %get-tuple-element.109), channel_id=1, source_target_pairs={{0,4},{2,6},{4,0},{6,2},{1,5},{3,7},{5,1},{7,3},{8,12},{10,14},{12... | collective-permute-start | bytes 276488 | tf_op jit(solution)/shard_map/ppermute | solution.py:92
  76.1 8.2 %collective-permute-start.25 = (bf16[40,1152]{1,0:T(8,128)(2,1)S(1)}, bf16[40,1152]{1,0:T(8,128)(2,1)S(1)}, u32[]{:S(2)}, u32[]{:S(2)}) collective-permute-start(bf16[40,1152]{1,0:T(8,128)(2,1)S(1)} %get-tuple-element.107), channel_id=1, source_target_pairs={{0,2},{2,0},{4,6},{6,4},{1,3},{3,1},{5,7},{7,5},{8,10},{10,8},{12,... | collective-permute-start | bytes 276488 | tf_op jit(solution)/shard_map/ppermute | solution.py:92
  76.1 13.7 %collective-permute-start.29 = (bf16[40,1152]{1,0:T(8,128)(2,1)S(1)}, bf16[40,1152]{1,0:T(8,128)(2,1)S(1)}, u32[]{:S(2)}, u32[]{:S(2)}) collective-permute-start(bf16[40,1152]{1,0:T(8,128)(2,1)S(1)} %get-tuple-element.105), channel_id=1, source_target_pairs={{0,4},{2,6},{4,0},{6,2},{1,5},{3,7},{5,1},{7,3},{8,12},{10,14},{12... | collective-permute-start | bytes 276488 | tf_op jit(solution)/shard_map/ppermute | solution.py:92
  79.0 10.8 %collective-permute-start.30 = (bf16[40,1152]{1,0:T(8,128)(2,1)S(1)}, bf16[40,1152]{1,0:T(8,128)(2,1)S(1)}, u32[]{:S(2)}, u32[]{:S(2)}) collective-permute-start(bf16[40,1152]{1,0:T(8,128)(2,1)S(1)} %get-tuple-element.106), channel_id=1, source_target_pairs={{0,6},{2,4},{4,2},{6,0},{1,7},{3,5},{5,3},{7,1},{8,14},{10,12},{12... | collective-permute-start | bytes 276488 | tf_op jit(solution)/shard_map/ppermute | solution.py:92
  82.0 10.2 %collective-permute-start.34 = (bf16[40,1152]{1,0:T(8,128)(2,1)S(1)}, bf16[40,1152]{1,0:T(8,128)(2,1)S(1)}, u32[]{:S(2)}, u32[]{:S(2)}) collective-permute-start(bf16[40,1152]{1,0:T(8,128)(2,1)S(1)} %fusion.60), channel_id=1, source_target_pairs={{0,8},{8,0},{16,24},{24,16},{1,9},{9,1},{17,25},{25,17},{2,10},{10... | collective-permute-start | bytes 276488 | tf_op jit(solution)/shard_map/ppermute | solution.py:92
  83.4 10.1 %collective-permute-start.35 = (bf16[40,1152]{1,0:T(8,128)(2,1)S(1)}, bf16[40,1152]{1,0:T(8,128)(2,1)S(1)}, u32[]{:S(2)}, u32[]{:S(2)}) collective-permute-start(bf16[40,1152]{1,0:T(8,128)(2,1)S(1)} %fusion.60), channel_id=1, source_target_pairs={{0,16},{8,24},{16,0},{24,8},{1,17},{9,25},{17,1},{25,9},{2,18},{10... | collective-permute-start | bytes 276488 | tf_op jit(solution)/shard_map/ppermute | solution.py:92
  84.3 9.2 %collective-permute-start.36 = (bf16[40,1152]{1,0:T(8,128)(2,1)S(1)}, bf16[40,1152]{1,0:T(8,128)(2,1)S(1)}, u32[]{:S(2)}, u32[]{:S(2)}) collective-permute-start(bf16[40,1152]{1,0:T(8,128)(2,1)S(1)} %fusion.60), channel_id=1, source_target_pairs={{0,24},{8,16},{16,8},{24,0},{1,25},{9,17},{17,9},{25,1},{2,26},{10... | collective-permute-start | bytes 276488 | tf_op jit(solution)/shard_map/ppermute | solution.py:92
  (20 other events, 126.8 us)

commit v3 on v1

v3 whole, which is shorter than its diff:
```python
import functools
import math

import jax
import jax.numpy as jnp
from jax import lax
from jax.experimental import pallas as pl
from jax.experimental.pallas import tpu as pltpu
from jax.sharding import Mesh
from jax.sharding import PartitionSpec as P

logit_scale = 32.0
logit_bias = -3.0
epsilon = 1e-06
low = jnp.bfloat16
wide = jnp.float32
cost_unit = 1_000_000_000


def dot(a, b, a_dim, b_dim):
    return lax.dot_general(a, b, (((a_dim,), (b_dim,)), ((), ())), preferred_element_type=wide)


def project(features, weight):
    before = dot(features, weight, 1, 0)
    return (before, normalized(before)[0].astype(low))


def normalized(before):
    inverse = lax.rsqrt(jnp.sum(before * before, axis=1, keepdims=True) + epsilon)
    return (before * inverse, inverse)


def call(kernel, outs, *arrays, cost=1, scratch=(), behind=()):
    specs = [pl.BlockSpec(memory_space=pltpu.VMEM)] * len(arrays)
    count = len(arrays)
    shapes = [shape for shape, _ in (*outs, *scratch)] + [array.shape for array in arrays]
    held = sum(math.prod(shape) * 4 for shape in shapes)

    def body(*refs):
        kernel(*refs[:count], *refs[count + len(behind) :])

    return pl.pallas_call(
        body,
        out_shape=tuple(jax.ShapeDtypeStruct(shape, kind) for shape, kind in outs),
        in_specs=specs + [pl.BlockSpec(memory_space=pl.ANY)] * len(behind),
        out_specs=(pl.BlockSpec(memory_space=pltpu.VMEM),) * len(outs),
        scratch_shapes=[pltpu.VMEM(shape, kind) for shape, kind in scratch],
        compiler_params=pltpu.CompilerParams(vmem_limit_bytes=min(48 * 2**20, 4 * 2**20 + held)),
        cost_estimate=pl.CostEstimate(flops=cost * cost_unit, bytes_accessed=cost * cost_unit, transcendentals=0),
    )(*arrays, *behind)


def ready_kernel(shape, image_head_ref, text_head_ref, *refs):
    groups, layers, cores = shape
    image_refs, text_refs, refs = refs[:groups], refs[groups : 2 * groups], refs[2 * groups :]
    image_before_ref, text_before_ref, mine_ref, theirs_ref, turned_ref = refs
    image_before_ref[...] = dot(image_refs[0][...], image_head_ref[...], 1, 0)
    text_before_ref[...] = dot(text_refs[0][...], text_head_ref[...], 1, 0)
    gathered = jnp.concatenate([ref[...].astype(wide) for ref in (*image_refs, *text_refs)])
    turned_ref[...] = gathered.T
    share, layer_pos, core_pos = mine_ref.shape[1], lax.axis_index("layer"), lax.axis_index("core")
    step = math.gcd(share, 8)
    for k in range(layers):
        for ref, core in ((mine_ref, core_pos), (theirs_ref, 1 - core_pos)):
            first = ((k ^ layer_pos) * cores + core) * share
            rows = turned_ref[pl.ds(pl.multiple_of(first // 8 * 8, 8), -(-share // 8) * 8), :]
            for start in range(step, 8, step):
                rows = jnp.where(first % 8 == start, pltpu.roll(rows, rows.shape[0] - start, 0), rows)
            ref[k] = rows[:share].astype(low)


def own_kernel(*refs):
    for k in range(len(refs) // 2):
        refs[len(refs) // 2 + k][...] = refs[k][...]


def text_kernel(image_ref, *refs):
    *in_refs, image_out_ref, low_ref = refs
    rows_kernel(*in_refs, low_ref)
    image_out_ref[...] = image_ref[...]


def rows_kernel(*refs):
    *block_refs, head_ref, low_ref = refs
    low_ref[...] = project(jnp.concatenate([ref[...] for ref in block_refs]), head_ref[...])[1]


def half_kernel(near_ref, far_ref, own_ref, *block_refs):
    total = near_ref[...] + far_ref[...].astype(wide)
    rows = own_ref.shape[0]
    own_ref[...] = total[:rows]
    for k, ref in enumerate(block_refs):
        ref[...] = total[(k + 1) * rows : (k + 2) * rows].astype(ref.dtype)


def back_of(own_ref, before_ref, part_refs):
    total = own_ref[...]
    for ref in part_refs:
        total = total + ref[...].astype(wide)
    unit, inverse = normalized(before_ref[...])
    grad_unit = logit_scale * total
    inner_sum = jnp.sum(unit * grad_unit, axis=1, keepdims=True)
    return (inverse * (grad_unit - unit * inner_sum)).astype(low)


def backs_kernel(layers, groups, *refs):
    image_refs, refs = refs[: layers + 1], refs[layers + 1 :]
    text_refs, refs = refs[: groups + 1], refs[groups + 1 :]
    image_ref, text_ref, *out_refs, all_ref = refs
    width, lanes = image_ref.shape[1], out_refs[0].shape[1]
    image_ref[...] = back_of(*image_refs[:2], image_refs[2:])
    text_ref[...] = back_of(*text_refs[:2], text_refs[2:])
    all_ref[:, :width] = image_ref[...]
    all_ref[:, width : 2 * width] = text_ref[...]
    if all_ref.shape[1] > 2 * width:
        all_ref[:, 2 * width :] = jnp.zeros((all_ref.shape[0], all_ref.shape[1] - 2 * width), low)
    for k, ref in enumerate(out_refs):
        ref[...] = all_ref[:, pl.ds(pl.multiple_of((k ^ lax.axis_index("blk")) * lanes, 128), lanes)]


def grad_kernel(back_ref, head_ref, out_ref):
    out_ref[...] = dot(back_ref[...], head_ref[...], 1, 1).astype(low)


def sum_kernel(own_ref, *refs):
    *part_refs, out_ref = refs
    total = own_ref[...]
    for ref in part_refs:
        total = total + ref[...].astype(wide)
    out_ref[...] = total.astype(low)


def tile_kernel(images_ref, near_ref, far_ref, own_ref, *refs):
    *part_refs, near_part_ref, far_part_ref = refs
    images = images_ref[...]
    rows = own_ref.shape[0]
    near, far = near_ref[...], far_ref[...]
    logits = logit_scale * dot(images, near, 1, 1) + logit_bias
    row = lax.broadcasted_iota(jnp.int32, logits.shape, 0)
    column = lax.broadcasted_iota(jnp.int32, logits.shape, 1)
    sign = jnp.where((row == column) & (row < rows), wide(1.0), wide(-1.0))
    near_weight = (-sign * jax.nn.sigmoid(-sign * logits)).astype(low)
    far_weight = jax.nn.sigmoid(logit_scale * dot(images, far, 1, 1) + logit_bias).astype(low)
    far_part_ref[...] = dot(far_weight, images, 0, 0).astype(low)
    near_part_ref[...] = dot(near_weight, images, 0, 0)
    parts = dot(near_weight, near, 1, 0) + dot(far_weight, far, 1, 0)
    own_ref[...] = parts[:rows]
    for k, ref in enumerate(part_refs):
        ref[...] = parts[(k + 1) * rows : (k + 2) * rows].astype(low)


def terms_kernel(width, turned_ref, *refs):
    *back_refs, out_ref = refs
    backs = jnp.concatenate([ref[...] for ref in back_refs])
    lanes = backs.shape[1]
    of_image = lax.broadcasted_iota(jnp.int32, backs.shape, 1) + lax.axis_index("blk") * lanes < width
    zero = jnp.zeros_like(backs)
    backs = jnp.concatenate([jnp.where(of_image, backs, zero), jnp.where(of_image, zero, backs)])
    for k in range(out_ref.shape[0]):
        out_ref[k] = dot(turned_ref[k], backs, 1, 0).astype(out_ref.dtype)


def token_kernel(out_ref):
    out_ref[...] = jnp.zeros_like(out_ref)


def layers_kernel(cut, mine_ref, theirs_ref, *refs):
    for k in range(mine_ref.shape[0]):
        total = mine_ref[k] + theirs_ref[k].astype(wide)
        refs[2 * k][...] = total[:, :cut].astype(refs[2 * k].dtype)
        refs[2 * k + 1][...] = total[:, cut:].astype(refs[2 * k].dtype)


def heads_kernel(groups, cut, *refs):
    *block_refs, image_ref, text_ref, all_ref = refs
    width, lanes = image_ref.shape[1], all_ref.shape[1] // groups
    for k in range(groups):
        first = pl.multiple_of((k ^ lax.axis_index("blk")) * lanes, 128)
        all_ref[:, pl.ds(first, cut)] = block_refs[k][...].astype(wide)
        all_ref[:, pl.ds(first + cut, lanes - cut)] = block_refs[groups + k][...].astype(wide)
    image_ref[...] = all_ref[:, :width]
    text_ref[...] = all_ref[:, width : 2 * width]


def per_device(images, captions, image_head, text_head):
    groups = lax.axis_size("blk")
    layers = lax.axis_size("layer")
    cores = lax.axis_size("core")
    rows, width = images.shape
    half = groups * rows

    def over(array, axis, by):
        return lax.ppermute(array, axis, [(i, i ^ by) for i in range(lax.axis_size(axis))])

    def over_blk(array):
        return [array] + [over(array, "blk", k) for k in range(1, groups)]

    def over_layers(blocks):
        parts = [over(block, "layer", k) for k, block in reversed(list(enumerate(blocks, 1)))]
        return parts[::-1]

    def over_core(array):
        return over(array, "core", 1)

    share = width // (layers * cores)
    lanes = -(-2 * width // (128 * groups)) * 128
    cut = -(-lanes // 256) * 128
    assert width % 128 == 0 and cores == 2

    block = (rows, width)

    caption_blocks = over_blk(captions)
    image_blocks = over_layers([images] * (layers - 1))
    image_own, text_own = call(own_kernel, [(block, low)] * 2, images, captions, cost=10)
    caption_blocks[0] = text_own
    outs = [(block, low), ((half, width), low)]
    image_own, near_low = call(text_kernel, outs, image_own, *caption_blocks, text_head, cost=2)
    image_group = over_blk(image_own)
    far_low = over_core(near_low)
    image_low = call(
        rows_kernel,
        [((layers * rows, width), low)],
        *(image_own, *image_blocks, image_head),
        behind=(near_low,),
        cost=10,
    )[0]
    outs = [(block, wide)] + [(block, low)] * (layers - 1) + [((half, width), wide), ((half, width), low)]
    image_total, *image_out, near_part, far_part = call(tile_kernel, outs, image_low, near_low, far_low, cost=1, behind=image_group[1:])
    image_parts = [over(block, "layer", k + 1) for k, block in enumerate(image_out)]
    outs = [(block, wide)] + [(block, low)] * (groups - 1)
    text_total, *text_out = call(half_kernel, outs, near_part, over_core(far_part), cost=1)
    text_parts = [over(block, "blk", k + 1) for k, block in enumerate(text_out)]

    turned = ((layers, share, 2 * half), low)
    image_before, text_before, turned_mine, turned_theirs = call(
        functools.partial(ready_kernel, (groups, layers, cores)),
        [(block, wide), (block, wide), turned, turned],
        *(image_head, text_head, *image_group, *caption_blocks),
        scratch=[((width, 2 * half), wide)],
        behind=text_out[:1],
    )
    image_back, text_back, *sends = call(
        functools.partial(backs_kernel, layers, groups),
        [(block, low)] * 2 + [((rows, lanes), low)] * groups,
        *(image_total, image_before, *image_parts, text_total, text_before, *text_parts),
        cost=80,
        scratch=[((rows, groups * lanes), low)],
    )
    backs = [sends[0]] + [over(block, "blk", k + 1) for k, block in enumerate(sends[1:])]
    shape = (layers, share, lanes)
    kernel = functools.partial(terms_kernel, width)
    theirs = call(kernel, [(shape, low)], turned_theirs, *backs)[0]
    mine = call(kernel, [(shape, wide)], turned_mine, *backs, behind=[theirs])[0]
    first, second = (share, cut), (share, lanes - cut)
    outs = [(first, wide), (second, wide)] + [(first, low), (second, low)] * (layers - 1)
    terms = call(functools.partial(layers_kernel, cut), outs, mine, over_core(theirs))
    first_parts, second_parts = (
        [over(part, "layer", k + 1) for k, part in enumerate(terms[i::2])] for i in (2, 3)
    )
    first_sum = call(sum_kernel, [(first, low)], terms[0], *first_parts, cost=50)[0]
    first_sums = over_blk(first_sum)
    second_sum = call(sum_kernel, [(second, low)], terms[1], *second_parts, cost=1)[0]
    token = call(token_kernel, [((8, 128), wide)], behind=first_sums, cost=10)[0]
    blocks = first_sums + over_blk(second_sum)
    grad_images = call(grad_kernel, [(block, low)], image_back, image_head, behind=[second_sum])[0]
    grad_captions = call(grad_kernel, [(block, low)], text_back, text_head, behind=[second_sum])[0]
    grad_image_head, grad_text_head = call(
        functools.partial(heads_kernel, groups, cut),
        [((share, width), wide)] * 2,
        *blocks,
        scratch=[((share, groups * lanes), wide)],
        behind=[token],
    )
    return (grad_images, grad_captions, grad_image_head, grad_text_head)


def solution(mesh):
    groups, members = mesh.devices.shape
    fine = Mesh(mesh.devices.reshape(groups, members // 2, 2), ("blk", "layer", "core"))
    pairs, share = P(("blk", "layer", "core"), None), P(("layer", "core"), None)
    return jax.shard_map(
        per_device,
        mesh=fine,
        in_specs=(pairs, pairs, P(), P()),
        out_specs=(pairs, pairs, share, share),
        check_vma=False,
    )
```

time: 124 us -> 86.8 us (0.70)
  matrix products: 25.3 us -> 0 us
  Pallas kernels: 0 us -> 12.1 us
  local copies, waits for them, and re-layouts: 11.1 us -> 0.95 us
  other arithmetic: 8.68 us -> 0 us
  starting transfers between devices: 42.8 us -> 39.7 us
  waiting for transfers between devices: 34.9 us -> 33.2 us
    dot_general x20 -> x0, matrix products: 25.3 us -> none  [dot(): lax.dot_general(a, b, (((a_dim,), (b_dim,)), ((), ())), preferred_element...]
    pallas_call x0 -> x16, Pallas kernels: none -> 12.1 us  [call(): pl.pallas_call(body, out_shape=tuple((jax.ShapeDtypeStruct(shape, kind) f...]
    unnamed x54 -> x6, local copies, waits for them, and re-layouts: 8.16 us -> 0.95 us
    convert_element_type x7 -> x0, other arithmetic: 3.42 us -> none  [the longest x2 2.1 us: head_gradient(): total = total.astype(low)]
    ppermute x38 -> x33, starting transfers between devices: 42.8 us -> 39.7 us  [over(): lax.ppermute(array, axis, [(i, i ^ by) for i in range(lax.axis_size(axis))])]
    slice x6 -> x0, local copies, waits for them, and re-layouts: 1.85 us -> none  [the longest x2 1.74 us: head_gradient(): block = terms[k * padded:(k + 1) * padded]]
    ppermute x38 -> x33, waiting for transfers between devices: 34.9 us -> 33.2 us  [over(): lax.ppermute(array, axis, [(i, i ^ by) for i in range(lax.axis_size(axis))])]
  transfers between devices with their start and end apart: 38 -> 33, of which waited for: 13 -> 15; matrix products, arithmetic and copies ran while one was open for 34% -> 0% of each run, Pallas kernels for 0% -> 10%
where the time goes in v3:
time: 86.8 us; the launch traced here: 86.7 us
  starting transfers between devices  39.7 us (46%)
  waiting for transfers between devices  33.2 us (38%)
  Pallas kernels  12.1 us (14%)
  local copies, waits for them, and re-layouts  0.95 us (1%)
    ppermute x33, starting transfers between devices, over(): lax.ppermute(array, axis, [(i, i ^ by) for i in range(lax.axis_size(axis))])  39.7 us
    ppermute x33, waiting for transfers between devices, over(): lax.ppermute(array, axis, [(i, i ^ by) for i in range(lax.axis_size(axis))])  33.2 us
    pallas_call x16, Pallas kernels, call(): pl.pallas_call(body, out_shape=tuple((jax.ShapeDtypeStruct(shape, kind) f...  12.1 us
  transfers between devices with their start and end apart: 33, of which 15 were waited for; matrix products, arithmetic and copies ran while one was open for 0% of the time, Pallas kernels for 10%

profile of v3, /device:TPU:0, one launch (start us, length us, event | category | flops | bytes accessed | tf_op | source)
XLA Modules:
  0.0 86.7 jit_solution(15075563069407617260)
XLA Ops:
  0.6 3.1 %collective-permute-start.3 = (bf16[64,1152]{1,0:T(8,128)(2,1)}, bf16[64,1152]{1,0:T(8,128)(2,1)S(1)}, u32[]{:S(2)}, u32[]{:S(2)}) collective-permute-start(bf16[64,1152]{1,0:T(8,128)(2,1)} %refs_0_.2), channel_id=1, source_target_pairs={{0,2},{2,0},{4,6},{6,4},{1,3},{3,1},{5,7},{7,5},{8,10},{10,8},{12,... | collective-permute-start | bytes 442376 | tf_op jit(solution)/shard_map/ppermute | solution.py:194
  3.7 2.5 %collective-permute-start.5 = (bf16[64,1152]{1,0:T(8,128)(2,1)}, bf16[64,1152]{1,0:T(8,128)(2,1)S(1)}, u32[]{:S(2)}, u32[]{:S(2)}) collective-permute-start(bf16[64,1152]{1,0:T(8,128)(2,1)} %refs_0_.2), channel_id=1, source_target_pairs={{0,6},{2,4},{4,2},{6,0},{1,7},{3,5},{5,3},{7,1},{8,14},{10,12},{12... | collective-permute-start | bytes 442376 | tf_op jit(solution)/shard_map/ppermute | solution.py:194
  6.2 1.5 %collective-permute-start = (bf16[64,1152]{1,0:T(8,128)(2,1)}, bf16[64,1152]{1,0:T(8,128)(2,1)S(1)}, u32[]{:S(2)}, u32[]{:S(2)}) collective-permute-start(bf16[64,1152]{1,0:T(8,128)(2,1)} %refs_1_.4), channel_id=1, source_target_pairs={{0,8},{8,0},{16,24},{24,16},{1,9},{9,1},{17,25},{25,17},{2,10},{10... | collective-permute-start | bytes 442376 | tf_op jit(solution)/shard_map/ppermute | solution.py:194
  7.7 1.5 %collective-permute-start.2 = (bf16[64,1152]{1,0:T(8,128)(2,1)}, bf16[64,1152]{1,0:T(8,128)(2,1)S(1)}, u32[]{:S(2)}, u32[]{:S(2)}) collective-permute-start(bf16[64,1152]{1,0:T(8,128)(2,1)} %refs_1_.4), channel_id=1, source_target_pairs={{0,24},{8,16},{16,8},{24,0},{1,25},{9,17},{17,9},{25,1},{2,26},{10... | collective-permute-start | bytes 442376 | tf_op jit(solution)/shard_map/ppermute | solution.py:194
  12.9 2.7 %collective-permute-done.2.refs_4_.refs_9_ = bf16[64,1152]{1,0:T(8,128)(2,1)S(1)} collective-permute-done((bf16[64,1152]{1,0:T(8,128)(2,1)}, bf16[64,1152]{1,0:T(8,128)(2,1)S(1)}, u32[]{:S(2)}, u32[]{:S(2)}) %collective-permute-start.2) | collective-permute-done | bytes 147488 | tf_op jit(solution)/shard_map/ppermute | solution.py:194
  18.1 1.5 %collective-permute-start.9 = (bf16[64,1152]{1,0:T(8,128)(2,1)S(1)}, bf16[64,1152]{1,0:T(8,128)(2,1)S(1)}, u32[]{:S(2)}, u32[]{:S(2)}) collective-permute-start(bf16[64,1152]{1,0:T(8,128)(2,1)S(1)} %get-tuple-element.40.refs_0_.refs_2_), channel_id=1, source_target_pairs={{0,24},{8,16},{16,8},{24,0},{1,25},{9,17},{17,9},{25,1},{2,26},{10... | collective-permute-start | bytes 442376 | tf_op jit(solution)/shard_map/ppermute | solution.py:194
  19.7 1.5 %collective-permute-start.8 = (bf16[64,1152]{1,0:T(8,128)(2,1)S(1)}, bf16[64,1152]{1,0:T(8,128)(2,1)S(1)}, u32[]{:S(2)}, u32[]{:S(2)}) collective-permute-start(bf16[64,1152]{1,0:T(8,128)(2,1)S(1)} %get-tuple-element.40.refs_0_.refs_2_), channel_id=1, source_target_pairs={{0,16},{8,24},{16,0},{24,8},{1,17},{9,25},{17,1},{25,9},{2,18},{10... | collective-permute-start | bytes 442376 | tf_op jit(solution)/shard_map/ppermute | solution.py:194
  22.8 2.6 %collective-permute-done.9.refs_5_ = bf16[64,1152]{1,0:T(8,128)(2,1)S(1)} collective-permute-done((bf16[64,1152]{1,0:T(8,128)(2,1)S(1)}, bf16[64,1152]{1,0:T(8,128)(2,1)S(1)}, u32[]{:S(2)}, u32[]{:S(2)}) %collective-permute-start.9) | collective-permute-done | bytes 147488 | tf_op jit(solution)/shard_map/ppermute | solution.py:194
  25.5 1.5 %collective-permute-done.8.refs_4_ = bf16[64,1152]{1,0:T(8,128)(2,1)S(1)} collective-permute-done((bf16[64,1152]{1,0:T(8,128)(2,1)S(1)}, bf16[64,1152]{1,0:T(8,128)(2,1)S(1)}, u32[]{:S(2)}, u32[]{:S(2)}) %collective-permute-start.8) | collective-permute-done | bytes 147488 | tf_op jit(solution)/shard_map/ppermute | solution.py:194
  30.5 2.5 %collective-permute-start.13 = (bf16[64,1152]{1,0:T(8,128)(2,1)S(1)}, bf16[64,1152]{1,0:T(8,128)(2,1)S(1)}, u32[]{:S(2)}, u32[]{:S(2)}) collective-permute-start(bf16[64,1152]{1,0:T(8,128)(2,1)S(1)} %get-tuple-element.49), channel_id=1, source_target_pairs={{0,6},{2,4},{4,2},{6,0},{1,7},{3,5},{5,3},{7,1},{8,14},{10,12},{12... | collective-permute-start | bytes 442376 | tf_op jit(solution)/shard_map/ppermute | solution.py:194
  33.7 1.6 %collective-permute-start.16 = (bf16[64,1152]{1,0:T(8,128)(2,1)S(1)}, bf16[64,1152]{1,0:T(8,128)(2,1)S(1)}, u32[]{:S(2)}, u32[]{:S(2)}) collective-permute-start(bf16[64,1152]{1,0:T(8,128)(2,1)S(1)} %get-tuple-element.53), channel_id=1, source_target_pairs={{0,24},{8,16},{16,8},{24,0},{1,25},{9,17},{17,9},{25,1},{2,26},{10... | collective-permute-start | bytes 442376 | tf_op jit(solution)/shard_map/ppermute | solution.py:194
  38.3 4.9 %collective-permute-done.12.refs_3_ = bf16[64,1152]{1,0:T(8,128)(2,1)S(1)} collective-permute-done((bf16[64,1152]{1,0:T(8,128)(2,1)S(1)}, bf16[64,1152]{1,0:T(8,128)(2,1)S(1)}, u32[]{:S(2)}, u32[]{:S(2)}) %collective-permute-start.12) | collective-permute-done | bytes 147488 | tf_op jit(solution)/shard_map/ppermute | solution.py:194
  44.4 1.4 %collective-permute-start.18 = (bf16[64,640]{1,0:T(8,128)(2,1)S(1)}, bf16[64,640]{1,0:T(8,128)(2,1)S(1)}, u32[]{:S(2)}, u32[]{:S(2)}) collective-permute-start(bf16[64,640]{1,0:T(8,128)(2,1)S(1)} %get-tuple-element.58), channel_id=1, source_target_pairs={{0,16},{8,24},{16,0},{24,8},{1,17},{9,25},{17,1},{25,9},{2,18},{10... | collective-permute-start | bytes 245768 | tf_op jit(solution)/shard_map/ppermute | solution.py:194
  49.5 1.7 %collective-permute-done.19.refs_4_ = bf16[64,640]{1,0:T(8,128)(2,1)S(1)} collective-permute-done((bf16[64,640]{1,0:T(8,128)(2,1)S(1)}, bf16[64,640]{1,0:T(8,128)(2,1)S(1)}, u32[]{:S(2)}, u32[]{:S(2)}) %collective-permute-start.19) | collective-permute-done | bytes 81952 | tf_op jit(solution)/shard_map/ppermute | solution.py:194
  52.5 1.6 %collective-permute-done.20.refs_1_ = bf16[4,144,640]{2,1,0:T(8,128)(2,1)S(1)} collective-permute-done((bf16[4,144,640]{2,1,0:T(8,128)(2,1)S(1)}, bf16[4,144,640]{2,1,0:T(8,128)(2,1)S(1)}, u32[]{:S(2)}, u32[]{:S(2)}) %collective-permute-start.20) | collective-permute-done | bytes 737312 | tf_op jit(solution)/shard_map/ppermute | solution.py:194
  54.2 3.0 %collective-permute-start.21 = (bf16[144,256]{1,0:T(8,128)(2,1)S(1)}, bf16[144,256]{1,0:T(8,128)(2,1)S(1)}, u32[]{:S(2)}, u32[]{:S(2)}) collective-permute-start(bf16[144,256]{1,0:T(8,128)(2,1)S(1)} %get-tuple-element.62), channel_id=1, source_target_pairs={{0,2},{2,0},{4,6},{6,4},{1,3},{3,1},{5,7},{7,5},{8,10},{10,8},{12,... | collective-permute-start | bytes 221192 | tf_op jit(solution)/shard_map/ppermute | solution.py:194
  57.2 2.4 %collective-permute-start.23 = (bf16[144,256]{1,0:T(8,128)(2,1)S(1)}, bf16[144,256]{1,0:T(8,128)(2,1)S(1)}, u32[]{:S(2)}, u32[]{:S(2)}) collective-permute-start(bf16[144,256]{1,0:T(8,128)(2,1)S(1)} %get-tuple-element.64), channel_id=1, source_target_pairs={{0,6},{2,4},{4,2},{6,0},{1,7},{3,5},{5,3},{7,1},{8,14},{10,12},{12... | collective-permute-start | bytes 221192 | tf_op jit(solution)/shard_map/ppermute | solution.py:194
  61.6 2.4 %collective-permute-start.26 = (bf16[144,384]{1,0:T(8,128)(2,1)S(1)}, bf16[144,384]{1,0:T(8,128)(2,1)S(1)}, u32[]{:S(2)}, u32[]{:S(2)}) collective-permute-start(bf16[144,384]{1,0:T(8,128)(2,1)S(1)} %get-tuple-element.69), channel_id=1, source_target_pairs={{0,6},{2,4},{4,2},{6,0},{1,7},{3,5},{5,3},{7,1},{8,14},{10,12},{12... | collective-permute-start | bytes 331784 | tf_op jit(solution)/shard_map/ppermute | solution.py:194
  64.0 1.6 %collective-permute-done.22.refs_2_ = bf16[144,256]{1,0:T(8,128)(2,1)S(1)} collective-permute-done((bf16[144,256]{1,0:T(8,128)(2,1)S(1)}, bf16[144,256]{1,0:T(8,128)(2,1)S(1)}, u32[]{:S(2)}, u32[]{:S(2)}) %collective-permute-start.22) | collective-permute-done | bytes 73760 | tf_op jit(solution)/shard_map/ppermute | solution.py:194
  67.7 6.6 %collective-permute-done.25.refs_2_ = bf16[144,384]{1,0:T(8,128)(2,1)S(1)} collective-permute-done((bf16[144,384]{1,0:T(8,128)(2,1)S(1)}, bf16[144,384]{1,0:T(8,128)(2,1)S(1)}, u32[]{:S(2)}, u32[]{:S(2)}) %collective-permute-start.25) | collective-permute-done | bytes 110624 | tf_op jit(solution)/shard_map/ppermute | solution.py:194
  76.4 1.5 %collective-permute-start.27 = (bf16[144,384]{1,0:T(8,128)(2,1)S(1)}, bf16[144,384]{1,0:T(8,128)(2,1)S(1)}, u32[]{:S(2)}, u32[]{:S(2)}) collective-permute-start(bf16[144,384]{1,0:T(8,128)(2,1)S(1)} %shard_map.88.refs_0_), channel_id=1, source_target_pairs={{0,8},{8,0},{16,24},{24,16},{1,9},{9,1},{17,25},{25,17},{2,10},{10... | collective-permute-start | bytes 331784 | tf_op jit(solution)/shard_map/ppermute | solution.py:194
  77.9 1.6 %shard_map.87 = bf16[64,1152]{1,0:T(8,128)(2,1)} custom-call(bf16[64,1152]{1,0:T(8,128)(2,1)S(1)} %get-tuple-element.65.refs_0_, bf16[1152,1152]{1,0:T(8,128)(2,1)S(1)} %copy-done, bf16[144,256]{1,0:T(8,128)(2,1)S(1)} %shard_map.85.refs_2_.refs_4_), custom_call_target="tpu_custom_call" | custom-call | flops 1000000000 | bytes 1000000000 | tf_op jit(solution)/shard_map/pallas_call | solution.py:43
  79.5 1.6 %shard_map.86 = bf16[64,1152]{1,0:T(8,128)(2,1)} custom-call(bf16[64,1152]{1,0:T(8,128)(2,1)S(1)} %get-tuple-element.54.refs_0_, bf16[1152,1152]{1,0:T(8,128)(2,1)S(1)} %copy-done.1, bf16[144,256]{1,0:T(8,128)(2,1)S(1)} %shard_map.85.refs_2_.refs_4_), custom_call_target="tpu_custom_call" | custom-call | flops 1000000000 | bytes 1000000000 | tf_op jit(solution)/shard_map/pallas_call | solution.py:43
  82.0 3.5 %collective-permute-done.30.refs_5_ = bf16[144,256]{1,0:T(8,128)(2,1)S(1)} collective-permute-done((bf16[144,256]{1,0:T(8,128)(2,1)S(1)}, bf16[144,256]{1,0:T(8,128)(2,1)S(1)}, u32[]{:S(2)}, u32[]{:S(2)}) %collective-permute-start.30) | collective-permute-done | bytes 73760 | tf_op jit(solution)/shard_map/ppermute | solution.py:194
  (64 shorter events, 29.5 us)
Async XLA Ops:
  0.6 20.5 %collective-permute-start.3 = (bf16[64,1152]{1,0:T(8,128)(2,1)}, bf16[64,1152]{1,0:T(8,128)(2,1)S(1)}, u32[]{:S(2)}, u32[]{:S(2)}) collective-permute-start(bf16[64,1152]{1,0:T(8,128)(2,1)} %refs_0_.2), channel_id=1, source_target_pairs={{0,2},{2,0},{4,6},{6,4},{1,3},{3,1},{5,7},{7,5},{8,10},{10,8},{12,... | collective-permute-start | bytes 442376 | tf_op jit(solution)/shard_map/ppermute | solution.py:194
  3.7 18.0 %collective-permute-start.5 = (bf16[64,1152]{1,0:T(8,128)(2,1)}, bf16[64,1152]{1,0:T(8,128)(2,1)S(1)}, u32[]{:S(2)}, u32[]{:S(2)}) collective-permute-start(bf16[64,1152]{1,0:T(8,128)(2,1)} %refs_0_.2), channel_id=1, source_target_pairs={{0,6},{2,4},{4,2},{6,0},{1,7},{3,5},{5,3},{7,1},{8,14},{10,12},{12... | collective-permute-start | bytes 442376 | tf_op jit(solution)/shard_map/ppermute | solution.py:194
  6.2 6.5 %collective-permute-start = (bf16[64,1152]{1,0:T(8,128)(2,1)}, bf16[64,1152]{1,0:T(8,128)(2,1)S(1)}, u32[]{:S(2)}, u32[]{:S(2)}) collective-permute-start(bf16[64,1152]{1,0:T(8,128)(2,1)} %refs_1_.4), channel_id=1, source_target_pairs={{0,8},{8,0},{16,24},{24,16},{1,9},{9,1},{17,25},{25,17},{2,10},{10... | collective-permute-start | bytes 442376 | tf_op jit(solution)/shard_map/ppermute | solution.py:194
  7.7 7.9 %collective-permute-start.2 = (bf16[64,1152]{1,0:T(8,128)(2,1)}, bf16[64,1152]{1,0:T(8,128)(2,1)S(1)}, u32[]{:S(2)}, u32[]{:S(2)}) collective-permute-start(bf16[64,1152]{1,0:T(8,128)(2,1)} %refs_1_.4), channel_id=1, source_target_pairs={{0,24},{8,16},{16,8},{24,0},{1,25},{9,17},{17,9},{25,1},{2,26},{10... | collective-permute-start | bytes 442376 | tf_op jit(solution)/shard_map/ppermute | solution.py:194
  9.2 7.8 %collective-permute-start.1 = (bf16[64,1152]{1,0:T(8,128)(2,1)}, bf16[64,1152]{1,0:T(8,128)(2,1)S(1)}, u32[]{:S(2)}, u32[]{:S(2)}) collective-permute-start(bf16[64,1152]{1,0:T(8,128)(2,1)} %refs_1_.4), channel_id=1, source_target_pairs={{0,16},{8,24},{16,0},{24,8},{1,17},{9,25},{17,1},{25,9},{2,18},{10... | collective-permute-start | bytes 442376 | tf_op jit(solution)/shard_map/ppermute | solution.py:194
  12.7 9.0 %collective-permute-start.4 = (bf16[64,1152]{1,0:T(8,128)(2,1)}, bf16[64,1152]{1,0:T(8,128)(2,1)S(1)}, u32[]{:S(2)}, u32[]{:S(2)}) collective-permute-start(bf16[64,1152]{1,0:T(8,128)(2,1)} %refs_0_.2), channel_id=1, source_target_pairs={{0,4},{2,6},{4,0},{6,2},{1,5},{3,7},{5,1},{7,3},{8,12},{10,14},{12... | collective-permute-start | bytes 442376 | tf_op jit(solution)/shard_map/ppermute | solution.py:194
  18.1 7.3 %collective-permute-start.9 = (bf16[64,1152]{1,0:T(8,128)(2,1)S(1)}, bf16[64,1152]{1,0:T(8,128)(2,1)S(1)}, u32[]{:S(2)}, u32[]{:S(2)}) collective-permute-start(bf16[64,1152]{1,0:T(8,128)(2,1)S(1)} %get-tuple-element.40.refs_0_.refs_2_), channel_id=1, source_target_pairs={{0,24},{8,16},{16,8},{24,0},{1,25},{9,17},{17,9},{25,1},{2,26},{10... | collective-permute-start | bytes 442376 | tf_op jit(solution)/shard_map/ppermute | solution.py:194
  19.7 7.3 %collective-permute-start.8 = (bf16[64,1152]{1,0:T(8,128)(2,1)S(1)}, bf16[64,1152]{1,0:T(8,128)(2,1)S(1)}, u32[]{:S(2)}, u32[]{:S(2)}) collective-permute-start(bf16[64,1152]{1,0:T(8,128)(2,1)S(1)} %get-tuple-element.40.refs_0_.refs_2_), channel_id=1, source_target_pairs={{0,16},{8,24},{16,0},{24,8},{1,17},{9,25},{17,1},{25,9},{2,18},{10... | collective-permute-start | bytes 442376 | tf_op jit(solution)/shard_map/ppermute | solution.py:194
  28.5 8.0 %collective-permute-start.11 = (bf16[64,1152]{1,0:T(8,128)(2,1)S(1)}, bf16[64,1152]{1,0:T(8,128)(2,1)S(1)}, u32[]{:S(2)}, u32[]{:S(2)}) collective-permute-start(bf16[64,1152]{1,0:T(8,128)(2,1)S(1)} %get-tuple-element.47), channel_id=1, source_target_pairs={{0,2},{2,0},{4,6},{6,4},{1,3},{3,1},{5,7},{7,5},{8,10},{10,8},{12,... | collective-permute-start | bytes 442376 | tf_op jit(solution)/shard_map/ppermute | solution.py:194
  29.2 14.0 %collective-permute-start.12 = (bf16[64,1152]{1,0:T(8,128)(2,1)S(1)}, bf16[64,1152]{1,0:T(8,128)(2,1)S(1)}, u32[]{:S(2)}, u32[]{:S(2)}) collective-permute-start(bf16[64,1152]{1,0:T(8,128)(2,1)S(1)} %get-tuple-element.48), channel_id=1, source_target_pairs={{0,4},{2,6},{4,0},{6,2},{1,5},{3,7},{5,1},{7,3},{8,12},{10,14},{12... | collective-permute-start | bytes 442376 | tf_op jit(solution)/shard_map/ppermute | solution.py:194
  30.5 12.7 %collective-permute-start.13 = (bf16[64,1152]{1,0:T(8,128)(2,1)S(1)}, bf16[64,1152]{1,0:T(8,128)(2,1)S(1)}, u32[]{:S(2)}, u32[]{:S(2)}) collective-permute-start(bf16[64,1152]{1,0:T(8,128)(2,1)S(1)} %get-tuple-element.49), channel_id=1, source_target_pairs={{0,6},{2,4},{4,2},{6,0},{1,7},{3,5},{5,3},{7,1},{8,14},{10,12},{12... | collective-permute-start | bytes 442376 | tf_op jit(solution)/shard_map/ppermute | solution.py:194
  33.0 10.1 %collective-permute-start.15 = (bf16[64,1152]{1,0:T(8,128)(2,1)S(1)}, bf16[64,1152]{1,0:T(8,128)(2,1)S(1)}, u32[]{:S(2)}, u32[]{:S(2)}) collective-permute-start(bf16[64,1152]{1,0:T(8,128)(2,1)S(1)} %get-tuple-element.52), channel_id=1, source_target_pairs={{0,16},{8,24},{16,0},{24,8},{1,17},{9,25},{17,1},{25,9},{2,18},{10... | collective-permute-start | bytes 442376 | tf_op jit(solution)/shard_map/ppermute | solution.py:194
  33.7 9.5 %collective-permute-start.16 = (bf16[64,1152]{1,0:T(8,128)(2,1)S(1)}, bf16[64,1152]{1,0:T(8,128)(2,1)S(1)}, u32[]{:S(2)}, u32[]{:S(2)}) collective-permute-start(bf16[64,1152]{1,0:T(8,128)(2,1)S(1)} %get-tuple-element.53), channel_id=1, source_target_pairs={{0,24},{8,16},{16,8},{24,0},{1,25},{9,17},{17,9},{25,1},{2,26},{10... | collective-permute-start | bytes 442376 | tf_op jit(solution)/shard_map/ppermute | solution.py:194
  36.5 6.7 %collective-permute-start.14 = (bf16[64,1152]{1,0:T(8,128)(2,1)S(1)}, bf16[64,1152]{1,0:T(8,128)(2,1)S(1)}, u32[]{:S(2)}, u32[]{:S(2)}) collective-permute-start(bf16[64,1152]{1,0:T(8,128)(2,1)S(1)} %get-tuple-element.45.refs_10_), channel_id=1, source_target_pairs={{0,8},{8,0},{16,24},{24,16},{1,9},{9,1},{17,25},{25,17},{2,10},{10... | collective-permute-start | bytes 442376 | tf_op jit(solution)/shard_map/ppermute | solution.py:194
  54.2 7.4 %collective-permute-start.21 = (bf16[144,256]{1,0:T(8,128)(2,1)S(1)}, bf16[144,256]{1,0:T(8,128)(2,1)S(1)}, u32[]{:S(2)}, u32[]{:S(2)}) collective-permute-start(bf16[144,256]{1,0:T(8,128)(2,1)S(1)} %get-tuple-element.62), channel_id=1, source_target_pairs={{0,2},{2,0},{4,6},{6,4},{1,3},{3,1},{5,7},{7,5},{8,10},{10,8},{12,... | collective-permute-start | bytes 221192 | tf_op jit(solution)/shard_map/ppermute | solution.py:194
  57.2 8.4 %collective-permute-start.22 = (bf16[144,256]{1,0:T(8,128)(2,1)S(1)}, bf16[144,256]{1,0:T(8,128)(2,1)S(1)}, u32[]{:S(2)}, u32[]{:S(2)}) collective-permute-start(bf16[144,256]{1,0:T(8,128)(2,1)S(1)} %get-tuple-element.63), channel_id=1, source_target_pairs={{0,4},{2,6},{4,0},{6,2},{1,5},{3,7},{5,1},{7,3},{8,12},{10,14},{12... | collective-permute-start | bytes 221192 | tf_op jit(solution)/shard_map/ppermute | solution.py:194
  57.2 8.4 %collective-permute-start.23 = (bf16[144,256]{1,0:T(8,128)(2,1)S(1)}, bf16[144,256]{1,0:T(8,128)(2,1)S(1)}, u32[]{:S(2)}, u32[]{:S(2)}) collective-permute-start(bf16[144,256]{1,0:T(8,128)(2,1)S(1)} %get-tuple-element.64), channel_id=1, source_target_pairs={{0,6},{2,4},{4,2},{6,0},{1,7},{3,5},{5,3},{7,1},{8,14},{10,12},{12... | collective-permute-start | bytes 221192 | tf_op jit(solution)/shard_map/ppermute | solution.py:194
  59.6 8.0 %collective-permute-start.24 = (bf16[144,384]{1,0:T(8,128)(2,1)S(1)}, bf16[144,384]{1,0:T(8,128)(2,1)S(1)}, u32[]{:S(2)}, u32[]{:S(2)}) collective-permute-start(bf16[144,384]{1,0:T(8,128)(2,1)S(1)} %get-tuple-element.67), channel_id=1, source_target_pairs={{0,2},{2,0},{4,6},{6,4},{1,3},{3,1},{5,7},{7,5},{8,10},{10,8},{12,... | collective-permute-start | bytes 331784 | tf_op jit(solution)/shard_map/ppermute | solution.py:194
  60.7 13.6 %collective-permute-start.25 = (bf16[144,384]{1,0:T(8,128)(2,1)S(1)}, bf16[144,384]{1,0:T(8,128)(2,1)S(1)}, u32[]{:S(2)}, u32[]{:S(2)}) collective-permute-start(bf16[144,384]{1,0:T(8,128)(2,1)S(1)} %get-tuple-element.68), channel_id=1, source_target_pairs={{0,4},{2,6},{4,0},{6,2},{1,5},{3,7},{5,1},{7,3},{8,12},{10,14},{12... | collective-permute-start | bytes 331784 | tf_op jit(solution)/shard_map/ppermute | solution.py:194
  61.6 12.7 %collective-permute-start.26 = (bf16[144,384]{1,0:T(8,128)(2,1)S(1)}, bf16[144,384]{1,0:T(8,128)(2,1)S(1)}, u32[]{:S(2)}, u32[]{:S(2)}) collective-permute-start(bf16[144,384]{1,0:T(8,128)(2,1)S(1)} %get-tuple-element.69), channel_id=1, source_target_pairs={{0,6},{2,4},{4,2},{6,0},{1,7},{3,5},{5,3},{7,1},{8,14},{10,12},{12... | collective-permute-start | bytes 331784 | tf_op jit(solution)/shard_map/ppermute | solution.py:194
  65.6 16.3 %collective-permute-start.32 = (bf16[144,256]{1,0:T(8,128)(2,1)S(1)}, bf16[144,256]{1,0:T(8,128)(2,1)S(1)}, u32[]{:S(2)}, u32[]{:S(2)}) collective-permute-start(bf16[144,256]{1,0:T(8,128)(2,1)S(1)} %shard_map.85.refs_2_.refs_4_), channel_id=1, source_target_pairs={{0,24},{8,16},{16,8},{24,0},{1,25},{9,17},{17,9},{25,1},{2,26},{10... | collective-permute-start | bytes 221192 | tf_op jit(solution)/shard_map/ppermute | solution.py:194
  67.1 14.9 %collective-permute-start.31 = (bf16[144,256]{1,0:T(8,128)(2,1)S(1)}, bf16[144,256]{1,0:T(8,128)(2,1)S(1)}, u32[]{:S(2)}, u32[]{:S(2)}) collective-permute-start(bf16[144,256]{1,0:T(8,128)(2,1)S(1)} %shard_map.85.refs_2_.refs_4_), channel_id=1, source_target_pairs={{0,16},{8,24},{16,0},{24,8},{1,17},{9,25},{17,1},{25,9},{2,18},{10... | collective-permute-start | bytes 221192 | tf_op jit(solution)/shard_map/ppermute | solution.py:194
  74.4 6.7 %collective-permute-start.29 = (bf16[144,384]{1,0:T(8,128)(2,1)S(1)}, bf16[144,384]{1,0:T(8,128)(2,1)S(1)}, u32[]{:S(2)}, u32[]{:S(2)}) collective-permute-start(bf16[144,384]{1,0:T(8,128)(2,1)S(1)} %shard_map.88.refs_0_), channel_id=1, source_target_pairs={{0,24},{8,16},{16,8},{24,0},{1,25},{9,17},{17,9},{25,1},{2,26},{10... | collective-permute-start | bytes 331784 | tf_op jit(solution)/shard_map/ppermute | solution.py:194
  75.8 6.2 %collective-permute-start.28 = (bf16[144,384]{1,0:T(8,128)(2,1)S(1)}, bf16[144,384]{1,0:T(8,128)(2,1)S(1)}, u32[]{:S(2)}, u32[]{:S(2)}) collective-permute-start(bf16[144,384]{1,0:T(8,128)(2,1)S(1)} %shard_map.88.refs_0_), channel_id=1, source_target_pairs={{0,16},{8,24},{16,0},{24,8},{1,17},{9,25},{17,1},{25,9},{2,18},{10... | collective-permute-start | bytes 331784 | tf_op jit(solution)/shard_map/ppermute | solution.py:194
  (12 other events, 65.1 us)

commit v4 on v3

--- a/solution.py
+++ b/solution.py
@@ -119,8 +119,10 @@
         ref[...] = all_ref[:, pl.ds(pl.multiple_of((k ^ lax.axis_index("blk")) * lanes, 128), lanes)]
 
 
-def grad_kernel(back_ref, head_ref, out_ref):
-    out_ref[...] = dot(back_ref[...], head_ref[...], 1, 1).astype(low)
+def grads_kernel(image_ref, image_head_ref, text_ref, text_head_ref, image_out_ref, text_out_ref, token_ref):
+    image_out_ref[...] = dot(image_ref[...], image_head_ref[...], 1, 1).astype(low)
+    text_out_ref[...] = dot(text_ref[...], text_head_ref[...], 1, 1).astype(low)
+    token_ref[...] = jnp.zeros_like(token_ref)
 
 
 def sum_kernel(own_ref, *refs):
@@ -161,10 +163,6 @@
         out_ref[k] = dot(turned_ref[k], backs, 1, 0).astype(out_ref.dtype)
 
 
-def token_kernel(out_ref):
-    out_ref[...] = jnp.zeros_like(out_ref)
-
-
 def layers_kernel(cut, mine_ref, theirs_ref, *refs):
     for k in range(mine_ref.shape[0]):
         total = mine_ref[k] + theirs_ref[k].astype(wide)
@@ -211,7 +209,7 @@
     block = (rows, width)
 
     caption_blocks = over_blk(captions)
-    image_blocks = over_layers([images] * (layers - 1))
+    image_blocks = [over(images, "layer", k) for k in range(1, layers)]
     image_own, text_own = call(own_kernel, [(block, low)] * 2, images, captions, cost=10)
     caption_blocks[0] = text_own
     outs = [(block, low), ((half, width), low)]
@@ -226,8 +224,9 @@
         cost=10,
     )[0]
     outs = [(block, wide)] + [(block, low)] * (layers - 1) + [((half, width), wide), ((half, width), low)]
-    image_total, *image_out, near_part, far_part = call(tile_kernel, outs, image_low, near_low, far_low, cost=1, behind=image_group[1:])
-    image_parts = [over(block, "layer", k + 1) for k, block in enumerate(image_out)]
+    image_total, *image_out, near_part, far_part = call(tile_kernel, outs, image_low, near_low, far_low, cost=1)
+    image_out[0] = call(own_kernel, [(block, low)], image_out[0], behind=image_group[1:], cost=6)[0]
+    image_parts = over_layers(image_out)
     outs = [(block, wide)] + [(block, low)] * (groups - 1)
     text_total, *text_out = call(half_kernel, outs, near_part, over_core(far_part), cost=1)
     text_parts = [over(block, "blk", k + 1) for k, block in enumerate(text_out)]
@@ -239,6 +238,7 @@
         *(image_head, text_head, *image_group, *caption_blocks),
         scratch=[((width, 2 * half), wide)],
         behind=text_out[:1],
+        cost=1,
     )
     image_back, text_back, *sends = call(
         functools.partial(backs_kernel, layers, groups),
@@ -256,21 +256,25 @@
     outs = [(first, wide), (second, wide)] + [(first, low), (second, low)] * (layers - 1)
     terms = call(functools.partial(layers_kernel, cut), outs, mine, over_core(theirs))
     first_parts, second_parts = (
-        [over(part, "layer", k + 1) for k, part in enumerate(terms[i::2])] for i in (2, 3)
-    )
-    first_sum = call(sum_kernel, [(first, low)], terms[0], *first_parts, cost=50)[0]
+        [over(terms[2 * k + i], "layer", k) for k in range(layers - 1, 0, -1)] for i in (0, 1)
+    )
+    grad_images, grad_captions, token = call(
+        grads_kernel,
+        [(block, low), (block, low), ((8, 128), wide)],
+        *(image_back, image_head, text_back, text_head),
+        behind=[first_parts[0]],
+    )
+    first_sum = call(sum_kernel, [(first, low)], terms[0], *first_parts, cost=50, behind=[token])[0]
     first_sums = over_blk(first_sum)
     second_sum = call(sum_kernel, [(second, low)], terms[1], *second_parts, cost=1)[0]
-    token = call(token_kernel, [((8, 128), wide)], behind=first_sums, cost=10)[0]
-    blocks = first_sums + over_blk(second_sum)
-    grad_images = call(grad_kernel, [(block, low)], image_back, image_head, behind=[second_sum])[0]
-    grad_captions = call(grad_kernel, [(block, low)], text_back, text_head, behind=[second_sum])[0]
+    last_sum = call(own_kernel, [(second, low)], second_sum, behind=first_sums[1:3], cost=1)[0]
+    second_sums = [second_sum] + [over(second_sum, "blk", k) for k in range(1, groups - 1)]
+    blocks = first_sums + second_sums + [over(last_sum, "blk", groups - 1)]
     grad_image_head, grad_text_head = call(
         functools.partial(heads_kernel, groups, cut),
         [((share, width), wide)] * 2,
         *blocks,
         scratch=[((share, groups * lanes), wide)],
-        behind=[token],
     )
     return (grad_images, grad_captions, grad_image_head, grad_text_head)
 

time: 86.8 us -> 82.3 us (0.948)
  waiting for transfers between devices: 33.2 us -> 23.6 us
  starting transfers between devices: 39.7 us -> 45.6 us
    ppermute x33, waiting for transfers between devices: 33.2 us -> 23.6 us  [over(): lax.ppermute(array, axis, [(i, i ^ by) for i in range(lax.axis_size(axis))])]
    ppermute x33, starting transfers between devices: 39.7 us -> 45.6 us  [over(): lax.ppermute(array, axis, [(i, i ^ by) for i in range(lax.axis_size(axis))])]
  transfers between devices with their start and end apart: 33 -> 33, of which waited for: 15 -> 13; matrix products, arithmetic and copies ran while one was open for 0% -> 0% of each run, Pallas kernels for 10% -> 11%
where the time goes in v4:
time: 82.3 us; the launch traced here: 82.2 us
  starting transfers between devices  45.6 us (55%)
  waiting for transfers between devices  23.6 us (29%)
  Pallas kernels  11.4 us (14%)
  local copies, waits for them, and re-layouts  0.92 us (1%)
    ppermute x33, starting transfers between devices, over(): lax.ppermute(array, axis, [(i, i ^ by) for i in range(lax.axis_size(axis))])  45.6 us
    ppermute x33, waiting for transfers between devices, over(): lax.ppermute(array, axis, [(i, i ^ by) for i in range(lax.axis_size(axis))])  23.6 us
    pallas_call x16, Pallas kernels, call(): pl.pallas_call(body, out_shape=tuple((jax.ShapeDtypeStruct(shape, kind) f...  11.4 us
  transfers between devices with their start and end apart: 33, of which 13 were waited for; matrix products, arithmetic and copies ran while one was open for 0% of the time, Pallas kernels for 11%

profile of v4, /device:TPU:0, one launch (start us, length us, event | category | flops | bytes accessed | tf_op | source)
XLA Modules:
  0.0 82.2 jit_solution(12600776689905509296)
XLA Ops:
  0.6 3.0 %collective-permute-start = (bf16[64,1152]{1,0:T(8,128)(2,1)}, bf16[64,1152]{1,0:T(8,128)(2,1)S(1)}, u32[]{:S(2)}, u32[]{:S(2)}) collective-permute-start(bf16[64,1152]{1,0:T(8,128)(2,1)} %refs_1_.3), channel_id=1, source_target_pairs={{0,8},{8,0},{16,24},{24,16},{1,9},{9,1},{17,25},{25,17},{2,10},{10... | collective-permute-start | bytes 442376 | tf_op jit(solution)/shard_map/ppermute | solution.py:192
  5.2 2.0 %collective-permute-start.3 = (bf16[64,1152]{1,0:T(8,128)(2,1)}, bf16[64,1152]{1,0:T(8,128)(2,1)S(1)}, u32[]{:S(2)}, u32[]{:S(2)}) collective-permute-start(bf16[64,1152]{1,0:T(8,128)(2,1)} %refs_0_.2), channel_id=1, source_target_pairs={{0,2},{2,0},{4,6},{6,4},{1,3},{3,1},{5,7},{7,5},{8,10},{10,8},{12,... | collective-permute-start | bytes 442376 | tf_op jit(solution)/shard_map/ppermute | solution.py:192
  7.2 2.6 %collective-permute-start.4 = (bf16[64,1152]{1,0:T(8,128)(2,1)}, bf16[64,1152]{1,0:T(8,128)(2,1)S(1)}, u32[]{:S(2)}, u32[]{:S(2)}) collective-permute-start(bf16[64,1152]{1,0:T(8,128)(2,1)} %refs_0_.2), channel_id=1, source_target_pairs={{0,4},{2,6},{4,0},{6,2},{1,5},{3,7},{5,1},{7,3},{8,12},{10,14},{12... | collective-permute-start | bytes 442376 | tf_op jit(solution)/shard_map/ppermute | solution.py:192
  13.5 1.9 %collective-permute-start.7 = (bf16[64,1152]{1,0:T(8,128)(2,1)S(1)}, bf16[64,1152]{1,0:T(8,128)(2,1)S(1)}, u32[]{:S(2)}, u32[]{:S(2)}) collective-permute-start(bf16[64,1152]{1,0:T(8,128)(2,1)S(1)} %get-tuple-element.43.refs_0_.refs_2_), channel_id=1, source_target_pairs={{0,8},{8,0},{16,24},{24,16},{1,9},{9,1},{17,25},{25,17},{2,10},{10... | collective-permute-start | bytes 442376 | tf_op jit(solution)/shard_map/ppermute | solution.py:192
  17.0 3.3 %collective-permute-done.4.refs_2_ = bf16[64,1152]{1,0:T(8,128)(2,1)S(1)} collective-permute-done((bf16[64,1152]{1,0:T(8,128)(2,1)}, bf16[64,1152]{1,0:T(8,128)(2,1)S(1)}, u32[]{:S(2)}, u32[]{:S(2)}) %collective-permute-start.4) | collective-permute-done | bytes 147488 | tf_op jit(solution)/shard_map/ppermute | solution.py:192
  24.0 1.7 %collective-permute-start.11 = (bf16[64,1152]{1,0:T(8,128)(2,1)S(1)}, bf16[64,1152]{1,0:T(8,128)(2,1)S(1)}, u32[]{:S(2)}, u32[]{:S(2)}) collective-permute-start(bf16[64,1152]{1,0:T(8,128)(2,1)S(1)} %shard_map.81), channel_id=1, source_target_pairs={{0,2},{2,0},{4,6},{6,4},{1,3},{3,1},{5,7},{7,5},{8,10},{10,8},{12,... | collective-permute-start | bytes 442376 | tf_op jit(solution)/shard_map/ppermute | solution.py:192
  25.6 1.9 %collective-permute-start.12 = (bf16[64,1152]{1,0:T(8,128)(2,1)S(1)}, bf16[64,1152]{1,0:T(8,128)(2,1)S(1)}, u32[]{:S(2)}, u32[]{:S(2)}) collective-permute-start(bf16[64,1152]{1,0:T(8,128)(2,1)S(1)} %get-tuple-element.51), channel_id=1, source_target_pairs={{0,4},{2,6},{4,0},{6,2},{1,5},{3,7},{5,1},{7,3},{8,12},{10,14},{12... | collective-permute-start | bytes 442376 | tf_op jit(solution)/shard_map/ppermute | solution.py:192
  28.5 1.6 %collective-permute-start.14 = (bf16[64,1152]{1,0:T(8,128)(2,1)S(1)}, bf16[64,1152]{1,0:T(8,128)(2,1)S(1)}, u32[]{:S(2)}, u32[]{:S(2)}) collective-permute-start(bf16[64,1152]{1,0:T(8,128)(2,1)S(1)} %get-tuple-element.48.refs_10_), channel_id=1, source_target_pairs={{0,8},{8,0},{16,24},{24,16},{1,9},{9,1},{17,25},{25,17},{2,10},{10... | collective-permute-start | bytes 442376 | tf_op jit(solution)/shard_map/ppermute | solution.py:192
  32.9 2.5 %collective-permute-start.16 = (bf16[64,1152]{1,0:T(8,128)(2,1)S(1)}, bf16[64,1152]{1,0:T(8,128)(2,1)S(1)}, u32[]{:S(2)}, u32[]{:S(2)}) collective-permute-start(bf16[64,1152]{1,0:T(8,128)(2,1)S(1)} %get-tuple-element.56), channel_id=1, source_target_pairs={{0,24},{8,16},{16,8},{24,0},{1,25},{9,17},{17,9},{25,1},{2,26},{10... | collective-permute-start | bytes 442376 | tf_op jit(solution)/shard_map/ppermute | solution.py:192
  36.5 3.1 %collective-permute-done.12.refs_3_ = bf16[64,1152]{1,0:T(8,128)(2,1)S(1)} collective-permute-done((bf16[64,1152]{1,0:T(8,128)(2,1)S(1)}, bf16[64,1152]{1,0:T(8,128)(2,1)S(1)}, u32[]{:S(2)}, u32[]{:S(2)}) %collective-permute-start.12) | collective-permute-done | bytes 147488 | tf_op jit(solution)/shard_map/ppermute | solution.py:192
  40.0 1.6 %collective-permute-start.17 = (bf16[64,640]{1,0:T(8,128)(2,1)S(1)}, bf16[64,640]{1,0:T(8,128)(2,1)S(1)}, u32[]{:S(2)}, u32[]{:S(2)}) collective-permute-start(bf16[64,640]{1,0:T(8,128)(2,1)S(1)} %get-tuple-element.61), channel_id=1, source_target_pairs={{0,8},{8,0},{16,24},{24,16},{1,9},{9,1},{17,25},{25,17},{2,10},{10... | collective-permute-start | bytes 245768 | tf_op jit(solution)/shard_map/ppermute | solution.py:192
  41.6 1.5 %collective-permute-start.18 = (bf16[64,640]{1,0:T(8,128)(2,1)S(1)}, bf16[64,640]{1,0:T(8,128)(2,1)S(1)}, u32[]{:S(2)}, u32[]{:S(2)}) collective-permute-start(bf16[64,640]{1,0:T(8,128)(2,1)S(1)} %get-tuple-element.62), channel_id=1, source_target_pairs={{0,16},{8,24},{16,0},{24,8},{1,17},{9,25},{17,1},{25,9},{2,18},{10... | collective-permute-start | bytes 245768 | tf_op jit(solution)/shard_map/ppermute | solution.py:192
  43.6 1.6 %collective-permute-done.17.refs_2_ = bf16[64,640]{1,0:T(8,128)(2,1)S(1)} collective-permute-done((bf16[64,640]{1,0:T(8,128)(2,1)S(1)}, bf16[64,640]{1,0:T(8,128)(2,1)S(1)}, u32[]{:S(2)}, u32[]{:S(2)}) %collective-permute-start.17) | collective-permute-done | bytes 81952 | tf_op jit(solution)/shard_map/ppermute | solution.py:192
  46.7 1.7 %collective-permute-done.19.refs_4_ = bf16[64,640]{1,0:T(8,128)(2,1)S(1)} collective-permute-done((bf16[64,640]{1,0:T(8,128)(2,1)S(1)}, bf16[64,640]{1,0:T(8,128)(2,1)S(1)}, u32[]{:S(2)}, u32[]{:S(2)}) %collective-permute-start.19) | collective-permute-done | bytes 81952 | tf_op jit(solution)/shard_map/ppermute | solution.py:192
  49.9 1.5 %collective-permute-done.20.refs_1_ = bf16[4,144,640]{2,1,0:T(8,128)(2,1)S(1)} collective-permute-done((bf16[4,144,640]{2,1,0:T(8,128)(2,1)S(1)}, bf16[4,144,640]{2,1,0:T(8,128)(2,1)S(1)}, u32[]{:S(2)}, u32[]{:S(2)}) %collective-permute-start.20) | collective-permute-done | bytes 737312 | tf_op jit(solution)/shard_map/ppermute | solution.py:192
  51.6 2.5 %collective-permute-start.21 = (bf16[144,384]{1,0:T(8,128)(2,1)S(1)}, bf16[144,384]{1,0:T(8,128)(2,1)S(1)}, u32[]{:S(2)}, u32[]{:S(2)}) collective-permute-start(bf16[144,384]{1,0:T(8,128)(2,1)S(1)} %get-tuple-element.65), channel_id=1, source_target_pairs={{0,6},{2,4},{4,2},{6,0},{1,7},{3,5},{5,3},{7,1},{8,14},{10,12},{12... | collective-permute-start | bytes 331784 | tf_op jit(solution)/shard_map/ppermute | solution.py:192
  54.1 2.0 %collective-permute-start.22 = (bf16[144,384]{1,0:T(8,128)(2,1)S(1)}, bf16[144,384]{1,0:T(8,128)(2,1)S(1)}, u32[]{:S(2)}, u32[]{:S(2)}) collective-permute-start(bf16[144,384]{1,0:T(8,128)(2,1)S(1)} %get-tuple-element.69), channel_id=1, source_target_pairs={{0,4},{2,6},{4,0},{6,2},{1,5},{3,7},{5,1},{7,3},{8,12},{10,14},{12... | collective-permute-start | bytes 331784 | tf_op jit(solution)/shard_map/ppermute | solution.py:192
  56.2 2.4 %collective-permute-start.27 = (bf16[144,256]{1,0:T(8,128)(2,1)S(1)}, bf16[144,256]{1,0:T(8,128)(2,1)S(1)}, u32[]{:S(2)}, u32[]{:S(2)}) collective-permute-start(bf16[144,256]{1,0:T(8,128)(2,1)S(1)} %get-tuple-element.73), channel_id=1, source_target_pairs={{0,6},{2,4},{4,2},{6,0},{1,7},{3,5},{5,3},{7,1},{8,14},{10,12},{12... | collective-permute-start | bytes 221192 | tf_op jit(solution)/shard_map/ppermute | solution.py:192
  59.6 5.1 %collective-permute-start.29 = (bf16[144,256]{1,0:T(8,128)(2,1)S(1)}, bf16[144,256]{1,0:T(8,128)(2,1)S(1)}, u32[]{:S(2)}, u32[]{:S(2)}) collective-permute-start(bf16[144,256]{1,0:T(8,128)(2,1)S(1)} %get-tuple-element.75), channel_id=1, source_target_pairs={{0,2},{2,0},{4,6},{6,4},{1,3},{3,1},{5,7},{7,5},{8,10},{10,8},{12,... | collective-permute-start | bytes 221192 | tf_op jit(solution)/shard_map/ppermute | solution.py:192
  64.7 2.4 %shard_map.86 = (bf16[64,1152]{1,0:T(8,128)(2,1)}, bf16[64,1152]{1,0:T(8,128)(2,1)}, f32[8,128]{1,0:T(8,128)S(1)}) custom-call(bf16[64,1152]{1,0:T(8,128)(2,1)S(1)} %get-tuple-element.57.refs_0_, bf16[1152,1152]{1,0:T(8,128)(2,1)S(1)} %copy-done.1, bf16[64,1152]{1,0:T(8,128)(2,1)S(1)} %get-tuple-element.58.refs_2_, bf16[1152,1152]{1,0:T(8,128)(2,1)S(1)} %copy-done, ...), custom_call_target="tpu_custom_call" | custom-call | flops 1000000000 | bytes 1000000000 | tf_op jit(solution)/shard_map/pallas_call | solution.py:43
  67.1 1.8 %collective-permute-done.22.refs_2_ = bf16[144,384]{1,0:T(8,128)(2,1)S(1)} collective-permute-done((bf16[144,384]{1,0:T(8,128)(2,1)S(1)}, bf16[144,384]{1,0:T(8,128)(2,1)S(1)}, u32[]{:S(2)}, u32[]{:S(2)}) %collective-permute-start.22) | collective-permute-done | bytes 110624 | tf_op jit(solution)/shard_map/ppermute | solution.py:192
  70.1 1.9 %collective-permute-done.28.refs_2_ = bf16[144,256]{1,0:T(8,128)(2,1)S(1)} collective-permute-done((bf16[144,256]{1,0:T(8,128)(2,1)S(1)}, bf16[144,256]{1,0:T(8,128)(2,1)S(1)}, u32[]{:S(2)}, u32[]{:S(2)}) %collective-permute-start.28) | collective-permute-done | bytes 73760 | tf_op jit(solution)/shard_map/ppermute | solution.py:192
  73.2 2.4 %collective-permute-start.26 = (bf16[144,384]{1,0:T(8,128)(2,1)S(1)}, bf16[144,384]{1,0:T(8,128)(2,1)S(1)}, u32[]{:S(2)}, u32[]{:S(2)}) collective-permute-start(bf16[144,384]{1,0:T(8,128)(2,1)S(1)} %shard_map.87.refs_0_), channel_id=1, source_target_pairs={{0,24},{8,16},{16,8},{24,0},{1,25},{9,17},{17,9},{25,1},{2,26},{10... | collective-permute-start | bytes 331784 | tf_op jit(solution)/shard_map/ppermute | solution.py:192
  76.9 3.2 %collective-permute-done.31.refs_6_ = bf16[144,256]{1,0:T(8,128)(2,1)S(1)} collective-permute-done((bf16[144,256]{1,0:T(8,128)(2,1)S(1)}, bf16[144,256]{1,0:T(8,128)(2,1)S(1)}, u32[]{:S(2)}, u32[]{:S(2)}) %collective-permute-start.31) | collective-permute-done | bytes 73760 | tf_op jit(solution)/shard_map/ppermute | solution.py:192
  (64 shorter events, 26.1 us)
Async XLA Ops:
  0.6 11.0 %collective-permute-start = (bf16[64,1152]{1,0:T(8,128)(2,1)}, bf16[64,1152]{1,0:T(8,128)(2,1)S(1)}, u32[]{:S(2)}, u32[]{:S(2)}) collective-permute-start(bf16[64,1152]{1,0:T(8,128)(2,1)} %refs_1_.3), channel_id=1, source_target_pairs={{0,8},{8,0},{16,24},{24,16},{1,9},{9,1},{17,25},{25,17},{2,10},{10... | collective-permute-start | bytes 442376 | tf_op jit(solution)/shard_map/ppermute | solution.py:192
  3.6 8.7 %collective-permute-start.1 = (bf16[64,1152]{1,0:T(8,128)(2,1)}, bf16[64,1152]{1,0:T(8,128)(2,1)S(1)}, u32[]{:S(2)}, u32[]{:S(2)}) collective-permute-start(bf16[64,1152]{1,0:T(8,128)(2,1)} %refs_1_.3), channel_id=1, source_target_pairs={{0,16},{8,24},{16,0},{24,8},{1,17},{9,25},{17,1},{25,9},{2,18},{10... | collective-permute-start | bytes 442376 | tf_op jit(solution)/shard_map/ppermute | solution.py:192
  5.2 7.2 %collective-permute-start.2 = (bf16[64,1152]{1,0:T(8,128)(2,1)}, bf16[64,1152]{1,0:T(8,128)(2,1)S(1)}, u32[]{:S(2)}, u32[]{:S(2)}) collective-permute-start(bf16[64,1152]{1,0:T(8,128)(2,1)} %refs_1_.3), channel_id=1, source_target_pairs={{0,24},{8,16},{16,8},{24,0},{1,25},{9,17},{17,9},{25,1},{2,26},{10... | collective-permute-start | bytes 442376 | tf_op jit(solution)/shard_map/ppermute | solution.py:192
  5.2 11.7 %collective-permute-start.3 = (bf16[64,1152]{1,0:T(8,128)(2,1)}, bf16[64,1152]{1,0:T(8,128)(2,1)S(1)}, u32[]{:S(2)}, u32[]{:S(2)}) collective-permute-start(bf16[64,1152]{1,0:T(8,128)(2,1)} %refs_0_.2), channel_id=1, source_target_pairs={{0,2},{2,0},{4,6},{6,4},{1,3},{3,1},{5,7},{7,5},{8,10},{10,8},{12,... | collective-permute-start | bytes 442376 | tf_op jit(solution)/shard_map/ppermute | solution.py:192
  7.2 13.1 %collective-permute-start.4 = (bf16[64,1152]{1,0:T(8,128)(2,1)}, bf16[64,1152]{1,0:T(8,128)(2,1)S(1)}, u32[]{:S(2)}, u32[]{:S(2)}) collective-permute-start(bf16[64,1152]{1,0:T(8,128)(2,1)} %refs_0_.2), channel_id=1, source_target_pairs={{0,4},{2,6},{4,0},{6,2},{1,5},{3,7},{5,1},{7,3},{8,12},{10,14},{12... | collective-permute-start | bytes 442376 | tf_op jit(solution)/shard_map/ppermute | solution.py:192
  11.7 8.7 %collective-permute-start.5 = (bf16[64,1152]{1,0:T(8,128)(2,1)}, bf16[64,1152]{1,0:T(8,128)(2,1)S(1)}, u32[]{:S(2)}, u32[]{:S(2)}) collective-permute-start(bf16[64,1152]{1,0:T(8,128)(2,1)} %refs_0_.2), channel_id=1, source_target_pairs={{0,6},{2,4},{4,2},{6,0},{1,7},{3,5},{5,3},{7,1},{8,14},{10,12},{12... | collective-permute-start | bytes 442376 | tf_op jit(solution)/shard_map/ppermute | solution.py:192
  13.5 10.5 %collective-permute-start.7 = (bf16[64,1152]{1,0:T(8,128)(2,1)S(1)}, bf16[64,1152]{1,0:T(8,128)(2,1)S(1)}, u32[]{:S(2)}, u32[]{:S(2)}) collective-permute-start(bf16[64,1152]{1,0:T(8,128)(2,1)S(1)} %get-tuple-element.43.refs_0_.refs_2_), channel_id=1, source_target_pairs={{0,8},{8,0},{16,24},{24,16},{1,9},{9,1},{17,25},{25,17},{2,10},{10... | collective-permute-start | bytes 442376 | tf_op jit(solution)/shard_map/ppermute | solution.py:192
  15.4 8.5 %collective-permute-start.8 = (bf16[64,1152]{1,0:T(8,128)(2,1)S(1)}, bf16[64,1152]{1,0:T(8,128)(2,1)S(1)}, u32[]{:S(2)}, u32[]{:S(2)}) collective-permute-start(bf16[64,1152]{1,0:T(8,128)(2,1)S(1)} %get-tuple-element.43.refs_0_.refs_2_), channel_id=1, source_target_pairs={{0,16},{8,24},{16,0},{24,8},{1,17},{9,25},{17,1},{25,9},{2,18},{10... | collective-permute-start | bytes 442376 | tf_op jit(solution)/shard_map/ppermute | solution.py:192
  16.9 7.0 %collective-permute-start.9 = (bf16[64,1152]{1,0:T(8,128)(2,1)S(1)}, bf16[64,1152]{1,0:T(8,128)(2,1)S(1)}, u32[]{:S(2)}, u32[]{:S(2)}) collective-permute-start(bf16[64,1152]{1,0:T(8,128)(2,1)S(1)} %get-tuple-element.43.refs_0_.refs_2_), channel_id=1, source_target_pairs={{0,24},{8,16},{16,8},{24,0},{1,25},{9,17},{17,9},{25,1},{2,26},{10... | collective-permute-start | bytes 442376 | tf_op jit(solution)/shard_map/ppermute | solution.py:192
  24.0 8.9 %collective-permute-start.11 = (bf16[64,1152]{1,0:T(8,128)(2,1)S(1)}, bf16[64,1152]{1,0:T(8,128)(2,1)S(1)}, u32[]{:S(2)}, u32[]{:S(2)}) collective-permute-start(bf16[64,1152]{1,0:T(8,128)(2,1)S(1)} %shard_map.81), channel_id=1, source_target_pairs={{0,2},{2,0},{4,6},{6,4},{1,3},{3,1},{5,7},{7,5},{8,10},{10,8},{12,... | collective-permute-start | bytes 442376 | tf_op jit(solution)/shard_map/ppermute | solution.py:192
  25.6 13.9 %collective-permute-start.12 = (bf16[64,1152]{1,0:T(8,128)(2,1)S(1)}, bf16[64,1152]{1,0:T(8,128)(2,1)S(1)}, u32[]{:S(2)}, u32[]{:S(2)}) collective-permute-start(bf16[64,1152]{1,0:T(8,128)(2,1)S(1)} %get-tuple-element.51), channel_id=1, source_target_pairs={{0,4},{2,6},{4,0},{6,2},{1,5},{3,7},{5,1},{7,3},{8,12},{10,14},{12... | collective-permute-start | bytes 442376 | tf_op jit(solution)/shard_map/ppermute | solution.py:192
  27.5 12.1 %collective-permute-start.13 = (bf16[64,1152]{1,0:T(8,128)(2,1)S(1)}, bf16[64,1152]{1,0:T(8,128)(2,1)S(1)}, u32[]{:S(2)}, u32[]{:S(2)}) collective-permute-start(bf16[64,1152]{1,0:T(8,128)(2,1)S(1)} %get-tuple-element.52), channel_id=1, source_target_pairs={{0,6},{2,4},{4,2},{6,0},{1,7},{3,5},{5,3},{7,1},{8,14},{10,12},{12... | collective-permute-start | bytes 442376 | tf_op jit(solution)/shard_map/ppermute | solution.py:192
  28.5 11.0 %collective-permute-start.14 = (bf16[64,1152]{1,0:T(8,128)(2,1)S(1)}, bf16[64,1152]{1,0:T(8,128)(2,1)S(1)}, u32[]{:S(2)}, u32[]{:S(2)}) collective-permute-start(bf16[64,1152]{1,0:T(8,128)(2,1)S(1)} %get-tuple-element.48.refs_10_), channel_id=1, source_target_pairs={{0,8},{8,0},{16,24},{24,16},{1,9},{9,1},{17,25},{25,17},{2,10},{10... | collective-permute-start | bytes 442376 | tf_op jit(solution)/shard_map/ppermute | solution.py:192
  30.1 9.5 %collective-permute-start.15 = (bf16[64,1152]{1,0:T(8,128)(2,1)S(1)}, bf16[64,1152]{1,0:T(8,128)(2,1)S(1)}, u32[]{:S(2)}, u32[]{:S(2)}) collective-permute-start(bf16[64,1152]{1,0:T(8,128)(2,1)S(1)} %get-tuple-element.55), channel_id=1, source_target_pairs={{0,16},{8,24},{16,0},{24,8},{1,17},{9,25},{17,1},{25,9},{2,18},{10... | collective-permute-start | bytes 442376 | tf_op jit(solution)/shard_map/ppermute | solution.py:192
  32.9 6.7 %collective-permute-start.16 = (bf16[64,1152]{1,0:T(8,128)(2,1)S(1)}, bf16[64,1152]{1,0:T(8,128)(2,1)S(1)}, u32[]{:S(2)}, u32[]{:S(2)}) collective-permute-start(bf16[64,1152]{1,0:T(8,128)(2,1)S(1)} %get-tuple-element.56), channel_id=1, source_target_pairs={{0,24},{8,16},{16,8},{24,0},{1,25},{9,17},{17,9},{25,1},{2,26},{10... | collective-permute-start | bytes 442376 | tf_op jit(solution)/shard_map/ppermute | solution.py:192
  51.6 8.0 %collective-permute-start.21 = (bf16[144,384]{1,0:T(8,128)(2,1)S(1)}, bf16[144,384]{1,0:T(8,128)(2,1)S(1)}, u32[]{:S(2)}, u32[]{:S(2)}) collective-permute-start(bf16[144,384]{1,0:T(8,128)(2,1)S(1)} %get-tuple-element.65), channel_id=1, source_target_pairs={{0,6},{2,4},{4,2},{6,0},{1,7},{3,5},{5,3},{7,1},{8,14},{10,12},{12... | collective-permute-start | bytes 331784 | tf_op jit(solution)/shard_map/ppermute | solution.py:192
  54.1 14.8 %collective-permute-start.22 = (bf16[144,384]{1,0:T(8,128)(2,1)S(1)}, bf16[144,384]{1,0:T(8,128)(2,1)S(1)}, u32[]{:S(2)}, u32[]{:S(2)}) collective-permute-start(bf16[144,384]{1,0:T(8,128)(2,1)S(1)} %get-tuple-element.69), channel_id=1, source_target_pairs={{0,4},{2,6},{4,0},{6,2},{1,5},{3,7},{5,1},{7,3},{8,12},{10,14},{12... | collective-permute-start | bytes 331784 | tf_op jit(solution)/shard_map/ppermute | solution.py:192
  56.1 12.9 %collective-permute-start.23 = (bf16[144,384]{1,0:T(8,128)(2,1)S(1)}, bf16[144,384]{1,0:T(8,128)(2,1)S(1)}, u32[]{:S(2)}, u32[]{:S(2)}) collective-permute-start(bf16[144,384]{1,0:T(8,128)(2,1)S(1)} %get-tuple-element.70), channel_id=1, source_target_pairs={{0,2},{2,0},{4,6},{6,4},{1,3},{3,1},{5,7},{7,5},{8,10},{10,8},{12,... | collective-permute-start | bytes 331784 | tf_op jit(solution)/shard_map/ppermute | solution.py:192
  56.2 13.9 %collective-permute-start.27 = (bf16[144,256]{1,0:T(8,128)(2,1)S(1)}, bf16[144,256]{1,0:T(8,128)(2,1)S(1)}, u32[]{:S(2)}, u32[]{:S(2)}) collective-permute-start(bf16[144,256]{1,0:T(8,128)(2,1)S(1)} %get-tuple-element.73), channel_id=1, source_target_pairs={{0,6},{2,4},{4,2},{6,0},{1,7},{3,5},{5,3},{7,1},{8,14},{10,12},{12... | collective-permute-start | bytes 221192 | tf_op jit(solution)/shard_map/ppermute | solution.py:192
  58.5 13.5 %collective-permute-start.28 = (bf16[144,256]{1,0:T(8,128)(2,1)S(1)}, bf16[144,256]{1,0:T(8,128)(2,1)S(1)}, u32[]{:S(2)}, u32[]{:S(2)}) collective-permute-start(bf16[144,256]{1,0:T(8,128)(2,1)S(1)} %get-tuple-element.74), channel_id=1, source_target_pairs={{0,4},{2,6},{4,0},{6,2},{1,5},{3,7},{5,1},{7,3},{8,12},{10,14},{12... | collective-permute-start | bytes 221192 | tf_op jit(solution)/shard_map/ppermute | solution.py:192
  59.6 12.4 %collective-permute-start.29 = (bf16[144,256]{1,0:T(8,128)(2,1)S(1)}, bf16[144,256]{1,0:T(8,128)(2,1)S(1)}, u32[]{:S(2)}, u32[]{:S(2)}) collective-permute-start(bf16[144,256]{1,0:T(8,128)(2,1)S(1)} %get-tuple-element.75), channel_id=1, source_target_pairs={{0,2},{2,0},{4,6},{6,4},{1,3},{3,1},{5,7},{7,5},{8,10},{10,8},{12,... | collective-permute-start | bytes 221192 | tf_op jit(solution)/shard_map/ppermute | solution.py:192
  69.0 6.6 %collective-permute-start.24 = (bf16[144,384]{1,0:T(8,128)(2,1)S(1)}, bf16[144,384]{1,0:T(8,128)(2,1)S(1)}, u32[]{:S(2)}, u32[]{:S(2)}) collective-permute-start(bf16[144,384]{1,0:T(8,128)(2,1)S(1)} %shard_map.87.refs_0_), channel_id=1, source_target_pairs={{0,8},{8,0},{16,24},{24,16},{1,9},{9,1},{17,25},{25,17},{2,10},{10... | collective-permute-start | bytes 331784 | tf_op jit(solution)/shard_map/ppermute | solution.py:192
  72.6 7.4 %collective-permute-start.31 = (bf16[144,256]{1,0:T(8,128)(2,1)S(1)}, bf16[144,256]{1,0:T(8,128)(2,1)S(1)}, u32[]{:S(2)}, u32[]{:S(2)}) collective-permute-start(bf16[144,256]{1,0:T(8,128)(2,1)S(1)} %shard_map.88.refs_0_.refs_4_), channel_id=1, source_target_pairs={{0,16},{8,24},{16,0},{24,8},{1,17},{9,25},{17,1},{25,9},{2,18},{10... | collective-permute-start | bytes 221192 | tf_op jit(solution)/shard_map/ppermute | solution.py:192
  73.2 6.8 %collective-permute-start.26 = (bf16[144,384]{1,0:T(8,128)(2,1)S(1)}, bf16[144,384]{1,0:T(8,128)(2,1)S(1)}, u32[]{:S(2)}, u32[]{:S(2)}) collective-permute-start(bf16[144,384]{1,0:T(8,128)(2,1)S(1)} %shard_map.87.refs_0_), channel_id=1, source_target_pairs={{0,24},{8,16},{16,8},{24,0},{1,25},{9,17},{17,9},{25,1},{2,26},{10... | collective-permute-start | bytes 331784 | tf_op jit(solution)/shard_map/ppermute | solution.py:192
  (12 other events, 61.4 us)

commit v5 on v4

--- a/solution.py
+++ b/solution.py
@@ -104,19 +104,37 @@
     return (inverse * (grad_unit - unit * inner_sum)).astype(low)
 
 
-def backs_kernel(layers, groups, *refs):
+def cuts(chunks, groups, share):
+    full, rest = divmod(chunks, groups)
+    parts = groups // rest if rest and groups % rest == 0 else 0
+    if parts and share % (8 * parts) == 0:
+        return full, parts
+    return full + (rest > 0), 0
+
+
+def extra_chunk(cut, groups, blk):
+    full, parts = cut
+    return groups * full + blk // parts
+
+
+def backs_kernel(layers, groups, cut, *refs):
     image_refs, refs = refs[: layers + 1], refs[layers + 1 :]
     text_refs, refs = refs[: groups + 1], refs[groups + 1 :]
     image_ref, text_ref, *out_refs, all_ref = refs
-    width, lanes = image_ref.shape[1], out_refs[0].shape[1]
+    width = image_ref.shape[1]
     image_ref[...] = back_of(*image_refs[:2], image_refs[2:])
     text_ref[...] = back_of(*text_refs[:2], text_refs[2:])
     all_ref[:, :width] = image_ref[...]
     all_ref[:, width : 2 * width] = text_ref[...]
     if all_ref.shape[1] > 2 * width:
         all_ref[:, 2 * width :] = jnp.zeros((all_ref.shape[0], all_ref.shape[1] - 2 * width), low)
+    own = cut[0] * 128
     for k, ref in enumerate(out_refs):
-        ref[...] = all_ref[:, pl.ds(pl.multiple_of((k ^ lax.axis_index("blk")) * lanes, 128), lanes)]
+        blk = k ^ lax.axis_index("blk")
+        ref[:, :own] = all_ref[:, pl.ds(pl.multiple_of(blk * own, 128), own)]
+        if cut[1]:
+            first = pl.multiple_of(extra_chunk(cut, groups, blk) * 128, 128)
+            ref[:, own:] = all_ref[:, pl.ds(first, 128)]
 
 
 def grads_kernel(image_ref, image_head_ref, text_ref, text_head_ref, image_out_ref, text_out_ref, token_ref):
@@ -152,11 +170,15 @@
         ref[...] = parts[(k + 1) * rows : (k + 2) * rows].astype(low)
 
 
-def terms_kernel(width, turned_ref, *refs):
+def terms_kernel(width, groups, cut, turned_ref, *refs):
     *back_refs, out_ref = refs
     backs = jnp.concatenate([ref[...] for ref in back_refs])
-    lanes = backs.shape[1]
-    of_image = lax.broadcasted_iota(jnp.int32, backs.shape, 1) + lax.axis_index("blk") * lanes < width
+    blk, own = lax.axis_index("blk"), cut[0] * 128
+    lane = lax.broadcasted_iota(jnp.int32, backs.shape, 1)
+    column = lane + blk * own
+    if cut[1]:
+        column = jnp.where(lane < own, column, lane - own + extra_chunk(cut, groups, blk) * 128)
+    of_image = column < width
     zero = jnp.zeros_like(backs)
     backs = jnp.concatenate([jnp.where(of_image, backs, zero), jnp.where(of_image, zero, backs)])
     for k in range(out_ref.shape[0]):
@@ -164,19 +186,36 @@
 
 
 def layers_kernel(cut, mine_ref, theirs_ref, *refs):
+    own, parts = cut[0] * 128, cut[1]
+    lanes = refs[0].shape[1]
     for k in range(mine_ref.shape[0]):
         total = mine_ref[k] + theirs_ref[k].astype(wide)
-        refs[2 * k][...] = total[:, :cut].astype(refs[2 * k].dtype)
-        refs[2 * k + 1][...] = total[:, cut:].astype(refs[2 * k].dtype)
+        second = total[:, lanes:own]
+        if parts:
+            part = total.shape[0] // parts
+            extra = total[:part, own:]
+            for i in range(1, parts):
+                mine = lax.axis_index("blk") % parts == i
+                extra = jnp.where(mine, total[i * part : (i + 1) * part, own:], extra)
+            second = jnp.concatenate([second, extra])
+        refs[2 * k][...] = total[:, :lanes].astype(refs[2 * k].dtype)
+        refs[2 * k + 1][...] = second.astype(refs[2 * k].dtype)
 
 
 def heads_kernel(groups, cut, *refs):
     *block_refs, image_ref, text_ref, all_ref = refs
-    width, lanes = image_ref.shape[1], all_ref.shape[1] // groups
+    (share, width), (_, lanes), (own, parts) = image_ref.shape, block_refs[0].shape, (cut[0] * 128, cut[1])
     for k in range(groups):
-        first = pl.multiple_of((k ^ lax.axis_index("blk")) * lanes, 128)
-        all_ref[:, pl.ds(first, cut)] = block_refs[k][...].astype(wide)
-        all_ref[:, pl.ds(first + cut, lanes - cut)] = block_refs[groups + k][...].astype(wide)
+        blk = k ^ lax.axis_index("blk")
+        first = pl.multiple_of(blk * own, 128)
+        second = block_refs[groups + k][...].astype(wide)
+        all_ref[:, pl.ds(first, lanes)] = block_refs[k][...].astype(wide)
+        all_ref[:, pl.ds(first + lanes, own - lanes)] = second[:share]
+        if parts:
+            part = share // parts
+            row = pl.multiple_of(blk % parts * part, 8)
+            column = pl.multiple_of(extra_chunk(cut, groups, blk) * 128, 128)
+            all_ref[pl.ds(row, part), pl.ds(column, 128)] = second[share:]
     image_ref[...] = all_ref[:, :width]
     text_ref[...] = all_ref[:, width : 2 * width]
 
@@ -202,8 +241,12 @@
         return over(array, "core", 1)
 
     share = width // (layers * cores)
-    lanes = -(-2 * width // (128 * groups)) * 128
-    cut = -(-lanes // 256) * 128
+    cut = cuts(2 * width // 128, groups, share)
+    own, parts = cut[0] * 128, cut[1]
+    lanes = own + 128 * (parts > 0)
+    columns = max(groups * own, 2 * width)
+    first = (share, own - 128 if parts else -(-own // 256) * 128)
+    second = (share + share // parts, 128) if parts else (share, own - first[1])
     assert width % 128 == 0 and cores == 2
 
     block = (rows, width)
@@ -241,18 +284,17 @@
         cost=1,
     )
     image_back, text_back, *sends = call(
-        functools.partial(backs_kernel, layers, groups),
+        functools.partial(backs_kernel, layers, groups, cut),
         [(block, low)] * 2 + [((rows, lanes), low)] * groups,
         *(image_total, image_before, *image_parts, text_total, text_before, *text_parts),
         cost=80,
-        scratch=[((rows, groups * lanes), low)],
+        scratch=[((rows, columns), low)],
     )
     backs = [sends[0]] + [over(block, "blk", k + 1) for k, block in enumerate(sends[1:])]
     shape = (layers, share, lanes)
-    kernel = functools.partial(terms_kernel, width)
+    kernel = functools.partial(terms_kernel, width, groups, cut)
     theirs = call(kernel, [(shape, low)], turned_theirs, *backs)[0]
     mine = call(kernel, [(shape, wide)], turned_mine, *backs, behind=[theirs])[0]
-    first, second = (share, cut), (share, lanes - cut)
     outs = [(first, wide), (second, wide)] + [(first, low), (second, low)] * (layers - 1)
     terms = call(functools.partial(layers_kernel, cut), outs, mine, over_core(theirs))
     first_parts, second_parts = (
@@ -274,7 +316,7 @@
         functools.partial(heads_kernel, groups, cut),
         [((share, width), wide)] * 2,
         *blocks,
-        scratch=[((share, groups * lanes), wide)],
+        scratch=[((share, columns), wide)],
     )
     return (grad_images, grad_captions, grad_image_head, grad_text_head)
 

time: 82.3 us -> 80.5 us (0.978)
  waiting for transfers between devices: 23.6 us -> 20.9 us
    ppermute x33, waiting for transfers between devices: 23.6 us -> 20.9 us  [over(): lax.ppermute(array, axis, [(i, i ^ by) for i in range(lax.axis_size(axis))])]
where the time goes in v5:
time: 80.5 us; the launch traced here: 80.3 us
  starting transfers between devices  46.4 us (58%)
  waiting for transfers between devices  20.9 us (26%)
  Pallas kernels  11.3 us (14%)
  local copies, waits for them, and re-layouts  0.92 us (1%)
    ppermute x33, starting transfers between devices, over(): lax.ppermute(array, axis, [(i, i ^ by) for i in range(lax.axis_size(axis))])  46.4 us
    ppermute x33, waiting for transfers between devices, over(): lax.ppermute(array, axis, [(i, i ^ by) for i in range(lax.axis_size(axis))])  20.9 us
    pallas_call x16, Pallas kernels, call(): pl.pallas_call(body, out_shape=tuple((jax.ShapeDtypeStruct(shape, kind) f...  11.3 us
  transfers between devices with their start and end apart: 33, of which 13 were waited for; matrix products, arithmetic and copies ran while one was open for 0% of the time, Pallas kernels for 11%

profile of v5, /device:TPU:0, one launch (start us, length us, event | category | flops | bytes accessed | tf_op | source)
XLA Modules:
  0.0 80.3 jit_solution(6274418343590957048)
XLA Ops:
  0.6 3.0 %collective-permute-start = (bf16[64,1152]{1,0:T(8,128)(2,1)}, bf16[64,1152]{1,0:T(8,128)(2,1)S(1)}, u32[]{:S(2)}, u32[]{:S(2)}) collective-permute-start(bf16[64,1152]{1,0:T(8,128)(2,1)} %refs_1_.3), channel_id=1, source_target_pairs={{0,8},{8,0},{16,24},{24,16},{1,9},{9,1},{17,25},{25,17},{2,10},{10... | collective-permute-start | bytes 442376 | tf_op jit(solution)/shard_map/ppermute | solution.py:231
  3.6 1.5 %collective-permute-start.1 = (bf16[64,1152]{1,0:T(8,128)(2,1)}, bf16[64,1152]{1,0:T(8,128)(2,1)S(1)}, u32[]{:S(2)}, u32[]{:S(2)}) collective-permute-start(bf16[64,1152]{1,0:T(8,128)(2,1)} %refs_1_.3), channel_id=1, source_target_pairs={{0,16},{8,24},{16,0},{24,8},{1,17},{9,25},{17,1},{25,9},{2,18},{10... | collective-permute-start | bytes 442376 | tf_op jit(solution)/shard_map/ppermute | solution.py:231
  5.2 2.0 %collective-permute-start.3 = (bf16[64,1152]{1,0:T(8,128)(2,1)}, bf16[64,1152]{1,0:T(8,128)(2,1)S(1)}, u32[]{:S(2)}, u32[]{:S(2)}) collective-permute-start(bf16[64,1152]{1,0:T(8,128)(2,1)} %refs_0_.2), channel_id=1, source_target_pairs={{0,2},{2,0},{4,6},{6,4},{1,3},{3,1},{5,7},{7,5},{8,10},{10,8},{12,... | collective-permute-start | bytes 442376 | tf_op jit(solution)/shard_map/ppermute | solution.py:231
  7.2 2.6 %collective-permute-start.4 = (bf16[64,1152]{1,0:T(8,128)(2,1)}, bf16[64,1152]{1,0:T(8,128)(2,1)S(1)}, u32[]{:S(2)}, u32[]{:S(2)}) collective-permute-start(bf16[64,1152]{1,0:T(8,128)(2,1)} %refs_0_.2), channel_id=1, source_target_pairs={{0,4},{2,6},{4,0},{6,2},{1,5},{3,7},{5,1},{7,3},{8,12},{10,14},{12... | collective-permute-start | bytes 442376 | tf_op jit(solution)/shard_map/ppermute | solution.py:231
  13.5 1.9 %collective-permute-start.7 = (bf16[64,1152]{1,0:T(8,128)(2,1)S(1)}, bf16[64,1152]{1,0:T(8,128)(2,1)S(1)}, u32[]{:S(2)}, u32[]{:S(2)}) collective-permute-start(bf16[64,1152]{1,0:T(8,128)(2,1)S(1)} %get-tuple-element.43.refs_0_.refs_2_), channel_id=1, source_target_pairs={{0,8},{8,0},{16,24},{24,16},{1,9},{9,1},{17,25},{25,17},{2,10},{10... | collective-permute-start | bytes 442376 | tf_op jit(solution)/shard_map/ppermute | solution.py:231
  15.4 1.5 %collective-permute-start.8 = (bf16[64,1152]{1,0:T(8,128)(2,1)S(1)}, bf16[64,1152]{1,0:T(8,128)(2,1)S(1)}, u32[]{:S(2)}, u32[]{:S(2)}) collective-permute-start(bf16[64,1152]{1,0:T(8,128)(2,1)S(1)} %get-tuple-element.43.refs_0_.refs_2_), channel_id=1, source_target_pairs={{0,16},{8,24},{16,0},{24,8},{1,17},{9,25},{17,1},{25,9},{2,18},{10... | collective-permute-start | bytes 442376 | tf_op jit(solution)/shard_map/ppermute | solution.py:231
  17.0 3.3 %collective-permute-done.4.refs_2_ = bf16[64,1152]{1,0:T(8,128)(2,1)S(1)} collective-permute-done((bf16[64,1152]{1,0:T(8,128)(2,1)}, bf16[64,1152]{1,0:T(8,128)(2,1)S(1)}, u32[]{:S(2)}, u32[]{:S(2)}) %collective-permute-start.4) | collective-permute-done | bytes 147488 | tf_op jit(solution)/shard_map/ppermute | solution.py:231
  24.0 1.7 %collective-permute-start.11 = (bf16[64,1152]{1,0:T(8,128)(2,1)S(1)}, bf16[64,1152]{1,0:T(8,128)(2,1)S(1)}, u32[]{:S(2)}, u32[]{:S(2)}) collective-permute-start(bf16[64,1152]{1,0:T(8,128)(2,1)S(1)} %shard_map.81), channel_id=1, source_target_pairs={{0,2},{2,0},{4,6},{6,4},{1,3},{3,1},{5,7},{7,5},{8,10},{10,8},{12,... | collective-permute-start | bytes 442376 | tf_op jit(solution)/shard_map/ppermute | solution.py:231
  25.6 1.9 %collective-permute-start.12 = (bf16[64,1152]{1,0:T(8,128)(2,1)S(1)}, bf16[64,1152]{1,0:T(8,128)(2,1)S(1)}, u32[]{:S(2)}, u32[]{:S(2)}) collective-permute-start(bf16[64,1152]{1,0:T(8,128)(2,1)S(1)} %get-tuple-element.51), channel_id=1, source_target_pairs={{0,4},{2,6},{4,0},{6,2},{1,5},{3,7},{5,1},{7,3},{8,12},{10,14},{12... | collective-permute-start | bytes 442376 | tf_op jit(solution)/shard_map/ppermute | solution.py:231
  28.5 1.6 %collective-permute-start.14 = (bf16[64,1152]{1,0:T(8,128)(2,1)S(1)}, bf16[64,1152]{1,0:T(8,128)(2,1)S(1)}, u32[]{:S(2)}, u32[]{:S(2)}) collective-permute-start(bf16[64,1152]{1,0:T(8,128)(2,1)S(1)} %get-tuple-element.48.refs_10_), channel_id=1, source_target_pairs={{0,8},{8,0},{16,24},{24,16},{1,9},{9,1},{17,25},{25,17},{2,10},{10... | collective-permute-start | bytes 442376 | tf_op jit(solution)/shard_map/ppermute | solution.py:231
  32.9 2.5 %collective-permute-start.16 = (bf16[64,1152]{1,0:T(8,128)(2,1)S(1)}, bf16[64,1152]{1,0:T(8,128)(2,1)S(1)}, u32[]{:S(2)}, u32[]{:S(2)}) collective-permute-start(bf16[64,1152]{1,0:T(8,128)(2,1)S(1)} %get-tuple-element.56), channel_id=1, source_target_pairs={{0,24},{8,16},{16,8},{24,0},{1,25},{9,17},{17,9},{25,1},{2,26},{10... | collective-permute-start | bytes 442376 | tf_op jit(solution)/shard_map/ppermute | solution.py:231
  36.5 3.1 %collective-permute-done.12.refs_3_ = bf16[64,1152]{1,0:T(8,128)(2,1)S(1)} collective-permute-done((bf16[64,1152]{1,0:T(8,128)(2,1)S(1)}, bf16[64,1152]{1,0:T(8,128)(2,1)S(1)}, u32[]{:S(2)}, u32[]{:S(2)}) %collective-permute-start.12) | collective-permute-done | bytes 147488 | tf_op jit(solution)/shard_map/ppermute | solution.py:231
  40.0 1.6 %collective-permute-start.17 = (bf16[64,640]{1,0:T(8,128)(2,1)S(1)}, bf16[64,640]{1,0:T(8,128)(2,1)S(1)}, u32[]{:S(2)}, u32[]{:S(2)}) collective-permute-start(bf16[64,640]{1,0:T(8,128)(2,1)S(1)} %get-tuple-element.61), channel_id=1, source_target_pairs={{0,8},{8,0},{16,24},{24,16},{1,9},{9,1},{17,25},{25,17},{2,10},{10... | collective-permute-start | bytes 245768 | tf_op jit(solution)/shard_map/ppermute | solution.py:231
  41.6 1.5 %collective-permute-start.18 = (bf16[64,640]{1,0:T(8,128)(2,1)S(1)}, bf16[64,640]{1,0:T(8,128)(2,1)S(1)}, u32[]{:S(2)}, u32[]{:S(2)}) collective-permute-start(bf16[64,640]{1,0:T(8,128)(2,1)S(1)} %get-tuple-element.62), channel_id=1, source_target_pairs={{0,16},{8,24},{16,0},{24,8},{1,17},{9,25},{17,1},{25,9},{2,18},{10... | collective-permute-start | bytes 245768 | tf_op jit(solution)/shard_map/ppermute | solution.py:231
  43.6 1.6 %collective-permute-done.17.refs_2_ = bf16[64,640]{1,0:T(8,128)(2,1)S(1)} collective-permute-done((bf16[64,640]{1,0:T(8,128)(2,1)S(1)}, bf16[64,640]{1,0:T(8,128)(2,1)S(1)}, u32[]{:S(2)}, u32[]{:S(2)}) %collective-permute-start.17) | collective-permute-done | bytes 81952 | tf_op jit(solution)/shard_map/ppermute | solution.py:231
  46.7 1.7 %collective-permute-done.19.refs_4_ = bf16[64,640]{1,0:T(8,128)(2,1)S(1)} collective-permute-done((bf16[64,640]{1,0:T(8,128)(2,1)S(1)}, bf16[64,640]{1,0:T(8,128)(2,1)S(1)}, u32[]{:S(2)}, u32[]{:S(2)}) %collective-permute-start.19) | collective-permute-done | bytes 81952 | tf_op jit(solution)/shard_map/ppermute | solution.py:231
  49.8 1.5 %collective-permute-done.20.refs_1_ = bf16[4,144,640]{2,1,0:T(8,128)(2,1)S(1)} collective-permute-done((bf16[4,144,640]{2,1,0:T(8,128)(2,1)S(1)}, bf16[4,144,640]{2,1,0:T(8,128)(2,1)S(1)}, u32[]{:S(2)}, u32[]{:S(2)}) %collective-permute-start.20) | collective-permute-done | bytes 737312 | tf_op jit(solution)/shard_map/ppermute | solution.py:231
  51.5 2.5 %collective-permute-start.21 = (bf16[144,384]{1,0:T(8,128)(2,1)S(1)}, bf16[144,384]{1,0:T(8,128)(2,1)S(1)}, u32[]{:S(2)}, u32[]{:S(2)}) collective-permute-start(bf16[144,384]{1,0:T(8,128)(2,1)S(1)} %get-tuple-element.65), channel_id=1, source_target_pairs={{0,6},{2,4},{4,2},{6,0},{1,7},{3,5},{5,3},{7,1},{8,14},{10,12},{12... | collective-permute-start | bytes 331784 | tf_op jit(solution)/shard_map/ppermute | solution.py:231
  54.1 2.0 %collective-permute-start.22 = (bf16[144,384]{1,0:T(8,128)(2,1)S(1)}, bf16[144,384]{1,0:T(8,128)(2,1)S(1)}, u32[]{:S(2)}, u32[]{:S(2)}) collective-permute-start(bf16[144,384]{1,0:T(8,128)(2,1)S(1)} %get-tuple-element.69), channel_id=1, source_target_pairs={{0,4},{2,6},{4,0},{6,2},{1,5},{3,7},{5,1},{7,3},{8,12},{10,14},{12... | collective-permute-start | bytes 331784 | tf_op jit(solution)/shard_map/ppermute | solution.py:231
  56.1 2.4 %collective-permute-start.27 = (bf16[216,128]{1,0:T(8,128)(2,1)S(1)}, bf16[216,128]{1,0:T(8,128)(2,1)S(1)}, u32[]{:S(2)}, u32[]{:S(2)}) collective-permute-start(bf16[216,128]{1,0:T(8,128)(2,1)S(1)} %get-tuple-element.73), channel_id=1, source_target_pairs={{0,6},{2,4},{4,2},{6,0},{1,7},{3,5},{5,3},{7,1},{8,14},{10,12},{12... | collective-permute-start | bytes 165896 | tf_op jit(solution)/shard_map/ppermute | solution.py:231
  59.5 5.1 %collective-permute-start.29 = (bf16[216,128]{1,0:T(8,128)(2,1)S(1)}, bf16[216,128]{1,0:T(8,128)(2,1)S(1)}, u32[]{:S(2)}, u32[]{:S(2)}) collective-permute-start(bf16[216,128]{1,0:T(8,128)(2,1)S(1)} %get-tuple-element.75), channel_id=1, source_target_pairs={{0,2},{2,0},{4,6},{6,4},{1,3},{3,1},{5,7},{7,5},{8,10},{10,8},{12,... | collective-permute-start | bytes 165896 | tf_op jit(solution)/shard_map/ppermute | solution.py:231
  64.7 2.4 %shard_map.86 = (bf16[64,1152]{1,0:T(8,128)(2,1)}, bf16[64,1152]{1,0:T(8,128)(2,1)}, f32[8,128]{1,0:T(8,128)S(1)}) custom-call(bf16[64,1152]{1,0:T(8,128)(2,1)S(1)} %get-tuple-element.57.refs_0_, bf16[1152,1152]{1,0:T(8,128)(2,1)S(1)} %copy-done.1, bf16[64,1152]{1,0:T(8,128)(2,1)S(1)} %get-tuple-element.58.refs_2_, bf16[1152,1152]{1,0:T(8,128)(2,1)S(1)} %copy-done, ...), custom_call_target="tpu_custom_call" | custom-call | flops 1000000000 | bytes 1000000000 | tf_op jit(solution)/shard_map/pallas_call | solution.py:43
  72.4 1.6 %collective-permute-start.26 = (bf16[144,384]{1,0:T(8,128)(2,1)S(1)}, bf16[144,384]{1,0:T(8,128)(2,1)S(1)}, u32[]{:S(2)}, u32[]{:S(2)}) collective-permute-start(bf16[144,384]{1,0:T(8,128)(2,1)S(1)} %shard_map.87.refs_0_), channel_id=1, source_target_pairs={{0,24},{8,16},{16,8},{24,0},{1,25},{9,17},{17,9},{25,1},{2,26},{10... | collective-permute-start | bytes 331784 | tf_op jit(solution)/shard_map/ppermute | solution.py:231
  75.4 2.3 %collective-permute-done.31.refs_6_ = bf16[216,128]{1,0:T(8,128)(2,1)S(1)} collective-permute-done((bf16[216,128]{1,0:T(8,128)(2,1)S(1)}, bf16[216,128]{1,0:T(8,128)(2,1)S(1)}, u32[]{:S(2)}, u32[]{:S(2)}) %collective-permute-start.31) | collective-permute-done | bytes 55328 | tf_op jit(solution)/shard_map/ppermute | solution.py:231
  (64 shorter events, 26.7 us)
Async XLA Ops:
  0.6 11.0 %collective-permute-start = (bf16[64,1152]{1,0:T(8,128)(2,1)}, bf16[64,1152]{1,0:T(8,128)(2,1)S(1)}, u32[]{:S(2)}, u32[]{:S(2)}) collective-permute-start(bf16[64,1152]{1,0:T(8,128)(2,1)} %refs_1_.3), channel_id=1, source_target_pairs={{0,8},{8,0},{16,24},{24,16},{1,9},{9,1},{17,25},{25,17},{2,10},{10... | collective-permute-start | bytes 442376 | tf_op jit(solution)/shard_map/ppermute | solution.py:231
  3.6 8.7 %collective-permute-start.1 = (bf16[64,1152]{1,0:T(8,128)(2,1)}, bf16[64,1152]{1,0:T(8,128)(2,1)S(1)}, u32[]{:S(2)}, u32[]{:S(2)}) collective-permute-start(bf16[64,1152]{1,0:T(8,128)(2,1)} %refs_1_.3), channel_id=1, source_target_pairs={{0,16},{8,24},{16,0},{24,8},{1,17},{9,25},{17,1},{25,9},{2,18},{10... | collective-permute-start | bytes 442376 | tf_op jit(solution)/shard_map/ppermute | solution.py:231
  5.2 7.2 %collective-permute-start.2 = (bf16[64,1152]{1,0:T(8,128)(2,1)}, bf16[64,1152]{1,0:T(8,128)(2,1)S(1)}, u32[]{:S(2)}, u32[]{:S(2)}) collective-permute-start(bf16[64,1152]{1,0:T(8,128)(2,1)} %refs_1_.3), channel_id=1, source_target_pairs={{0,24},{8,16},{16,8},{24,0},{1,25},{9,17},{17,9},{25,1},{2,26},{10... | collective-permute-start | bytes 442376 | tf_op jit(solution)/shard_map/ppermute | solution.py:231
  5.2 11.7 %collective-permute-start.3 = (bf16[64,1152]{1,0:T(8,128)(2,1)}, bf16[64,1152]{1,0:T(8,128)(2,1)S(1)}, u32[]{:S(2)}, u32[]{:S(2)}) collective-permute-start(bf16[64,1152]{1,0:T(8,128)(2,1)} %refs_0_.2), channel_id=1, source_target_pairs={{0,2},{2,0},{4,6},{6,4},{1,3},{3,1},{5,7},{7,5},{8,10},{10,8},{12,... | collective-permute-start | bytes 442376 | tf_op jit(solution)/shard_map/ppermute | solution.py:231
  7.2 13.1 %collective-permute-start.4 = (bf16[64,1152]{1,0:T(8,128)(2,1)}, bf16[64,1152]{1,0:T(8,128)(2,1)S(1)}, u32[]{:S(2)}, u32[]{:S(2)}) collective-permute-start(bf16[64,1152]{1,0:T(8,128)(2,1)} %refs_0_.2), channel_id=1, source_target_pairs={{0,4},{2,6},{4,0},{6,2},{1,5},{3,7},{5,1},{7,3},{8,12},{10,14},{12... | collective-permute-start | bytes 442376 | tf_op jit(solution)/shard_map/ppermute | solution.py:231
  11.7 8.7 %collective-permute-start.5 = (bf16[64,1152]{1,0:T(8,128)(2,1)}, bf16[64,1152]{1,0:T(8,128)(2,1)S(1)}, u32[]{:S(2)}, u32[]{:S(2)}) collective-permute-start(bf16[64,1152]{1,0:T(8,128)(2,1)} %refs_0_.2), channel_id=1, source_target_pairs={{0,6},{2,4},{4,2},{6,0},{1,7},{3,5},{5,3},{7,1},{8,14},{10,12},{12... | collective-permute-start | bytes 442376 | tf_op jit(solution)/shard_map/ppermute | solution.py:231
  13.5 10.5 %collective-permute-start.7 = (bf16[64,1152]{1,0:T(8,128)(2,1)S(1)}, bf16[64,1152]{1,0:T(8,128)(2,1)S(1)}, u32[]{:S(2)}, u32[]{:S(2)}) collective-permute-start(bf16[64,1152]{1,0:T(8,128)(2,1)S(1)} %get-tuple-element.43.refs_0_.refs_2_), channel_id=1, source_target_pairs={{0,8},{8,0},{16,24},{24,16},{1,9},{9,1},{17,25},{25,17},{2,10},{10... | collective-permute-start | bytes 442376 | tf_op jit(solution)/shard_map/ppermute | solution.py:231
  15.4 8.5 %collective-permute-start.8 = (bf16[64,1152]{1,0:T(8,128)(2,1)S(1)}, bf16[64,1152]{1,0:T(8,128)(2,1)S(1)}, u32[]{:S(2)}, u32[]{:S(2)}) collective-permute-start(bf16[64,1152]{1,0:T(8,128)(2,1)S(1)} %get-tuple-element.43.refs_0_.refs_2_), channel_id=1, source_target_pairs={{0,16},{8,24},{16,0},{24,8},{1,17},{9,25},{17,1},{25,9},{2,18},{10... | collective-permute-start | bytes 442376 | tf_op jit(solution)/shard_map/ppermute | solution.py:231
  16.9 7.0 %collective-permute-start.9 = (bf16[64,1152]{1,0:T(8,128)(2,1)S(1)}, bf16[64,1152]{1,0:T(8,128)(2,1)S(1)}, u32[]{:S(2)}, u32[]{:S(2)}) collective-permute-start(bf16[64,1152]{1,0:T(8,128)(2,1)S(1)} %get-tuple-element.43.refs_0_.refs_2_), channel_id=1, source_target_pairs={{0,24},{8,16},{16,8},{24,0},{1,25},{9,17},{17,9},{25,1},{2,26},{10... | collective-permute-start | bytes 442376 | tf_op jit(solution)/shard_map/ppermute | solution.py:231
  24.0 8.9 %collective-permute-start.11 = (bf16[64,1152]{1,0:T(8,128)(2,1)S(1)}, bf16[64,1152]{1,0:T(8,128)(2,1)S(1)}, u32[]{:S(2)}, u32[]{:S(2)}) collective-permute-start(bf16[64,1152]{1,0:T(8,128)(2,1)S(1)} %shard_map.81), channel_id=1, source_target_pairs={{0,2},{2,0},{4,6},{6,4},{1,3},{3,1},{5,7},{7,5},{8,10},{10,8},{12,... | collective-permute-start | bytes 442376 | tf_op jit(solution)/shard_map/ppermute | solution.py:231
  25.6 13.9 %collective-permute-start.12 = (bf16[64,1152]{1,0:T(8,128)(2,1)S(1)}, bf16[64,1152]{1,0:T(8,128)(2,1)S(1)}, u32[]{:S(2)}, u32[]{:S(2)}) collective-permute-start(bf16[64,1152]{1,0:T(8,128)(2,1)S(1)} %get-tuple-element.51), channel_id=1, source_target_pairs={{0,4},{2,6},{4,0},{6,2},{1,5},{3,7},{5,1},{7,3},{8,12},{10,14},{12... | collective-permute-start | bytes 442376 | tf_op jit(solution)/shard_map/ppermute | solution.py:231
  27.5 12.1 %collective-permute-start.13 = (bf16[64,1152]{1,0:T(8,128)(2,1)S(1)}, bf16[64,1152]{1,0:T(8,128)(2,1)S(1)}, u32[]{:S(2)}, u32[]{:S(2)}) collective-permute-start(bf16[64,1152]{1,0:T(8,128)(2,1)S(1)} %get-tuple-element.52), channel_id=1, source_target_pairs={{0,6},{2,4},{4,2},{6,0},{1,7},{3,5},{5,3},{7,1},{8,14},{10,12},{12... | collective-permute-start | bytes 442376 | tf_op jit(solution)/shard_map/ppermute | solution.py:231
  28.5 11.0 %collective-permute-start.14 = (bf16[64,1152]{1,0:T(8,128)(2,1)S(1)}, bf16[64,1152]{1,0:T(8,128)(2,1)S(1)}, u32[]{:S(2)}, u32[]{:S(2)}) collective-permute-start(bf16[64,1152]{1,0:T(8,128)(2,1)S(1)} %get-tuple-element.48.refs_10_), channel_id=1, source_target_pairs={{0,8},{8,0},{16,24},{24,16},{1,9},{9,1},{17,25},{25,17},{2,10},{10... | collective-permute-start | bytes 442376 | tf_op jit(solution)/shard_map/ppermute | solution.py:231
  30.1 9.5 %collective-permute-start.15 = (bf16[64,1152]{1,0:T(8,128)(2,1)S(1)}, bf16[64,1152]{1,0:T(8,128)(2,1)S(1)}, u32[]{:S(2)}, u32[]{:S(2)}) collective-permute-start(bf16[64,1152]{1,0:T(8,128)(2,1)S(1)} %get-tuple-element.55), channel_id=1, source_target_pairs={{0,16},{8,24},{16,0},{24,8},{1,17},{9,25},{17,1},{25,9},{2,18},{10... | collective-permute-start | bytes 442376 | tf_op jit(solution)/shard_map/ppermute | solution.py:231
  32.9 6.7 %collective-permute-start.16 = (bf16[64,1152]{1,0:T(8,128)(2,1)S(1)}, bf16[64,1152]{1,0:T(8,128)(2,1)S(1)}, u32[]{:S(2)}, u32[]{:S(2)}) collective-permute-start(bf16[64,1152]{1,0:T(8,128)(2,1)S(1)} %get-tuple-element.56), channel_id=1, source_target_pairs={{0,24},{8,16},{16,8},{24,0},{1,25},{9,17},{17,9},{25,1},{2,26},{10... | collective-permute-start | bytes 442376 | tf_op jit(solution)/shard_map/ppermute | solution.py:231
  51.5 8.0 %collective-permute-start.21 = (bf16[144,384]{1,0:T(8,128)(2,1)S(1)}, bf16[144,384]{1,0:T(8,128)(2,1)S(1)}, u32[]{:S(2)}, u32[]{:S(2)}) collective-permute-start(bf16[144,384]{1,0:T(8,128)(2,1)S(1)} %get-tuple-element.65), channel_id=1, source_target_pairs={{0,6},{2,4},{4,2},{6,0},{1,7},{3,5},{5,3},{7,1},{8,14},{10,12},{12... | collective-permute-start | bytes 331784 | tf_op jit(solution)/shard_map/ppermute | solution.py:231
  54.1 14.0 %collective-permute-start.22 = (bf16[144,384]{1,0:T(8,128)(2,1)S(1)}, bf16[144,384]{1,0:T(8,128)(2,1)S(1)}, u32[]{:S(2)}, u32[]{:S(2)}) collective-permute-start(bf16[144,384]{1,0:T(8,128)(2,1)S(1)} %get-tuple-element.69), channel_id=1, source_target_pairs={{0,4},{2,6},{4,0},{6,2},{1,5},{3,7},{5,1},{7,3},{8,12},{10,14},{12... | collective-permute-start | bytes 331784 | tf_op jit(solution)/shard_map/ppermute | solution.py:231
  56.1 12.0 %collective-permute-start.23 = (bf16[144,384]{1,0:T(8,128)(2,1)S(1)}, bf16[144,384]{1,0:T(8,128)(2,1)S(1)}, u32[]{:S(2)}, u32[]{:S(2)}) collective-permute-start(bf16[144,384]{1,0:T(8,128)(2,1)S(1)} %get-tuple-element.70), channel_id=1, source_target_pairs={{0,2},{2,0},{4,6},{6,4},{1,3},{3,1},{5,7},{7,5},{8,10},{10,8},{12,... | collective-permute-start | bytes 331784 | tf_op jit(solution)/shard_map/ppermute | solution.py:231
  56.1 13.1 %collective-permute-start.27 = (bf16[216,128]{1,0:T(8,128)(2,1)S(1)}, bf16[216,128]{1,0:T(8,128)(2,1)S(1)}, u32[]{:S(2)}, u32[]{:S(2)}) collective-permute-start(bf16[216,128]{1,0:T(8,128)(2,1)S(1)} %get-tuple-element.73), channel_id=1, source_target_pairs={{0,6},{2,4},{4,2},{6,0},{1,7},{3,5},{5,3},{7,1},{8,14},{10,12},{12... | collective-permute-start | bytes 165896 | tf_op jit(solution)/shard_map/ppermute | solution.py:231
  58.5 11.9 %collective-permute-start.28 = (bf16[216,128]{1,0:T(8,128)(2,1)S(1)}, bf16[216,128]{1,0:T(8,128)(2,1)S(1)}, u32[]{:S(2)}, u32[]{:S(2)}) collective-permute-start(bf16[216,128]{1,0:T(8,128)(2,1)S(1)} %get-tuple-element.74), channel_id=1, source_target_pairs={{0,4},{2,6},{4,0},{6,2},{1,5},{3,7},{5,1},{7,3},{8,12},{10,14},{12... | collective-permute-start | bytes 165896 | tf_op jit(solution)/shard_map/ppermute | solution.py:231
  59.5 10.8 %collective-permute-start.29 = (bf16[216,128]{1,0:T(8,128)(2,1)S(1)}, bf16[216,128]{1,0:T(8,128)(2,1)S(1)}, u32[]{:S(2)}, u32[]{:S(2)}) collective-permute-start(bf16[216,128]{1,0:T(8,128)(2,1)S(1)} %get-tuple-element.75), channel_id=1, source_target_pairs={{0,2},{2,0},{4,6},{6,4},{1,3},{3,1},{5,7},{7,5},{8,10},{10,8},{12,... | collective-permute-start | bytes 165896 | tf_op jit(solution)/shard_map/ppermute | solution.py:231
  68.2 5.8 %collective-permute-start.24 = (bf16[144,384]{1,0:T(8,128)(2,1)S(1)}, bf16[144,384]{1,0:T(8,128)(2,1)S(1)}, u32[]{:S(2)}, u32[]{:S(2)}) collective-permute-start(bf16[144,384]{1,0:T(8,128)(2,1)S(1)} %shard_map.87.refs_0_), channel_id=1, source_target_pairs={{0,8},{8,0},{16,24},{24,16},{1,9},{9,1},{17,25},{25,17},{2,10},{10... | collective-permute-start | bytes 331784 | tf_op jit(solution)/shard_map/ppermute | solution.py:231
  71.0 6.6 %collective-permute-start.31 = (bf16[216,128]{1,0:T(8,128)(2,1)S(1)}, bf16[216,128]{1,0:T(8,128)(2,1)S(1)}, u32[]{:S(2)}, u32[]{:S(2)}) collective-permute-start(bf16[216,128]{1,0:T(8,128)(2,1)S(1)} %shard_map.88.refs_0_.refs_4_), channel_id=1, source_target_pairs={{0,16},{8,24},{16,0},{24,8},{1,17},{9,25},{17,1},{25,9},{2,18},{10... | collective-permute-start | bytes 165896 | tf_op jit(solution)/shard_map/ppermute | solution.py:231
  72.4 6.1 %collective-permute-start.26 = (bf16[144,384]{1,0:T(8,128)(2,1)S(1)}, bf16[144,384]{1,0:T(8,128)(2,1)S(1)}, u32[]{:S(2)}, u32[]{:S(2)}) collective-permute-start(bf16[144,384]{1,0:T(8,128)(2,1)S(1)} %shard_map.87.refs_0_), channel_id=1, source_target_pairs={{0,24},{8,16},{16,8},{24,0},{1,25},{9,17},{17,9},{25,1},{2,26},{10... | collective-permute-start | bytes 331784 | tf_op jit(solution)/shard_map/ppermute | solution.py:231
  (12 other events, 60.6 us)

commit v6 on v5

--- a/solution.py
+++ b/solution.py
@@ -13,6 +13,7 @@
 logit_bias = -3.0
 epsilon = 1e-06
 low = jnp.bfloat16
+near = 2
 wide = jnp.float32
 cost_unit = 1_000_000_000
 
@@ -54,20 +55,20 @@
 def ready_kernel(shape, image_head_ref, text_head_ref, *refs):
     groups, layers, cores = shape
     image_refs, text_refs, refs = refs[:groups], refs[groups : 2 * groups], refs[2 * groups :]
-    image_before_ref, text_before_ref, mine_ref, theirs_ref, turned_ref = refs
+    image_before_ref, text_before_ref, *out_refs, turned_ref = refs
     image_before_ref[...] = dot(image_refs[0][...], image_head_ref[...], 1, 0)
     text_before_ref[...] = dot(text_refs[0][...], text_head_ref[...], 1, 0)
     gathered = jnp.concatenate([ref[...].astype(wide) for ref in (*image_refs, *text_refs)])
     turned_ref[...] = gathered.T
-    share, layer_pos, core_pos = mine_ref.shape[1], lax.axis_index("layer"), lax.axis_index("core")
+    share, layer_pos, core_pos = out_refs[0].shape[1], lax.axis_index("layer"), lax.axis_index("core")
     step = math.gcd(share, 8)
     for k in range(layers):
-        for ref, core in ((mine_ref, core_pos), (theirs_ref, 1 - core_pos)):
+        for i, core in enumerate((core_pos, 1 - core_pos)):
             first = ((k ^ layer_pos) * cores + core) * share
             rows = turned_ref[pl.ds(pl.multiple_of(first // 8 * 8, 8), -(-share // 8) * 8), :]
             for start in range(step, 8, step):
                 rows = jnp.where(first % 8 == start, pltpu.roll(rows, rows.shape[0] - start, 0), rows)
-            ref[k] = rows[:share].astype(low)
+            out_refs[2 * i + (k >= near)][k - near * (k >= near)] = rows[:share].astype(low)
 
 
 def own_kernel(*refs):
@@ -84,6 +85,10 @@
 def rows_kernel(*refs):
     *block_refs, head_ref, low_ref = refs
     low_ref[...] = project(jnp.concatenate([ref[...] for ref in block_refs]), head_ref[...])[1]
+
+
+def token_kernel(out_ref):
+    out_ref[...] = jnp.zeros_like(out_ref)
 
 
 def half_kernel(near_ref, far_ref, own_ref, *block_refs):
@@ -143,6 +148,14 @@
     token_ref[...] = jnp.zeros_like(token_ref)
 
 
+def add_kernel(*refs):
+    *part_refs, out_ref = refs
+    total = part_refs[0][...].astype(wide)
+    for ref in part_refs[1:]:
+        total = total + ref[...].astype(wide)
+    out_ref[...] = total
+
+
 def sum_kernel(own_ref, *refs):
     *part_refs, out_ref = refs
     total = own_ref[...]
@@ -172,7 +185,7 @@
 
 def terms_kernel(width, groups, cut, turned_ref, *refs):
     *back_refs, out_ref = refs
-    backs = jnp.concatenate([ref[...] for ref in back_refs])
+    backs = jnp.concatenate([ref[...] for ref in back_refs[:1] + back_refs[:0:-1]])
     blk, own = lax.axis_index("blk"), cut[0] * 128
     lane = lax.broadcasted_iota(jnp.int32, backs.shape, 1)
     column = lane + blk * own
@@ -185,9 +198,10 @@
         out_ref[k] = dot(turned_ref[k], backs, 1, 0).astype(out_ref.dtype)
 
 
-def layers_kernel(cut, mine_ref, theirs_ref, *refs):
+def layers_kernel(cut, both, mine_ref, theirs_ref, *refs):
     own, parts = cut[0] * 128, cut[1]
     lanes = refs[0].shape[1]
+    refs = list(refs)
     for k in range(mine_ref.shape[0]):
         total = mine_ref[k] + theirs_ref[k].astype(wide)
         second = total[:, lanes:own]
@@ -198,8 +212,29 @@
                 mine = lax.axis_index("blk") % parts == i
                 extra = jnp.where(mine, total[i * part : (i + 1) * part, own:], extra)
             second = jnp.concatenate([second, extra])
-        refs[2 * k][...] = total[:, :lanes].astype(refs[2 * k].dtype)
-        refs[2 * k + 1][...] = second.astype(refs[2 * k].dtype)
+        found = [total[:, :lanes], second]
+        for value in [joined(*found)] if both and k == 1 else found:
+            ref = refs.pop(0)
+            ref[...] = value.astype(ref.dtype)
+
+
+def joined(first, second):
+    count = first.shape[1] // second.shape[1]
+    step = second.shape[0] // count
+    return jnp.concatenate([first, jnp.concatenate([second[i * step : (i + 1) * step] for i in range(count)], axis=1)])
+
+
+def parted(array, share):
+    rest = array[share:]
+    return array[:share], jnp.concatenate([rest[:, i : i + 128] for i in range(0, array.shape[1], 128)])
+
+
+def sums_kernel(share, group, own_ref, both_ref, *refs):
+    *part_refs, out_ref = refs
+    total = own_ref[...] + parted(both_ref[...].astype(wide), share)[group]
+    for ref in part_refs:
+        total = total + ref[...].astype(wide)
+    out_ref[...] = total.astype(low)
 
 
 def heads_kernel(groups, cut, *refs):
@@ -207,10 +242,10 @@
     (share, width), (_, lanes), (own, parts) = image_ref.shape, block_refs[0].shape, (cut[0] * 128, cut[1])
     for k in range(groups):
         blk = k ^ lax.axis_index("blk")
-        first = pl.multiple_of(blk * own, 128)
-        second = block_refs[groups + k][...].astype(wide)
-        all_ref[:, pl.ds(first, lanes)] = block_refs[k][...].astype(wide)
-        all_ref[:, pl.ds(first + lanes, own - lanes)] = second[:share]
+        start = pl.multiple_of(blk * own, 128)
+        first, second = (block_refs[i * groups + k][...].astype(wide) for i in (0, 1))
+        all_ref[:, pl.ds(start, lanes)] = first
+        all_ref[:, pl.ds(start + lanes, own - lanes)] = second[:share]
         if parts:
             part = share // parts
             row = pl.multiple_of(blk % parts * part, 8)
@@ -274,10 +309,10 @@
     text_total, *text_out = call(half_kernel, outs, near_part, over_core(far_part), cost=1)
     text_parts = [over(block, "blk", k + 1) for k, block in enumerate(text_out)]
 
-    turned = ((layers, share, 2 * half), low)
-    image_before, text_before, turned_mine, turned_theirs = call(
+    turned = [((count, share, 2 * half), low) for count in (near, layers - near)]
+    image_before, text_before, *turned = call(
         functools.partial(ready_kernel, (groups, layers, cores)),
-        [(block, wide), (block, wide), turned, turned],
+        [(block, wide), (block, wide), *turned, *turned],
         *(image_head, text_head, *image_group, *caption_blocks),
         scratch=[((width, 2 * half), wide)],
         behind=text_out[:1],
@@ -290,33 +325,50 @@
         cost=80,
         scratch=[((rows, columns), low)],
     )
-    backs = [sends[0]] + [over(block, "blk", k + 1) for k, block in enumerate(sends[1:])]
-    shape = (layers, share, lanes)
+    backs = [sends[0]] + [over(sends[k], "blk", k) for k in range(groups - 1, 0, -1)]
+    count = first[1] // 128
+    both = second[1] == 128 and second[0] % (8 * count) == 0 and share % 8 == 0
+    pair = [(first, low), (second, low)]
+    joint = (share + second[0] // count, first[1])
     kernel = functools.partial(terms_kernel, width, groups, cut)
-    theirs = call(kernel, [(shape, low)], turned_theirs, *backs)[0]
-    mine = call(kernel, [(shape, wide)], turned_mine, *backs, behind=[theirs])[0]
-    outs = [(first, wide), (second, wide)] + [(first, low), (second, low)] * (layers - 1)
-    terms = call(functools.partial(layers_kernel, cut), outs, mine, over_core(theirs))
+    sums, made = [], backs[:1]
+    for i, outs in ((1, pair * (layers - near)), (0, [(first, wide), (second, wide)] + ([(joint, low)] if both else pair))):
+        shape = (layers - near if i else near, share, lanes)
+        theirs = call(kernel, [(shape, low)], turned[2 + i], *backs, behind=made)[0]
+        mine = call(kernel, [(shape, wide)], turned[i], *backs, behind=[theirs])[0]
+        made = [theirs]
+        sums.append(call(functools.partial(layers_kernel, cut, both and not i), outs, mine, over_core(theirs)))
+    terms, (first_own, second_own, *nearest) = sums
+    next_layer = [over(block, "layer", 1) for block in nearest]
     first_parts, second_parts = (
-        [over(terms[2 * k + i], "layer", k) for k in range(layers - 1, 0, -1)] for i in (0, 1)
+        [over(terms[2 * k - 4 + i], "layer", k) for k in range(layers - 1, 1, -1)] for i in (0, 1)
     )
     grad_images, grad_captions, token = call(
         grads_kernel,
         [(block, low), (block, low), ((8, 128), wide)],
         *(image_back, image_head, text_back, text_head),
-        behind=[first_parts[0]],
-    )
-    first_sum = call(sum_kernel, [(first, low)], terms[0], *first_parts, cost=50, behind=[token])[0]
+        behind=[mine],
+    )
+    if both:
+        kernels = [functools.partial(sums_kernel, share, i) for i in (0, 1)]
+        next_layer = next_layer * 2
+    else:
+        kernels = [sum_kernel] * 2
+    added = call(add_kernel, [(first, wide)], *first_parts, cost=6)[0]
+    first_sum = call(kernels[0], [(first, low)], first_own, next_layer[0], added, cost=50, behind=[token])[0]
     first_sums = over_blk(first_sum)
-    second_sum = call(sum_kernel, [(second, low)], terms[1], *second_parts, cost=1)[0]
-    last_sum = call(own_kernel, [(second, low)], second_sum, behind=first_sums[1:3], cost=1)[0]
-    second_sums = [second_sum] + [over(second_sum, "blk", k) for k in range(1, groups - 1)]
-    blocks = first_sums + second_sums + [over(last_sum, "blk", groups - 1)]
+    second_sum = call(kernels[1], [(second, low)], second_own, next_layer[1], *second_parts, cost=1)[0]
+    later_sum = call(own_kernel, [(second, low)], second_sum, behind=first_sums[1:2], cost=1)[0]
+    second_sums = [over(second_sum, "blk", k) for k in range(groups - 1, 0, -1) if k != 1][::-1]
+    second_sums.insert(1 - 1, over(later_sum, "blk", 1))
+    blocks = first_sums + [second_sum] + second_sums
+    token = call(token_kernel, [((8, 128), wide)], behind=first_sums[2:], cost=10)[0]
     grad_image_head, grad_text_head = call(
         functools.partial(heads_kernel, groups, cut),
         [((share, width), wide)] * 2,
         *blocks,
         scratch=[((share, columns), wide)],
+        behind=[token],
     )
     return (grad_images, grad_captions, grad_image_head, grad_text_head)
 

time: 80.5 us -> 78 us (0.969)
  starting transfers between devices: 46.4 us -> 42.7 us
    ppermute x33, starting transfers between devices: 46.4 us -> 42.7 us  [over(): lax.ppermute(array, axis, [(i, i ^ by) for i in range(lax.axis_size(axis))])]
    ppermute x33, waiting for transfers between devices: 20.9 us -> 21.7 us  [over(): lax.ppermute(array, axis, [(i, i ^ by) for i in range(lax.axis_size(axis))])]
    pallas_call x16 -> x21, Pallas kernels: 11.3 us -> 11.7 us  [call(): pl.pallas_call(body, out_shape=tuple((jax.ShapeDtypeStruct(shape, kind) f...]
  transfers between devices with their start and end apart: 33 -> 33, of which waited for: 13 -> 13; matrix products, arithmetic and copies ran while one was open for 0% -> 0% of each run, Pallas kernels for 11% -> 12%
where the time goes in v6:
time: 78 us; the launch traced here: 77.9 us
  starting transfers between devices  42.7 us (55%)
  waiting for transfers between devices  21.7 us (28%)
  Pallas kernels  11.7 us (15%)
  local copies, waits for them, and re-layouts  0.92 us (1%)
  between operations  0.81 us (1%)
    ppermute x33, starting transfers between devices, over(): lax.ppermute(array, axis, [(i, i ^ by) for i in range(lax.axis_size(axis))])  42.7 us
    ppermute x33, waiting for transfers between devices, over(): lax.ppermute(array, axis, [(i, i ^ by) for i in range(lax.axis_size(axis))])  21.7 us
    pallas_call x21, Pallas kernels, call(): pl.pallas_call(body, out_shape=tuple((jax.ShapeDtypeStruct(shape, kind) f...  11.7 us
  transfers between devices with their start and end apart: 33, of which 13 were waited for; matrix products, arithmetic and copies ran while one was open for 0% of the time, Pallas kernels for 12%

profile of v6, /device:TPU:0, one launch (start us, length us, event | category | flops | bytes accessed | tf_op | source)
XLA Modules:
  0.0 77.9 jit_solution(5551947668788493148)
XLA Ops:
  0.6 3.0 %collective-permute-start = (bf16[64,1152]{1,0:T(8,128)(2,1)}, bf16[64,1152]{1,0:T(8,128)(2,1)S(1)}, u32[]{:S(2)}, u32[]{:S(2)}) collective-permute-start(bf16[64,1152]{1,0:T(8,128)(2,1)} %refs_1_.3), channel_id=1, source_target_pairs={{0,8},{8,0},{16,24},{24,16},{1,9},{9,1},{17,25},{25,17},{2,10},{10... | collective-permute-start | bytes 442376 | tf_op jit(solution)/shard_map/ppermute | solution.py:266
  3.6 1.5 %collective-permute-start.1 = (bf16[64,1152]{1,0:T(8,128)(2,1)}, bf16[64,1152]{1,0:T(8,128)(2,1)S(1)}, u32[]{:S(2)}, u32[]{:S(2)}) collective-permute-start(bf16[64,1152]{1,0:T(8,128)(2,1)} %refs_1_.3), channel_id=1, source_target_pairs={{0,16},{8,24},{16,0},{24,8},{1,17},{9,25},{17,1},{25,9},{2,18},{10... | collective-permute-start | bytes 442376 | tf_op jit(solution)/shard_map/ppermute | solution.py:266
  5.2 2.0 %collective-permute-start.3 = (bf16[64,1152]{1,0:T(8,128)(2,1)}, bf16[64,1152]{1,0:T(8,128)(2,1)S(1)}, u32[]{:S(2)}, u32[]{:S(2)}) collective-permute-start(bf16[64,1152]{1,0:T(8,128)(2,1)} %refs_0_.2), channel_id=1, source_target_pairs={{0,2},{2,0},{4,6},{6,4},{1,3},{3,1},{5,7},{7,5},{8,10},{10,8},{12,... | collective-permute-start | bytes 442376 | tf_op jit(solution)/shard_map/ppermute | solution.py:266
  7.2 2.6 %collective-permute-start.4 = (bf16[64,1152]{1,0:T(8,128)(2,1)}, bf16[64,1152]{1,0:T(8,128)(2,1)S(1)}, u32[]{:S(2)}, u32[]{:S(2)}) collective-permute-start(bf16[64,1152]{1,0:T(8,128)(2,1)} %refs_0_.2), channel_id=1, source_target_pairs={{0,4},{2,6},{4,0},{6,2},{1,5},{3,7},{5,1},{7,3},{8,12},{10,14},{12... | collective-permute-start | bytes 442376 | tf_op jit(solution)/shard_map/ppermute | solution.py:266
  13.5 1.9 %collective-permute-start.7 = (bf16[64,1152]{1,0:T(8,128)(2,1)S(1)}, bf16[64,1152]{1,0:T(8,128)(2,1)S(1)}, u32[]{:S(2)}, u32[]{:S(2)}) collective-permute-start(bf16[64,1152]{1,0:T(8,128)(2,1)S(1)} %get-tuple-element.44.refs_0_.refs_2_), channel_id=1, source_target_pairs={{0,8},{8,0},{16,24},{24,16},{1,9},{9,1},{17,25},{25,17},{2,10},{10... | collective-permute-start | bytes 442376 | tf_op jit(solution)/shard_map/ppermute | solution.py:266
  15.4 1.5 %collective-permute-start.8 = (bf16[64,1152]{1,0:T(8,128)(2,1)S(1)}, bf16[64,1152]{1,0:T(8,128)(2,1)S(1)}, u32[]{:S(2)}, u32[]{:S(2)}) collective-permute-start(bf16[64,1152]{1,0:T(8,128)(2,1)S(1)} %get-tuple-element.44.refs_0_.refs_2_), channel_id=1, source_target_pairs={{0,16},{8,24},{16,0},{24,8},{1,17},{9,25},{17,1},{25,9},{2,18},{10... | collective-permute-start | bytes 442376 | tf_op jit(solution)/shard_map/ppermute | solution.py:266
  17.0 3.3 %collective-permute-done.4.refs_2_ = bf16[64,1152]{1,0:T(8,128)(2,1)S(1)} collective-permute-done((bf16[64,1152]{1,0:T(8,128)(2,1)}, bf16[64,1152]{1,0:T(8,128)(2,1)S(1)}, u32[]{:S(2)}, u32[]{:S(2)}) %collective-permute-start.4) | collective-permute-done | bytes 147488 | tf_op jit(solution)/shard_map/ppermute | solution.py:266
  22.3 1.4 %shard_map.78 = (f32[64,1152]{1,0:T(8,128)S(1)}, bf16[64,1152]{1,0:T(8,128)(2,1)S(1)}, bf16[64,1152]{1,0:T(8,128)(2,1)S(1)}, bf16[64,1152]{1,0:T(8,128)(2,1)S(1)...) custom-call(bf16[256,1152]{1,0:T(8,128)(2,1)S(1)} %shard_map.77.refs_0_, ...), custom_call_target="tpu_custom_call" | custom-call | flops 1000000000 | bytes 1000000000 | tf_op jit(solution)/shard_map/pallas_call | solution.py:44
  24.0 1.7 %collective-permute-start.11 = (bf16[64,1152]{1,0:T(8,128)(2,1)S(1)}, bf16[64,1152]{1,0:T(8,128)(2,1)S(1)}, u32[]{:S(2)}, u32[]{:S(2)}) collective-permute-start(bf16[64,1152]{1,0:T(8,128)(2,1)S(1)} %shard_map.81), channel_id=1, source_target_pairs={{0,2},{2,0},{4,6},{6,4},{1,3},{3,1},{5,7},{7,5},{8,10},{10,8},{12,... | collective-permute-start | bytes 442376 | tf_op jit(solution)/shard_map/ppermute | solution.py:266
  25.6 1.9 %collective-permute-start.12 = (bf16[64,1152]{1,0:T(8,128)(2,1)S(1)}, bf16[64,1152]{1,0:T(8,128)(2,1)S(1)}, u32[]{:S(2)}, u32[]{:S(2)}) collective-permute-start(bf16[64,1152]{1,0:T(8,128)(2,1)S(1)} %get-tuple-element.52), channel_id=1, source_target_pairs={{0,4},{2,6},{4,0},{6,2},{1,5},{3,7},{5,1},{7,3},{8,12},{10,14},{12... | collective-permute-start | bytes 442376 | tf_op jit(solution)/shard_map/ppermute | solution.py:266
  28.5 1.6 %collective-permute-start.14 = (bf16[64,1152]{1,0:T(8,128)(2,1)S(1)}, bf16[64,1152]{1,0:T(8,128)(2,1)S(1)}, u32[]{:S(2)}, u32[]{:S(2)}) collective-permute-start(bf16[64,1152]{1,0:T(8,128)(2,1)S(1)} %get-tuple-element.49.refs_10_), channel_id=1, source_target_pairs={{0,8},{8,0},{16,24},{24,16},{1,9},{9,1},{17,25},{25,17},{2,10},{10... | collective-permute-start | bytes 442376 | tf_op jit(solution)/shard_map/ppermute | solution.py:266
  30.1 1.5 %collective-permute-start.15 = (bf16[64,1152]{1,0:T(8,128)(2,1)S(1)}, bf16[64,1152]{1,0:T(8,128)(2,1)S(1)}, u32[]{:S(2)}, u32[]{:S(2)}) collective-permute-start(bf16[64,1152]{1,0:T(8,128)(2,1)S(1)} %get-tuple-element.56), channel_id=1, source_target_pairs={{0,16},{8,24},{16,0},{24,8},{1,17},{9,25},{17,1},{25,9},{2,18},{10... | collective-permute-start | bytes 442376 | tf_op jit(solution)/shard_map/ppermute | solution.py:266
  32.9 2.5 %collective-permute-start.16 = (bf16[64,1152]{1,0:T(8,128)(2,1)S(1)}, bf16[64,1152]{1,0:T(8,128)(2,1)S(1)}, u32[]{:S(2)}, u32[]{:S(2)}) collective-permute-start(bf16[64,1152]{1,0:T(8,128)(2,1)S(1)} %get-tuple-element.57), channel_id=1, source_target_pairs={{0,24},{8,16},{16,8},{24,0},{1,25},{9,17},{17,9},{25,1},{2,26},{10... | collective-permute-start | bytes 442376 | tf_op jit(solution)/shard_map/ppermute | solution.py:266
  36.5 3.1 %collective-permute-done.12.refs_3_ = bf16[64,1152]{1,0:T(8,128)(2,1)S(1)} collective-permute-done((bf16[64,1152]{1,0:T(8,128)(2,1)S(1)}, bf16[64,1152]{1,0:T(8,128)(2,1)S(1)}, u32[]{:S(2)}, u32[]{:S(2)}) %collective-permute-start.12) | collective-permute-done | bytes 147488 | tf_op jit(solution)/shard_map/ppermute | solution.py:266
  40.0 2.5 %collective-permute-start.17 = (bf16[64,640]{1,0:T(8,128)(2,1)S(1)}, bf16[64,640]{1,0:T(8,128)(2,1)S(1)}, u32[]{:S(2)}, u32[]{:S(2)}) collective-permute-start(bf16[64,640]{1,0:T(8,128)(2,1)S(1)} %get-tuple-element.62), channel_id=1, source_target_pairs={{0,24},{8,16},{16,8},{24,0},{1,25},{9,17},{17,9},{25,1},{2,26},{10... | collective-permute-start | bytes 245768 | tf_op jit(solution)/shard_map/ppermute | solution.py:266
  43.6 2.5 %collective-permute-done.17.refs_2_ = bf16[64,640]{1,0:T(8,128)(2,1)S(1)} collective-permute-done((bf16[64,640]{1,0:T(8,128)(2,1)S(1)}, bf16[64,640]{1,0:T(8,128)(2,1)S(1)}, u32[]{:S(2)}, u32[]{:S(2)}) %collective-permute-start.17) | collective-permute-done | bytes 81952 | tf_op jit(solution)/shard_map/ppermute | solution.py:266
  49.9 2.5 %collective-permute-start.23 = (bf16[144,384]{1,0:T(8,128)(2,1)S(1)}, bf16[144,384]{1,0:T(8,128)(2,1)S(1)}, u32[]{:S(2)}, u32[]{:S(2)}) collective-permute-start(bf16[144,384]{1,0:T(8,128)(2,1)S(1)} %get-tuple-element.72), channel_id=1, source_target_pairs={{0,6},{2,4},{4,2},{6,0},{1,7},{3,5},{5,3},{7,1},{8,14},{10,12},{12... | collective-permute-start | bytes 331784 | tf_op jit(solution)/shard_map/ppermute | solution.py:266
  52.4 2.0 %collective-permute-start.24 = (bf16[144,384]{1,0:T(8,128)(2,1)S(1)}, bf16[144,384]{1,0:T(8,128)(2,1)S(1)}, u32[]{:S(2)}, u32[]{:S(2)}) collective-permute-start(bf16[144,384]{1,0:T(8,128)(2,1)S(1)} %get-tuple-element.73), channel_id=1, source_target_pairs={{0,4},{2,6},{4,0},{6,2},{1,5},{3,7},{5,1},{7,3},{8,12},{10,14},{12... | collective-permute-start | bytes 331784 | tf_op jit(solution)/shard_map/ppermute | solution.py:266
  54.4 2.4 %shard_map.86 = (bf16[64,1152]{1,0:T(8,128)(2,1)}, bf16[64,1152]{1,0:T(8,128)(2,1)}, f32[8,128]{1,0:T(8,128)S(1)}) custom-call(bf16[64,1152]{1,0:T(8,128)(2,1)S(1)} %get-tuple-element.58.refs_0_, bf16[1152,1152]{1,0:T(8,128)(2,1)S(1)} %copy-done.1, bf16[64,1152]{1,0:T(8,128)(2,1)S(1)} %get-tuple-element.59.refs_2_, bf16[1152,1152]{1,0:T(8,128)(2,1)S(1)} %copy-done, ...), custom_call_target="tpu_custom_call" | custom-call | flops 1000000000 | bytes 1000000000 | tf_op jit(solution)/shard_map/pallas_call | solution.py:44
  57.0 2.4 %collective-permute-start.28 = (bf16[216,128]{1,0:T(8,128)(2,1)S(1)}, bf16[216,128]{1,0:T(8,128)(2,1)S(1)}, u32[]{:S(2)}, u32[]{:S(2)}) collective-permute-start(bf16[216,128]{1,0:T(8,128)(2,1)S(1)} %get-tuple-element.76), channel_id=1, source_target_pairs={{0,6},{2,4},{4,2},{6,0},{1,7},{3,5},{5,3},{7,1},{8,14},{10,12},{12... | collective-permute-start | bytes 165896 | tf_op jit(solution)/shard_map/ppermute | solution.py:266
  60.4 5.9 %collective-permute-done.24.refs_1_ = bf16[144,384]{1,0:T(8,128)(2,1)S(1)} collective-permute-done((bf16[144,384]{1,0:T(8,128)(2,1)S(1)}, bf16[144,384]{1,0:T(8,128)(2,1)S(1)}, u32[]{:S(2)}, u32[]{:S(2)}) %collective-permute-start.24) | collective-permute-done | bytes 110624 | tf_op jit(solution)/shard_map/ppermute | solution.py:266
  67.0 1.5 %collective-permute-start.26 = (bf16[144,384]{1,0:T(8,128)(2,1)S(1)}, bf16[144,384]{1,0:T(8,128)(2,1)S(1)}, u32[]{:S(2)}, u32[]{:S(2)}) collective-permute-start(bf16[144,384]{1,0:T(8,128)(2,1)S(1)} %shard_map.91.refs_0_), channel_id=1, source_target_pairs={{0,16},{8,24},{16,0},{24,8},{1,17},{9,25},{17,1},{25,9},{2,18},{10... | collective-permute-start | bytes 331784 | tf_op jit(solution)/shard_map/ppermute | solution.py:266
  68.5 1.4 %collective-permute-start.27 = (bf16[144,384]{1,0:T(8,128)(2,1)S(1)}, bf16[144,384]{1,0:T(8,128)(2,1)S(1)}, u32[]{:S(2)}, u32[]{:S(2)}) collective-permute-start(bf16[144,384]{1,0:T(8,128)(2,1)S(1)} %shard_map.91.refs_0_), channel_id=1, source_target_pairs={{0,24},{8,16},{16,8},{24,0},{1,25},{9,17},{17,9},{25,1},{2,26},{10... | collective-permute-start | bytes 331784 | tf_op jit(solution)/shard_map/ppermute | solution.py:266
  70.0 1.6 %collective-permute-start.31 = (bf16[216,128]{1,0:T(8,128)(2,1)S(1)}, bf16[216,128]{1,0:T(8,128)(2,1)S(1)}, u32[]{:S(2)}, u32[]{:S(2)}) collective-permute-start(bf16[216,128]{1,0:T(8,128)(2,1)S(1)} %shard_map.92.refs_0_.refs_4_), channel_id=1, source_target_pairs={{0,16},{8,24},{16,0},{24,8},{1,17},{9,25},{17,1},{25,9},{2,18},{10... | collective-permute-start | bytes 165896 | tf_op jit(solution)/shard_map/ppermute | solution.py:266
  (69 shorter events, 22.7 us)
Async XLA Ops:
  0.6 11.0 %collective-permute-start = (bf16[64,1152]{1,0:T(8,128)(2,1)}, bf16[64,1152]{1,0:T(8,128)(2,1)S(1)}, u32[]{:S(2)}, u32[]{:S(2)}) collective-permute-start(bf16[64,1152]{1,0:T(8,128)(2,1)} %refs_1_.3), channel_id=1, source_target_pairs={{0,8},{8,0},{16,24},{24,16},{1,9},{9,1},{17,25},{25,17},{2,10},{10... | collective-permute-start | bytes 442376 | tf_op jit(solution)/shard_map/ppermute | solution.py:266
  3.6 8.7 %collective-permute-start.1 = (bf16[64,1152]{1,0:T(8,128)(2,1)}, bf16[64,1152]{1,0:T(8,128)(2,1)S(1)}, u32[]{:S(2)}, u32[]{:S(2)}) collective-permute-start(bf16[64,1152]{1,0:T(8,128)(2,1)} %refs_1_.3), channel_id=1, source_target_pairs={{0,16},{8,24},{16,0},{24,8},{1,17},{9,25},{17,1},{25,9},{2,18},{10... | collective-permute-start | bytes 442376 | tf_op jit(solution)/shard_map/ppermute | solution.py:266
  5.2 7.2 %collective-permute-start.2 = (bf16[64,1152]{1,0:T(8,128)(2,1)}, bf16[64,1152]{1,0:T(8,128)(2,1)S(1)}, u32[]{:S(2)}, u32[]{:S(2)}) collective-permute-start(bf16[64,1152]{1,0:T(8,128)(2,1)} %refs_1_.3), channel_id=1, source_target_pairs={{0,24},{8,16},{16,8},{24,0},{1,25},{9,17},{17,9},{25,1},{2,26},{10... | collective-permute-start | bytes 442376 | tf_op jit(solution)/shard_map/ppermute | solution.py:266
  5.2 11.7 %collective-permute-start.3 = (bf16[64,1152]{1,0:T(8,128)(2,1)}, bf16[64,1152]{1,0:T(8,128)(2,1)S(1)}, u32[]{:S(2)}, u32[]{:S(2)}) collective-permute-start(bf16[64,1152]{1,0:T(8,128)(2,1)} %refs_0_.2), channel_id=1, source_target_pairs={{0,2},{2,0},{4,6},{6,4},{1,3},{3,1},{5,7},{7,5},{8,10},{10,8},{12,... | collective-permute-start | bytes 442376 | tf_op jit(solution)/shard_map/ppermute | solution.py:266
  7.2 13.1 %collective-permute-start.4 = (bf16[64,1152]{1,0:T(8,128)(2,1)}, bf16[64,1152]{1,0:T(8,128)(2,1)S(1)}, u32[]{:S(2)}, u32[]{:S(2)}) collective-permute-start(bf16[64,1152]{1,0:T(8,128)(2,1)} %refs_0_.2), channel_id=1, source_target_pairs={{0,4},{2,6},{4,0},{6,2},{1,5},{3,7},{5,1},{7,3},{8,12},{10,14},{12... | collective-permute-start | bytes 442376 | tf_op jit(solution)/shard_map/ppermute | solution.py:266
  11.7 8.7 %collective-permute-start.5 = (bf16[64,1152]{1,0:T(8,128)(2,1)}, bf16[64,1152]{1,0:T(8,128)(2,1)S(1)}, u32[]{:S(2)}, u32[]{:S(2)}) collective-permute-start(bf16[64,1152]{1,0:T(8,128)(2,1)} %refs_0_.2), channel_id=1, source_target_pairs={{0,6},{2,4},{4,2},{6,0},{1,7},{3,5},{5,3},{7,1},{8,14},{10,12},{12... | collective-permute-start | bytes 442376 | tf_op jit(solution)/shard_map/ppermute | solution.py:266
  13.5 10.5 %collective-permute-start.7 = (bf16[64,1152]{1,0:T(8,128)(2,1)S(1)}, bf16[64,1152]{1,0:T(8,128)(2,1)S(1)}, u32[]{:S(2)}, u32[]{:S(2)}) collective-permute-start(bf16[64,1152]{1,0:T(8,128)(2,1)S(1)} %get-tuple-element.44.refs_0_.refs_2_), channel_id=1, source_target_pairs={{0,8},{8,0},{16,24},{24,16},{1,9},{9,1},{17,25},{25,17},{2,10},{10... | collective-permute-start | bytes 442376 | tf_op jit(solution)/shard_map/ppermute | solution.py:266
  15.4 8.5 %collective-permute-start.8 = (bf16[64,1152]{1,0:T(8,128)(2,1)S(1)}, bf16[64,1152]{1,0:T(8,128)(2,1)S(1)}, u32[]{:S(2)}, u32[]{:S(2)}) collective-permute-start(bf16[64,1152]{1,0:T(8,128)(2,1)S(1)} %get-tuple-element.44.refs_0_.refs_2_), channel_id=1, source_target_pairs={{0,16},{8,24},{16,0},{24,8},{1,17},{9,25},{17,1},{25,9},{2,18},{10... | collective-permute-start | bytes 442376 | tf_op jit(solution)/shard_map/ppermute | solution.py:266
  16.9 7.0 %collective-permute-start.9 = (bf16[64,1152]{1,0:T(8,128)(2,1)S(1)}, bf16[64,1152]{1,0:T(8,128)(2,1)S(1)}, u32[]{:S(2)}, u32[]{:S(2)}) collective-permute-start(bf16[64,1152]{1,0:T(8,128)(2,1)S(1)} %get-tuple-element.44.refs_0_.refs_2_), channel_id=1, source_target_pairs={{0,24},{8,16},{16,8},{24,0},{1,25},{9,17},{17,9},{25,1},{2,26},{10... | collective-permute-start | bytes 442376 | tf_op jit(solution)/shard_map/ppermute | solution.py:266
  24.0 8.9 %collective-permute-start.11 = (bf16[64,1152]{1,0:T(8,128)(2,1)S(1)}, bf16[64,1152]{1,0:T(8,128)(2,1)S(1)}, u32[]{:S(2)}, u32[]{:S(2)}) collective-permute-start(bf16[64,1152]{1,0:T(8,128)(2,1)S(1)} %shard_map.81), channel_id=1, source_target_pairs={{0,2},{2,0},{4,6},{6,4},{1,3},{3,1},{5,7},{7,5},{8,10},{10,8},{12,... | collective-permute-start | bytes 442376 | tf_op jit(solution)/shard_map/ppermute | solution.py:266
  25.6 13.9 %collective-permute-start.12 = (bf16[64,1152]{1,0:T(8,128)(2,1)S(1)}, bf16[64,1152]{1,0:T(8,128)(2,1)S(1)}, u32[]{:S(2)}, u32[]{:S(2)}) collective-permute-start(bf16[64,1152]{1,0:T(8,128)(2,1)S(1)} %get-tuple-element.52), channel_id=1, source_target_pairs={{0,4},{2,6},{4,0},{6,2},{1,5},{3,7},{5,1},{7,3},{8,12},{10,14},{12... | collective-permute-start | bytes 442376 | tf_op jit(solution)/shard_map/ppermute | solution.py:266
  27.5 12.1 %collective-permute-start.13 = (bf16[64,1152]{1,0:T(8,128)(2,1)S(1)}, bf16[64,1152]{1,0:T(8,128)(2,1)S(1)}, u32[]{:S(2)}, u32[]{:S(2)}) collective-permute-start(bf16[64,1152]{1,0:T(8,128)(2,1)S(1)} %get-tuple-element.53), channel_id=1, source_target_pairs={{0,6},{2,4},{4,2},{6,0},{1,7},{3,5},{5,3},{7,1},{8,14},{10,12},{12... | collective-permute-start | bytes 442376 | tf_op jit(solution)/shard_map/ppermute | solution.py:266
  28.5 11.0 %collective-permute-start.14 = (bf16[64,1152]{1,0:T(8,128)(2,1)S(1)}, bf16[64,1152]{1,0:T(8,128)(2,1)S(1)}, u32[]{:S(2)}, u32[]{:S(2)}) collective-permute-start(bf16[64,1152]{1,0:T(8,128)(2,1)S(1)} %get-tuple-element.49.refs_10_), channel_id=1, source_target_pairs={{0,8},{8,0},{16,24},{24,16},{1,9},{9,1},{17,25},{25,17},{2,10},{10... | collective-permute-start | bytes 442376 | tf_op jit(solution)/shard_map/ppermute | solution.py:266
  30.1 9.5 %collective-permute-start.15 = (bf16[64,1152]{1,0:T(8,128)(2,1)S(1)}, bf16[64,1152]{1,0:T(8,128)(2,1)S(1)}, u32[]{:S(2)}, u32[]{:S(2)}) collective-permute-start(bf16[64,1152]{1,0:T(8,128)(2,1)S(1)} %get-tuple-element.56), channel_id=1, source_target_pairs={{0,16},{8,24},{16,0},{24,8},{1,17},{9,25},{17,1},{25,9},{2,18},{10... | collective-permute-start | bytes 442376 | tf_op jit(solution)/shard_map/ppermute | solution.py:266
  32.9 6.7 %collective-permute-start.16 = (bf16[64,1152]{1,0:T(8,128)(2,1)S(1)}, bf16[64,1152]{1,0:T(8,128)(2,1)S(1)}, u32[]{:S(2)}, u32[]{:S(2)}) collective-permute-start(bf16[64,1152]{1,0:T(8,128)(2,1)S(1)} %get-tuple-element.57), channel_id=1, source_target_pairs={{0,24},{8,16},{16,8},{24,0},{1,25},{9,17},{17,9},{25,1},{2,26},{10... | collective-permute-start | bytes 442376 | tf_op jit(solution)/shard_map/ppermute | solution.py:266
  40.0 6.0 %collective-permute-start.17 = (bf16[64,640]{1,0:T(8,128)(2,1)S(1)}, bf16[64,640]{1,0:T(8,128)(2,1)S(1)}, u32[]{:S(2)}, u32[]{:S(2)}) collective-permute-start(bf16[64,640]{1,0:T(8,128)(2,1)S(1)} %get-tuple-element.62), channel_id=1, source_target_pairs={{0,24},{8,16},{16,8},{24,0},{1,25},{9,17},{17,9},{25,1},{2,26},{10... | collective-permute-start | bytes 245768 | tf_op jit(solution)/shard_map/ppermute | solution.py:266
  48.4 8.4 %collective-permute-start.20 = (bf16[2,144,640]{2,1,0:T(8,128)(2,1)S(1)}, bf16[2,144,640]{2,1,0:T(8,128)(2,1)S(1)}, u32[]{:S(2)}, u32[]{:S(2)}) collective-permute-start(bf16[2,144,640]{2,1,0:T(8,128)(2,1)S(1)} %shard_map.84.refs_5_), channel_id=1, source_target_pairs={{0,1},{1,0},{2,3},{3,2},{4,5},{5,4},{6,7},{7,6},{8,9},{9,8},{10,11... | collective-permute-start | bytes 1105928 | tf_op jit(solution)/shard_map/ppermute | solution.py:266
  49.9 10.5 %collective-permute-start.23 = (bf16[144,384]{1,0:T(8,128)(2,1)S(1)}, bf16[144,384]{1,0:T(8,128)(2,1)S(1)}, u32[]{:S(2)}, u32[]{:S(2)}) collective-permute-start(bf16[144,384]{1,0:T(8,128)(2,1)S(1)} %get-tuple-element.72), channel_id=1, source_target_pairs={{0,6},{2,4},{4,2},{6,0},{1,7},{3,5},{5,3},{7,1},{8,14},{10,12},{12... | collective-permute-start | bytes 331784 | tf_op jit(solution)/shard_map/ppermute | solution.py:266
  52.4 13.9 %collective-permute-start.24 = (bf16[144,384]{1,0:T(8,128)(2,1)S(1)}, bf16[144,384]{1,0:T(8,128)(2,1)S(1)}, u32[]{:S(2)}, u32[]{:S(2)}) collective-permute-start(bf16[144,384]{1,0:T(8,128)(2,1)S(1)} %get-tuple-element.73), channel_id=1, source_target_pairs={{0,4},{2,6},{4,0},{6,2},{1,5},{3,7},{5,1},{7,3},{8,12},{10,14},{12... | collective-permute-start | bytes 331784 | tf_op jit(solution)/shard_map/ppermute | solution.py:266
  56.9 9.5 %collective-permute-start.21 = (bf16[216,384]{1,0:T(8,128)(2,1)S(1)}, bf16[216,384]{1,0:T(8,128)(2,1)S(1)}, u32[]{:S(2)}, u32[]{:S(2)}) collective-permute-start(bf16[216,384]{1,0:T(8,128)(2,1)S(1)} %get-tuple-element.70), channel_id=1, source_target_pairs={{0,2},{2,0},{4,6},{6,4},{1,3},{3,1},{5,7},{7,5},{8,10},{10,8},{12,... | collective-permute-start | bytes 497672 | tf_op jit(solution)/shard_map/ppermute | solution.py:266
  57.0 12.9 %collective-permute-start.28 = (bf16[216,128]{1,0:T(8,128)(2,1)S(1)}, bf16[216,128]{1,0:T(8,128)(2,1)S(1)}, u32[]{:S(2)}, u32[]{:S(2)}) collective-permute-start(bf16[216,128]{1,0:T(8,128)(2,1)S(1)} %get-tuple-element.76), channel_id=1, source_target_pairs={{0,6},{2,4},{4,2},{6,0},{1,7},{3,5},{5,3},{7,1},{8,14},{10,12},{12... | collective-permute-start | bytes 165896 | tf_op jit(solution)/shard_map/ppermute | solution.py:266
  59.5 10.5 %collective-permute-start.29 = (bf16[216,128]{1,0:T(8,128)(2,1)S(1)}, bf16[216,128]{1,0:T(8,128)(2,1)S(1)}, u32[]{:S(2)}, u32[]{:S(2)}) collective-permute-start(bf16[216,128]{1,0:T(8,128)(2,1)S(1)} %get-tuple-element.77), channel_id=1, source_target_pairs={{0,4},{2,6},{4,0},{6,2},{1,5},{3,7},{5,1},{7,3},{8,12},{10,14},{12... | collective-permute-start | bytes 165896 | tf_op jit(solution)/shard_map/ppermute | solution.py:266
  67.0 7.1 %collective-permute-start.26 = (bf16[144,384]{1,0:T(8,128)(2,1)S(1)}, bf16[144,384]{1,0:T(8,128)(2,1)S(1)}, u32[]{:S(2)}, u32[]{:S(2)}) collective-permute-start(bf16[144,384]{1,0:T(8,128)(2,1)S(1)} %shard_map.91.refs_0_), channel_id=1, source_target_pairs={{0,16},{8,24},{16,0},{24,8},{1,17},{9,25},{17,1},{25,9},{2,18},{10... | collective-permute-start | bytes 331784 | tf_op jit(solution)/shard_map/ppermute | solution.py:266
  68.5 6.9 %collective-permute-start.27 = (bf16[144,384]{1,0:T(8,128)(2,1)S(1)}, bf16[144,384]{1,0:T(8,128)(2,1)S(1)}, u32[]{:S(2)}, u32[]{:S(2)}) collective-permute-start(bf16[144,384]{1,0:T(8,128)(2,1)S(1)} %shard_map.91.refs_0_), channel_id=1, source_target_pairs={{0,24},{8,16},{16,8},{24,0},{1,25},{9,17},{17,9},{25,1},{2,26},{10... | collective-permute-start | bytes 331784 | tf_op jit(solution)/shard_map/ppermute | solution.py:266
  (12 other events, 59.3 us)

commit v7 on v6

--- a/solution.py
+++ b/solution.py
@@ -326,13 +326,20 @@
         scratch=[((rows, columns), low)],
     )
     backs = [sends[0]] + [over(sends[k], "blk", k) for k in range(groups - 1, 0, -1)]
+    grad_images, grad_captions, token = call(
+        grads_kernel,
+        [(block, low), (block, low), ((8, 128), wide)],
+        *(image_back, image_head, text_back, text_head),
+        behind=sends[:1],
+    )
     count = first[1] // 128
     both = second[1] == 128 and second[0] % (8 * count) == 0 and share % 8 == 0
     pair = [(first, low), (second, low)]
     joint = (share + second[0] // count, first[1])
     kernel = functools.partial(terms_kernel, width, groups, cut)
-    sums, made = [], backs[:1]
-    for i, outs in ((1, pair * (layers - near)), (0, [(first, wide), (second, wide)] + ([(joint, low)] if both else pair))):
+    sums, made = [], [token]
+    farther = [part for k in range(near, layers) for part in ((first, low), (second, wide if both and k % 2 == 0 else low))]
+    for i, outs in ((1, farther), (0, [(first, wide), (second, wide)] + ([(joint, low)] if both else pair))):
         shape = (layers - near if i else near, share, lanes)
         theirs = call(kernel, [(shape, low)], turned[2 + i], *backs, behind=made)[0]
         mine = call(kernel, [(shape, wide)], turned[i], *backs, behind=[theirs])[0]
@@ -340,22 +347,22 @@
         sums.append(call(functools.partial(layers_kernel, cut, both and not i), outs, mine, over_core(theirs)))
     terms, (first_own, second_own, *nearest) = sums
     next_layer = [over(block, "layer", 1) for block in nearest]
-    first_parts, second_parts = (
-        [over(terms[2 * k - 4 + i], "layer", k) for k in range(layers - 1, 1, -1)] for i in (0, 1)
-    )
-    grad_images, grad_captions, token = call(
-        grads_kernel,
-        [(block, low), (block, low), ((8, 128), wide)],
-        *(image_back, image_head, text_back, text_head),
-        behind=[mine],
-    )
+    first_parts = [over(part, "layer", k) for k, part in reversed(list(enumerate(terms[::2], near)))]
+    second_parts = []
+    if both:
+        for k in range(near, layers, 2):
+            passed = over(terms[2 * (k + 1 - near) + 1], "layer", 1)
+            passed = call(sum_kernel, [(second, low)], terms[2 * (k - near) + 1], passed, cost=1)[0]
+            second_parts.append(over(passed, "layer", k))
+    else:
+        second_parts = [over(part, "layer", k) for k, part in reversed(list(enumerate(terms[1::2], near)))]
     if both:
         kernels = [functools.partial(sums_kernel, share, i) for i in (0, 1)]
         next_layer = next_layer * 2
     else:
         kernels = [sum_kernel] * 2
     added = call(add_kernel, [(first, wide)], *first_parts, cost=6)[0]
-    first_sum = call(kernels[0], [(first, low)], first_own, next_layer[0], added, cost=50, behind=[token])[0]
+    first_sum = call(kernels[0], [(first, low)], first_own, next_layer[0], added, cost=50)[0]
     first_sums = over_blk(first_sum)
     second_sum = call(kernels[1], [(second, low)], second_own, next_layer[1], *second_parts, cost=1)[0]
     later_sum = call(own_kernel, [(second, low)], second_sum, behind=first_sums[1:2], cost=1)[0]

time: 78 us -> 76.1 us (0.976)
  waiting for transfers between devices: 21.7 us -> 18 us
  starting transfers between devices: 42.7 us -> 44.6 us
    ppermute x33, waiting for transfers between devices: 21.7 us -> 18 us  [over(): lax.ppermute(array, axis, [(i, i ^ by) for i in range(lax.axis_size(axis))])]
    ppermute x33, starting transfers between devices: 42.7 us -> 44.6 us  [over(): lax.ppermute(array, axis, [(i, i ^ by) for i in range(lax.axis_size(axis))])]
    pallas_call x21 -> x22, Pallas kernels: 11.7 us -> 11.7 us  [call(): pl.pallas_call(body, out_shape=tuple((jax.ShapeDtypeStruct(shape, kind) f...]
  transfers between devices with their start and end apart: 33 -> 33, of which waited for: 13 -> 14; matrix products, arithmetic and copies ran while one was open for 0% -> 0% of each run, Pallas kernels for 12% -> 13%
where the time goes in v7:
time: 76.1 us; the launch traced here: 76 us
  starting transfers between devices  44.6 us (59%)
  waiting for transfers between devices  18 us (24%)
  Pallas kernels  11.7 us (15%)
  local copies, waits for them, and re-layouts  0.92 us (1%)
  between operations  0.82 us (1%)
    ppermute x33, starting transfers between devices, over(): lax.ppermute(array, axis, [(i, i ^ by) for i in range(lax.axis_size(axis))])  44.6 us
    ppermute x33, waiting for transfers between devices, over(): lax.ppermute(array, axis, [(i, i ^ by) for i in range(lax.axis_size(axis))])  18 us
    pallas_call x22, Pallas kernels, call(): pl.pallas_call(body, out_shape=tuple((jax.ShapeDtypeStruct(shape, kind) f...  11.7 us
  transfers between devices with their start and end apart: 33, of which 14 were waited for; matrix products, arithmetic and copies ran while one was open for 0% of the time, Pallas kernels for 13%

profile of v7, /device:TPU:0, one launch (start us, length us, event | category | flops | bytes accessed | tf_op | source)
XLA Modules:
  0.0 76.0 jit_solution(7146039997516265365)
XLA Ops:
  0.6 3.0 %collective-permute-start = (bf16[64,1152]{1,0:T(8,128)(2,1)}, bf16[64,1152]{1,0:T(8,128)(2,1)S(1)}, u32[]{:S(2)}, u32[]{:S(2)}) collective-permute-start(bf16[64,1152]{1,0:T(8,128)(2,1)} %refs_1_.3), channel_id=1, source_target_pairs={{0,8},{8,0},{16,24},{24,16},{1,9},{9,1},{17,25},{25,17},{2,10},{10... | collective-permute-start | bytes 442376 | tf_op jit(solution)/shard_map/ppermute | solution.py:266
  3.6 1.5 %collective-permute-start.1 = (bf16[64,1152]{1,0:T(8,128)(2,1)}, bf16[64,1152]{1,0:T(8,128)(2,1)S(1)}, u32[]{:S(2)}, u32[]{:S(2)}) collective-permute-start(bf16[64,1152]{1,0:T(8,128)(2,1)} %refs_1_.3), channel_id=1, source_target_pairs={{0,16},{8,24},{16,0},{24,8},{1,17},{9,25},{17,1},{25,9},{2,18},{10... | collective-permute-start | bytes 442376 | tf_op jit(solution)/shard_map/ppermute | solution.py:266
  5.2 2.0 %collective-permute-start.3 = (bf16[64,1152]{1,0:T(8,128)(2,1)}, bf16[64,1152]{1,0:T(8,128)(2,1)S(1)}, u32[]{:S(2)}, u32[]{:S(2)}) collective-permute-start(bf16[64,1152]{1,0:T(8,128)(2,1)} %refs_0_.2), channel_id=1, source_target_pairs={{0,2},{2,0},{4,6},{6,4},{1,3},{3,1},{5,7},{7,5},{8,10},{10,8},{12,... | collective-permute-start | bytes 442376 | tf_op jit(solution)/shard_map/ppermute | solution.py:266
  7.2 2.6 %collective-permute-start.4 = (bf16[64,1152]{1,0:T(8,128)(2,1)}, bf16[64,1152]{1,0:T(8,128)(2,1)S(1)}, u32[]{:S(2)}, u32[]{:S(2)}) collective-permute-start(bf16[64,1152]{1,0:T(8,128)(2,1)} %refs_0_.2), channel_id=1, source_target_pairs={{0,4},{2,6},{4,0},{6,2},{1,5},{3,7},{5,1},{7,3},{8,12},{10,14},{12... | collective-permute-start | bytes 442376 | tf_op jit(solution)/shard_map/ppermute | solution.py:266
  13.5 1.9 %collective-permute-start.7 = (bf16[64,1152]{1,0:T(8,128)(2,1)S(1)}, bf16[64,1152]{1,0:T(8,128)(2,1)S(1)}, u32[]{:S(2)}, u32[]{:S(2)}) collective-permute-start(bf16[64,1152]{1,0:T(8,128)(2,1)S(1)} %get-tuple-element.44.refs_0_.refs_2_), channel_id=1, source_target_pairs={{0,8},{8,0},{16,24},{24,16},{1,9},{9,1},{17,25},{25,17},{2,10},{10... | collective-permute-start | bytes 442376 | tf_op jit(solution)/shard_map/ppermute | solution.py:266
  15.4 1.5 %collective-permute-start.8 = (bf16[64,1152]{1,0:T(8,128)(2,1)S(1)}, bf16[64,1152]{1,0:T(8,128)(2,1)S(1)}, u32[]{:S(2)}, u32[]{:S(2)}) collective-permute-start(bf16[64,1152]{1,0:T(8,128)(2,1)S(1)} %get-tuple-element.44.refs_0_.refs_2_), channel_id=1, source_target_pairs={{0,16},{8,24},{16,0},{24,8},{1,17},{9,25},{17,1},{25,9},{2,18},{10... | collective-permute-start | bytes 442376 | tf_op jit(solution)/shard_map/ppermute | solution.py:266
  17.0 3.3 %collective-permute-done.4.refs_2_ = bf16[64,1152]{1,0:T(8,128)(2,1)S(1)} collective-permute-done((bf16[64,1152]{1,0:T(8,128)(2,1)}, bf16[64,1152]{1,0:T(8,128)(2,1)S(1)}, u32[]{:S(2)}, u32[]{:S(2)}) %collective-permute-start.4) | collective-permute-done | bytes 147488 | tf_op jit(solution)/shard_map/ppermute | solution.py:266
  24.0 1.7 %collective-permute-start.11 = (bf16[64,1152]{1,0:T(8,128)(2,1)S(1)}, bf16[64,1152]{1,0:T(8,128)(2,1)S(1)}, u32[]{:S(2)}, u32[]{:S(2)}) collective-permute-start(bf16[64,1152]{1,0:T(8,128)(2,1)S(1)} %shard_map.81), channel_id=1, source_target_pairs={{0,2},{2,0},{4,6},{6,4},{1,3},{3,1},{5,7},{7,5},{8,10},{10,8},{12,... | collective-permute-start | bytes 442376 | tf_op jit(solution)/shard_map/ppermute | solution.py:266
  25.6 1.9 %collective-permute-start.12 = (bf16[64,1152]{1,0:T(8,128)(2,1)S(1)}, bf16[64,1152]{1,0:T(8,128)(2,1)S(1)}, u32[]{:S(2)}, u32[]{:S(2)}) collective-permute-start(bf16[64,1152]{1,0:T(8,128)(2,1)S(1)} %get-tuple-element.52), channel_id=1, source_target_pairs={{0,4},{2,6},{4,0},{6,2},{1,5},{3,7},{5,1},{7,3},{8,12},{10,14},{12... | collective-permute-start | bytes 442376 | tf_op jit(solution)/shard_map/ppermute | solution.py:266
  28.5 1.6 %collective-permute-start.14 = (bf16[64,1152]{1,0:T(8,128)(2,1)S(1)}, bf16[64,1152]{1,0:T(8,128)(2,1)S(1)}, u32[]{:S(2)}, u32[]{:S(2)}) collective-permute-start(bf16[64,1152]{1,0:T(8,128)(2,1)S(1)} %get-tuple-element.49.refs_10_), channel_id=1, source_target_pairs={{0,8},{8,0},{16,24},{24,16},{1,9},{9,1},{17,25},{25,17},{2,10},{10... | collective-permute-start | bytes 442376 | tf_op jit(solution)/shard_map/ppermute | solution.py:266
  30.1 1.5 %collective-permute-start.15 = (bf16[64,1152]{1,0:T(8,128)(2,1)S(1)}, bf16[64,1152]{1,0:T(8,128)(2,1)S(1)}, u32[]{:S(2)}, u32[]{:S(2)}) collective-permute-start(bf16[64,1152]{1,0:T(8,128)(2,1)S(1)} %get-tuple-element.56), channel_id=1, source_target_pairs={{0,16},{8,24},{16,0},{24,8},{1,17},{9,25},{17,1},{25,9},{2,18},{10... | collective-permute-start | bytes 442376 | tf_op jit(solution)/shard_map/ppermute | solution.py:266
  32.9 2.5 %collective-permute-start.16 = (bf16[64,1152]{1,0:T(8,128)(2,1)S(1)}, bf16[64,1152]{1,0:T(8,128)(2,1)S(1)}, u32[]{:S(2)}, u32[]{:S(2)}) collective-permute-start(bf16[64,1152]{1,0:T(8,128)(2,1)S(1)} %get-tuple-element.57), channel_id=1, source_target_pairs={{0,24},{8,16},{16,8},{24,0},{1,25},{9,17},{17,9},{25,1},{2,26},{10... | collective-permute-start | bytes 442376 | tf_op jit(solution)/shard_map/ppermute | solution.py:266
  36.5 3.1 %collective-permute-done.12.refs_3_ = bf16[64,1152]{1,0:T(8,128)(2,1)S(1)} collective-permute-done((bf16[64,1152]{1,0:T(8,128)(2,1)S(1)}, bf16[64,1152]{1,0:T(8,128)(2,1)S(1)}, u32[]{:S(2)}, u32[]{:S(2)}) %collective-permute-start.12) | collective-permute-done | bytes 147488 | tf_op jit(solution)/shard_map/ppermute | solution.py:266
  40.0 2.5 %collective-permute-start.17 = (bf16[64,640]{1,0:T(8,128)(2,1)S(1)}, bf16[64,640]{1,0:T(8,128)(2,1)S(1)}, u32[]{:S(2)}, u32[]{:S(2)}) collective-permute-start(bf16[64,640]{1,0:T(8,128)(2,1)S(1)} %get-tuple-element.64), channel_id=1, source_target_pairs={{0,24},{8,16},{16,8},{24,0},{1,25},{9,17},{17,9},{25,1},{2,26},{10... | collective-permute-start | bytes 245768 | tf_op jit(solution)/shard_map/ppermute | solution.py:266
  43.6 2.4 %shard_map.83 = (bf16[64,1152]{1,0:T(8,128)(2,1)}, bf16[64,1152]{1,0:T(8,128)(2,1)}, f32[8,128]{1,0:T(8,128)S(1)}) custom-call(bf16[64,1152]{1,0:T(8,128)(2,1)S(1)} %get-tuple-element.58.refs_0_, bf16[1152,1152]{1,0:T(8,128)(2,1)S(1)} %copy-done.1, bf16[64,1152]{1,0:T(8,128)(2,1)S(1)} %get-tuple-element.59.refs_2_, bf16[1152,1152]{1,0:T(8,128)(2,1)S(1)} %copy-done, ...), custom_call_target="tpu_custom_call" | custom-call | flops 1000000000 | bytes 1000000000 | tf_op jit(solution)/shard_map/pallas_call | solution.py:44
  49.9 2.5 %collective-permute-start.23 = (bf16[144,384]{1,0:T(8,128)(2,1)S(1)}, bf16[144,384]{1,0:T(8,128)(2,1)S(1)}, u32[]{:S(2)}, u32[]{:S(2)}) collective-permute-start(bf16[144,384]{1,0:T(8,128)(2,1)S(1)} %get-tuple-element.73), channel_id=1, source_target_pairs={{0,6},{2,4},{4,2},{6,0},{1,7},{3,5},{5,3},{7,1},{8,14},{10,12},{12... | collective-permute-start | bytes 331784 | tf_op jit(solution)/shard_map/ppermute | solution.py:266
  52.4 2.0 %collective-permute-start.24 = (bf16[144,384]{1,0:T(8,128)(2,1)S(1)}, bf16[144,384]{1,0:T(8,128)(2,1)S(1)}, u32[]{:S(2)}, u32[]{:S(2)}) collective-permute-start(bf16[144,384]{1,0:T(8,128)(2,1)S(1)} %get-tuple-element.74), channel_id=1, source_target_pairs={{0,4},{2,6},{4,0},{6,2},{1,5},{3,7},{5,1},{7,3},{8,12},{10,14},{12... | collective-permute-start | bytes 331784 | tf_op jit(solution)/shard_map/ppermute | solution.py:266
  54.5 2.0 %collective-permute-start.21 = (bf16[216,384]{1,0:T(8,128)(2,1)S(1)}, bf16[216,384]{1,0:T(8,128)(2,1)S(1)}, u32[]{:S(2)}, u32[]{:S(2)}) collective-permute-start(bf16[216,384]{1,0:T(8,128)(2,1)S(1)} %get-tuple-element.71), channel_id=1, source_target_pairs={{0,2},{2,0},{4,6},{6,4},{1,3},{3,1},{5,7},{7,5},{8,10},{10,8},{12,... | collective-permute-start | bytes 497672 | tf_op jit(solution)/shard_map/ppermute | solution.py:266
  56.5 2.7 %collective-permute-done.28.refs_1_ = bf16[216,128]{1,0:T(8,128)(2,1)S(1)} collective-permute-done((bf16[216,128]{1,0:T(8,128)(2,1)S(1)}, bf16[216,128]{1,0:T(8,128)(2,1)S(1)}, u32[]{:S(2)}, u32[]{:S(2)}) %collective-permute-start.28) | collective-permute-done | bytes 55328 | tf_op jit(solution)/shard_map/ppermute | solution.py:266
  59.2 3.4 %collective-permute-start.29 = (bf16[216,128]{1,0:T(8,128)(2,1)S(1)}, bf16[216,128]{1,0:T(8,128)(2,1)S(1)}, u32[]{:S(2)}, u32[]{:S(2)}) collective-permute-start(bf16[216,128]{1,0:T(8,128)(2,1)S(1)} %shard_map.92), channel_id=1, source_target_pairs={{0,4},{2,6},{4,0},{6,2},{1,5},{3,7},{5,1},{7,3},{8,12},{10,14},{12... | collective-permute-start | bytes 165896 | tf_op jit(solution)/shard_map/ppermute | solution.py:266
  62.6 1.8 %collective-permute-done.24.refs_1_ = bf16[144,384]{1,0:T(8,128)(2,1)S(1)} collective-permute-done((bf16[144,384]{1,0:T(8,128)(2,1)S(1)}, bf16[144,384]{1,0:T(8,128)(2,1)S(1)}, u32[]{:S(2)}, u32[]{:S(2)}) %collective-permute-start.24) | collective-permute-done | bytes 110624 | tf_op jit(solution)/shard_map/ppermute | solution.py:266
  65.0 1.6 %collective-permute-start.26 = (bf16[144,384]{1,0:T(8,128)(2,1)S(1)}, bf16[144,384]{1,0:T(8,128)(2,1)S(1)}, u32[]{:S(2)}, u32[]{:S(2)}) collective-permute-start(bf16[144,384]{1,0:T(8,128)(2,1)S(1)} %shard_map.91.refs_0_), channel_id=1, source_target_pairs={{0,16},{8,24},{16,0},{24,8},{1,17},{9,25},{17,1},{25,9},{2,18},{10... | collective-permute-start | bytes 331784 | tf_op jit(solution)/shard_map/ppermute | solution.py:266
  66.7 1.4 %collective-permute-start.27 = (bf16[144,384]{1,0:T(8,128)(2,1)S(1)}, bf16[144,384]{1,0:T(8,128)(2,1)S(1)}, u32[]{:S(2)}, u32[]{:S(2)}) collective-permute-start(bf16[144,384]{1,0:T(8,128)(2,1)S(1)} %shard_map.91.refs_0_), channel_id=1, source_target_pairs={{0,24},{8,16},{16,8},{24,0},{1,25},{9,17},{17,9},{25,1},{2,26},{10... | collective-permute-start | bytes 331784 | tf_op jit(solution)/shard_map/ppermute | solution.py:266
  68.1 1.6 %collective-permute-start.31 = (bf16[216,128]{1,0:T(8,128)(2,1)S(1)}, bf16[216,128]{1,0:T(8,128)(2,1)S(1)}, u32[]{:S(2)}, u32[]{:S(2)}) collective-permute-start(bf16[216,128]{1,0:T(8,128)(2,1)S(1)} %shard_map.93.refs_0_.refs_4_), channel_id=1, source_target_pairs={{0,16},{8,24},{16,0},{24,8},{1,17},{9,25},{17,1},{25,9},{2,18},{10... | collective-permute-start | bytes 165896 | tf_op jit(solution)/shard_map/ppermute | solution.py:266
  (70 shorter events, 23.1 us)
Async XLA Ops:
  0.6 11.0 %collective-permute-start = (bf16[64,1152]{1,0:T(8,128)(2,1)}, bf16[64,1152]{1,0:T(8,128)(2,1)S(1)}, u32[]{:S(2)}, u32[]{:S(2)}) collective-permute-start(bf16[64,1152]{1,0:T(8,128)(2,1)} %refs_1_.3), channel_id=1, source_target_pairs={{0,8},{8,0},{16,24},{24,16},{1,9},{9,1},{17,25},{25,17},{2,10},{10... | collective-permute-start | bytes 442376 | tf_op jit(solution)/shard_map/ppermute | solution.py:266
  3.6 8.7 %collective-permute-start.1 = (bf16[64,1152]{1,0:T(8,128)(2,1)}, bf16[64,1152]{1,0:T(8,128)(2,1)S(1)}, u32[]{:S(2)}, u32[]{:S(2)}) collective-permute-start(bf16[64,1152]{1,0:T(8,128)(2,1)} %refs_1_.3), channel_id=1, source_target_pairs={{0,16},{8,24},{16,0},{24,8},{1,17},{9,25},{17,1},{25,9},{2,18},{10... | collective-permute-start | bytes 442376 | tf_op jit(solution)/shard_map/ppermute | solution.py:266
  5.2 7.2 %collective-permute-start.2 = (bf16[64,1152]{1,0:T(8,128)(2,1)}, bf16[64,1152]{1,0:T(8,128)(2,1)S(1)}, u32[]{:S(2)}, u32[]{:S(2)}) collective-permute-start(bf16[64,1152]{1,0:T(8,128)(2,1)} %refs_1_.3), channel_id=1, source_target_pairs={{0,24},{8,16},{16,8},{24,0},{1,25},{9,17},{17,9},{25,1},{2,26},{10... | collective-permute-start | bytes 442376 | tf_op jit(solution)/shard_map/ppermute | solution.py:266
  5.2 11.7 %collective-permute-start.3 = (bf16[64,1152]{1,0:T(8,128)(2,1)}, bf16[64,1152]{1,0:T(8,128)(2,1)S(1)}, u32[]{:S(2)}, u32[]{:S(2)}) collective-permute-start(bf16[64,1152]{1,0:T(8,128)(2,1)} %refs_0_.2), channel_id=1, source_target_pairs={{0,2},{2,0},{4,6},{6,4},{1,3},{3,1},{5,7},{7,5},{8,10},{10,8},{12,... | collective-permute-start | bytes 442376 | tf_op jit(solution)/shard_map/ppermute | solution.py:266
  7.2 13.1 %collective-permute-start.4 = (bf16[64,1152]{1,0:T(8,128)(2,1)}, bf16[64,1152]{1,0:T(8,128)(2,1)S(1)}, u32[]{:S(2)}, u32[]{:S(2)}) collective-permute-start(bf16[64,1152]{1,0:T(8,128)(2,1)} %refs_0_.2), channel_id=1, source_target_pairs={{0,4},{2,6},{4,0},{6,2},{1,5},{3,7},{5,1},{7,3},{8,12},{10,14},{12... | collective-permute-start | bytes 442376 | tf_op jit(solution)/shard_map/ppermute | solution.py:266
  11.7 8.7 %collective-permute-start.5 = (bf16[64,1152]{1,0:T(8,128)(2,1)}, bf16[64,1152]{1,0:T(8,128)(2,1)S(1)}, u32[]{:S(2)}, u32[]{:S(2)}) collective-permute-start(bf16[64,1152]{1,0:T(8,128)(2,1)} %refs_0_.2), channel_id=1, source_target_pairs={{0,6},{2,4},{4,2},{6,0},{1,7},{3,5},{5,3},{7,1},{8,14},{10,12},{12... | collective-permute-start | bytes 442376 | tf_op jit(solution)/shard_map/ppermute | solution.py:266
  13.5 10.5 %collective-permute-start.7 = (bf16[64,1152]{1,0:T(8,128)(2,1)S(1)}, bf16[64,1152]{1,0:T(8,128)(2,1)S(1)}, u32[]{:S(2)}, u32[]{:S(2)}) collective-permute-start(bf16[64,1152]{1,0:T(8,128)(2,1)S(1)} %get-tuple-element.44.refs_0_.refs_2_), channel_id=1, source_target_pairs={{0,8},{8,0},{16,24},{24,16},{1,9},{9,1},{17,25},{25,17},{2,10},{10... | collective-permute-start | bytes 442376 | tf_op jit(solution)/shard_map/ppermute | solution.py:266
  15.4 8.5 %collective-permute-start.8 = (bf16[64,1152]{1,0:T(8,128)(2,1)S(1)}, bf16[64,1152]{1,0:T(8,128)(2,1)S(1)}, u32[]{:S(2)}, u32[]{:S(2)}) collective-permute-start(bf16[64,1152]{1,0:T(8,128)(2,1)S(1)} %get-tuple-element.44.refs_0_.refs_2_), channel_id=1, source_target_pairs={{0,16},{8,24},{16,0},{24,8},{1,17},{9,25},{17,1},{25,9},{2,18},{10... | collective-permute-start | bytes 442376 | tf_op jit(solution)/shard_map/ppermute | solution.py:266
  16.9 7.0 %collective-permute-start.9 = (bf16[64,1152]{1,0:T(8,128)(2,1)S(1)}, bf16[64,1152]{1,0:T(8,128)(2,1)S(1)}, u32[]{:S(2)}, u32[]{:S(2)}) collective-permute-start(bf16[64,1152]{1,0:T(8,128)(2,1)S(1)} %get-tuple-element.44.refs_0_.refs_2_), channel_id=1, source_target_pairs={{0,24},{8,16},{16,8},{24,0},{1,25},{9,17},{17,9},{25,1},{2,26},{10... | collective-permute-start | bytes 442376 | tf_op jit(solution)/shard_map/ppermute | solution.py:266
  24.0 8.9 %collective-permute-start.11 = (bf16[64,1152]{1,0:T(8,128)(2,1)S(1)}, bf16[64,1152]{1,0:T(8,128)(2,1)S(1)}, u32[]{:S(2)}, u32[]{:S(2)}) collective-permute-start(bf16[64,1152]{1,0:T(8,128)(2,1)S(1)} %shard_map.81), channel_id=1, source_target_pairs={{0,2},{2,0},{4,6},{6,4},{1,3},{3,1},{5,7},{7,5},{8,10},{10,8},{12,... | collective-permute-start | bytes 442376 | tf_op jit(solution)/shard_map/ppermute | solution.py:266
  25.6 13.9 %collective-permute-start.12 = (bf16[64,1152]{1,0:T(8,128)(2,1)S(1)}, bf16[64,1152]{1,0:T(8,128)(2,1)S(1)}, u32[]{:S(2)}, u32[]{:S(2)}) collective-permute-start(bf16[64,1152]{1,0:T(8,128)(2,1)S(1)} %get-tuple-element.52), channel_id=1, source_target_pairs={{0,4},{2,6},{4,0},{6,2},{1,5},{3,7},{5,1},{7,3},{8,12},{10,14},{12... | collective-permute-start | bytes 442376 | tf_op jit(solution)/shard_map/ppermute | solution.py:266
  27.5 12.1 %collective-permute-start.13 = (bf16[64,1152]{1,0:T(8,128)(2,1)S(1)}, bf16[64,1152]{1,0:T(8,128)(2,1)S(1)}, u32[]{:S(2)}, u32[]{:S(2)}) collective-permute-start(bf16[64,1152]{1,0:T(8,128)(2,1)S(1)} %get-tuple-element.53), channel_id=1, source_target_pairs={{0,6},{2,4},{4,2},{6,0},{1,7},{3,5},{5,3},{7,1},{8,14},{10,12},{12... | collective-permute-start | bytes 442376 | tf_op jit(solution)/shard_map/ppermute | solution.py:266
  28.5 11.0 %collective-permute-start.14 = (bf16[64,1152]{1,0:T(8,128)(2,1)S(1)}, bf16[64,1152]{1,0:T(8,128)(2,1)S(1)}, u32[]{:S(2)}, u32[]{:S(2)}) collective-permute-start(bf16[64,1152]{1,0:T(8,128)(2,1)S(1)} %get-tuple-element.49.refs_10_), channel_id=1, source_target_pairs={{0,8},{8,0},{16,24},{24,16},{1,9},{9,1},{17,25},{25,17},{2,10},{10... | collective-permute-start | bytes 442376 | tf_op jit(solution)/shard_map/ppermute | solution.py:266
  30.1 9.5 %collective-permute-start.15 = (bf16[64,1152]{1,0:T(8,128)(2,1)S(1)}, bf16[64,1152]{1,0:T(8,128)(2,1)S(1)}, u32[]{:S(2)}, u32[]{:S(2)}) collective-permute-start(bf16[64,1152]{1,0:T(8,128)(2,1)S(1)} %get-tuple-element.56), channel_id=1, source_target_pairs={{0,16},{8,24},{16,0},{24,8},{1,17},{9,25},{17,1},{25,9},{2,18},{10... | collective-permute-start | bytes 442376 | tf_op jit(solution)/shard_map/ppermute | solution.py:266
  32.9 6.7 %collective-permute-start.16 = (bf16[64,1152]{1,0:T(8,128)(2,1)S(1)}, bf16[64,1152]{1,0:T(8,128)(2,1)S(1)}, u32[]{:S(2)}, u32[]{:S(2)}) collective-permute-start(bf16[64,1152]{1,0:T(8,128)(2,1)S(1)} %get-tuple-element.57), channel_id=1, source_target_pairs={{0,24},{8,16},{16,8},{24,0},{1,25},{9,17},{17,9},{25,1},{2,26},{10... | collective-permute-start | bytes 442376 | tf_op jit(solution)/shard_map/ppermute | solution.py:266
  40.0 6.0 %collective-permute-start.17 = (bf16[64,640]{1,0:T(8,128)(2,1)S(1)}, bf16[64,640]{1,0:T(8,128)(2,1)S(1)}, u32[]{:S(2)}, u32[]{:S(2)}) collective-permute-start(bf16[64,640]{1,0:T(8,128)(2,1)S(1)} %get-tuple-element.64), channel_id=1, source_target_pairs={{0,24},{8,16},{16,8},{24,0},{1,25},{9,17},{17,9},{25,1},{2,26},{10... | collective-permute-start | bytes 245768 | tf_op jit(solution)/shard_map/ppermute | solution.py:266
  48.4 6.1 %collective-permute-start.20 = (bf16[2,144,640]{2,1,0:T(8,128)(2,1)S(1)}, bf16[2,144,640]{2,1,0:T(8,128)(2,1)S(1)}, u32[]{:S(2)}, u32[]{:S(2)}) collective-permute-start(bf16[2,144,640]{2,1,0:T(8,128)(2,1)S(1)} %shard_map.85.refs_5_), channel_id=1, source_target_pairs={{0,1},{1,0},{2,3},{3,2},{4,5},{5,4},{6,7},{7,6},{8,9},{9,8},{10,11... | collective-permute-start | bytes 1105928 | tf_op jit(solution)/shard_map/ppermute | solution.py:266
  49.9 12.7 %collective-permute-start.23 = (bf16[144,384]{1,0:T(8,128)(2,1)S(1)}, bf16[144,384]{1,0:T(8,128)(2,1)S(1)}, u32[]{:S(2)}, u32[]{:S(2)}) collective-permute-start(bf16[144,384]{1,0:T(8,128)(2,1)S(1)} %get-tuple-element.73), channel_id=1, source_target_pairs={{0,6},{2,4},{4,2},{6,0},{1,7},{3,5},{5,3},{7,1},{8,14},{10,12},{12... | collective-permute-start | bytes 331784 | tf_op jit(solution)/shard_map/ppermute | solution.py:266
  52.4 12.1 %collective-permute-start.24 = (bf16[144,384]{1,0:T(8,128)(2,1)S(1)}, bf16[144,384]{1,0:T(8,128)(2,1)S(1)}, u32[]{:S(2)}, u32[]{:S(2)}) collective-permute-start(bf16[144,384]{1,0:T(8,128)(2,1)S(1)} %get-tuple-element.74), channel_id=1, source_target_pairs={{0,4},{2,6},{4,0},{6,2},{1,5},{3,7},{5,1},{7,3},{8,12},{10,14},{12... | collective-permute-start | bytes 331784 | tf_op jit(solution)/shard_map/ppermute | solution.py:266
  54.5 9.9 %collective-permute-start.21 = (bf16[216,384]{1,0:T(8,128)(2,1)S(1)}, bf16[216,384]{1,0:T(8,128)(2,1)S(1)}, u32[]{:S(2)}, u32[]{:S(2)}) collective-permute-start(bf16[216,384]{1,0:T(8,128)(2,1)S(1)} %get-tuple-element.71), channel_id=1, source_target_pairs={{0,2},{2,0},{4,6},{6,4},{1,3},{3,1},{5,7},{7,5},{8,10},{10,8},{12,... | collective-permute-start | bytes 497672 | tf_op jit(solution)/shard_map/ppermute | solution.py:266
  59.2 8.9 %collective-permute-start.29 = (bf16[216,128]{1,0:T(8,128)(2,1)S(1)}, bf16[216,128]{1,0:T(8,128)(2,1)S(1)}, u32[]{:S(2)}, u32[]{:S(2)}) collective-permute-start(bf16[216,128]{1,0:T(8,128)(2,1)S(1)} %shard_map.92), channel_id=1, source_target_pairs={{0,4},{2,6},{4,0},{6,2},{1,5},{3,7},{5,1},{7,3},{8,12},{10,14},{12... | collective-permute-start | bytes 165896 | tf_op jit(solution)/shard_map/ppermute | solution.py:266
  64.5 5.9 %collective-permute-start.25 = (bf16[144,384]{1,0:T(8,128)(2,1)S(1)}, bf16[144,384]{1,0:T(8,128)(2,1)S(1)}, u32[]{:S(2)}, u32[]{:S(2)}) collective-permute-start(bf16[144,384]{1,0:T(8,128)(2,1)S(1)} %shard_map.91.refs_0_), channel_id=1, source_target_pairs={{0,8},{8,0},{16,24},{24,16},{1,9},{9,1},{17,25},{25,17},{2,10},{10... | collective-permute-start | bytes 331784 | tf_op jit(solution)/shard_map/ppermute | solution.py:266
  65.0 7.2 %collective-permute-start.26 = (bf16[144,384]{1,0:T(8,128)(2,1)S(1)}, bf16[144,384]{1,0:T(8,128)(2,1)S(1)}, u32[]{:S(2)}, u32[]{:S(2)}) collective-permute-start(bf16[144,384]{1,0:T(8,128)(2,1)S(1)} %shard_map.91.refs_0_), channel_id=1, source_target_pairs={{0,16},{8,24},{16,0},{24,8},{1,17},{9,25},{17,1},{25,9},{2,18},{10... | collective-permute-start | bytes 331784 | tf_op jit(solution)/shard_map/ppermute | solution.py:266
  66.7 6.8 %collective-permute-start.27 = (bf16[144,384]{1,0:T(8,128)(2,1)S(1)}, bf16[144,384]{1,0:T(8,128)(2,1)S(1)}, u32[]{:S(2)}, u32[]{:S(2)}) collective-permute-start(bf16[144,384]{1,0:T(8,128)(2,1)S(1)} %shard_map.91.refs_0_), channel_id=1, source_target_pairs={{0,24},{8,16},{16,8},{24,0},{1,25},{9,17},{17,9},{25,1},{2,26},{10... | collective-permute-start | bytes 331784 | tf_op jit(solution)/shard_map/ppermute | solution.py:266
  (12 other events, 58.1 us)

commit v8 on v7

--- a/solution.py
+++ b/solution.py
@@ -32,7 +32,7 @@
     return (before * inverse, inverse)
 
 
-def call(kernel, outs, *arrays, cost=1, scratch=(), behind=()):
+def call(kernel, outs, *arrays, cost=1, scratch=(), behind=(), copies=0):
     specs = [pl.BlockSpec(memory_space=pltpu.VMEM)] * len(arrays)
     count = len(arrays)
     shapes = [shape for shape, _ in (*outs, *scratch)] + [array.shape for array in arrays]
@@ -45,8 +45,9 @@
         body,
         out_shape=tuple(jax.ShapeDtypeStruct(shape, kind) for shape, kind in outs),
         in_specs=specs + [pl.BlockSpec(memory_space=pl.ANY)] * len(behind),
-        out_specs=(pl.BlockSpec(memory_space=pltpu.VMEM),) * len(outs),
-        scratch_shapes=[pltpu.VMEM(shape, kind) for shape, kind in scratch],
+        out_specs=(pl.BlockSpec(memory_space=pl.ANY if copies else pltpu.VMEM),) * len(outs),
+        scratch_shapes=[pltpu.VMEM(shape, kind) for shape, kind in scratch]
+        + [pltpu.SemaphoreType.DMA((copies,))] * (copies > 0),
         compiler_params=pltpu.CompilerParams(vmem_limit_bytes=min(48 * 2**20, 4 * 2**20 + held)),
         cost_estimate=pl.CostEstimate(flops=cost * cost_unit, bytes_accessed=cost * cost_unit, transcendentals=0),
     )(*arrays, *behind)
@@ -238,21 +239,33 @@
 
 
 def heads_kernel(groups, cut, *refs):
-    *block_refs, image_ref, text_ref, all_ref = refs
+    *block_refs, image_ref, text_ref, all_ref, sems = refs
     (share, width), (_, lanes), (own, parts) = image_ref.shape, block_refs[0].shape, (cut[0] * 128, cut[1])
-    for k in range(groups):
-        blk = k ^ lax.axis_index("blk")
-        start = pl.multiple_of(blk * own, 128)
-        first, second = (block_refs[i * groups + k][...].astype(wide) for i in (0, 1))
-        all_ref[:, pl.ds(start, lanes)] = first
-        all_ref[:, pl.ds(start + lanes, own - lanes)] = second[:share]
-        if parts:
-            part = share // parts
-            row = pl.multiple_of(blk % parts * part, 8)
-            column = pl.multiple_of(extra_chunk(cut, groups, blk) * 128, 128)
-            all_ref[pl.ds(row, part), pl.ds(column, 128)] = second[share:]
-    image_ref[...] = all_ref[:, :width]
-    text_ref[...] = all_ref[:, width : 2 * width]
+    steps = parts or 1
+    part = share // steps
+    copies = []
+    for step in range(steps):
+        at = slice(step * part, (step + 1) * part)
+        for k in range(groups):
+            blk = k ^ lax.axis_index("blk")
+            start = pl.multiple_of(blk * own, 128)
+            first, second = (block_refs[i * groups + k][...].astype(wide) for i in (0, 1))
+            all_ref[at, pl.ds(start, lanes)] = first[at]
+            all_ref[at, pl.ds(start + lanes, own - lanes)] = second[at]
+            if parts:
+                column = pl.multiple_of(extra_chunk(cut, groups, blk) * 128, 128)
+
+                @pl.when(blk % parts == step)
+                def _():
+                    all_ref[at, pl.ds(column, 128)] = second[share:]
+
+        for i, ref in enumerate((image_ref, text_ref)):
+            copies.append(
+                pltpu.make_async_copy(all_ref.at[at, i * width : (i + 1) * width], ref.at[at], sems.at[len(copies)])
+            )
+            copies[-1].start()
+    for copy in copies:
+        copy.wait()
 
 
 def per_device(images, captions, image_head, text_head):
@@ -342,7 +355,7 @@
     for i, outs in ((1, farther), (0, [(first, wide), (second, wide)] + ([(joint, low)] if both else pair))):
         shape = (layers - near if i else near, share, lanes)
         theirs = call(kernel, [(shape, low)], turned[2 + i], *backs, behind=made)[0]
-        mine = call(kernel, [(shape, wide)], turned[i], *backs, behind=[theirs])[0]
+        mine = call(kernel, [(shape, wide)], turned[i], *backs, behind=[theirs, *sums[0][:1]] if sums else [theirs])[0]
         made = [theirs]
         sums.append(call(functools.partial(layers_kernel, cut, both and not i), outs, mine, over_core(theirs)))
     terms, (first_own, second_own, *nearest) = sums
@@ -375,6 +388,7 @@
         [((share, width), wide)] * 2,
         *blocks,
         scratch=[((share, columns), wide)],
+        copies=2 * max(parts, 1),
         behind=[token],
     )
     return (grad_images, grad_captions, grad_image_head, grad_text_head)

time: 76.1 us -> 76 us (level)
  transfers between devices with their start and end apart: 33 -> 33, of which waited for: 14 -> 15; matrix products, arithmetic and copies ran while one was open for 0% -> 0% of each run, Pallas kernels for 13% -> 13%
where the time goes in v8:
time: 76 us; the launch traced here: 75.9 us
  starting transfers between devices  44.5 us (59%)
  waiting for transfers between devices  18 us (24%)
  Pallas kernels  11.7 us (15%)
  local copies, waits for them, and re-layouts  0.92 us (1%)
  between operations  0.81 us (1%)
    ppermute x33, starting transfers between devices, over(): lax.ppermute(array, axis, [(i, i ^ by) for i in range(lax.axis_size(axis))])  44.5 us
    ppermute x33, waiting for transfers between devices, over(): lax.ppermute(array, axis, [(i, i ^ by) for i in range(lax.axis_size(axis))])  18 us
    pallas_call x22, Pallas kernels, call(): pl.pallas_call(body, out_shape=tuple((jax.ShapeDtypeStruct(shape, kind) f...  11.7 us
  transfers between devices with their start and end apart: 33, of which 15 were waited for; matrix products, arithmetic and copies ran while one was open for 0% of the time, Pallas kernels for 13%

profile of v8, /device:TPU:0, one launch (start us, length us, event | category | flops | bytes accessed | tf_op | source)
XLA Modules:
  0.0 75.9 jit_solution(3656156937963562975)
XLA Ops:
  0.6 3.0 %collective-permute-start = (bf16[64,1152]{1,0:T(8,128)(2,1)}, bf16[64,1152]{1,0:T(8,128)(2,1)S(1)}, u32[]{:S(2)}, u32[]{:S(2)}) collective-permute-start(bf16[64,1152]{1,0:T(8,128)(2,1)} %refs_1_.3), channel_id=1, source_target_pairs={{0,8},{8,0},{16,24},{24,16},{1,9},{9,1},{17,25},{25,17},{2,10},{10... | collective-permute-start | bytes 442376 | tf_op jit(solution)/shard_map/ppermute | solution.py:279
  3.6 1.5 %collective-permute-start.1 = (bf16[64,1152]{1,0:T(8,128)(2,1)}, bf16[64,1152]{1,0:T(8,128)(2,1)S(1)}, u32[]{:S(2)}, u32[]{:S(2)}) collective-permute-start(bf16[64,1152]{1,0:T(8,128)(2,1)} %refs_1_.3), channel_id=1, source_target_pairs={{0,16},{8,24},{16,0},{24,8},{1,17},{9,25},{17,1},{25,9},{2,18},{10... | collective-permute-start | bytes 442376 | tf_op jit(solution)/shard_map/ppermute | solution.py:279
  5.2 2.0 %collective-permute-start.3 = (bf16[64,1152]{1,0:T(8,128)(2,1)}, bf16[64,1152]{1,0:T(8,128)(2,1)S(1)}, u32[]{:S(2)}, u32[]{:S(2)}) collective-permute-start(bf16[64,1152]{1,0:T(8,128)(2,1)} %refs_0_.2), channel_id=1, source_target_pairs={{0,2},{2,0},{4,6},{6,4},{1,3},{3,1},{5,7},{7,5},{8,10},{10,8},{12,... | collective-permute-start | bytes 442376 | tf_op jit(solution)/shard_map/ppermute | solution.py:279
  7.2 2.6 %collective-permute-start.4 = (bf16[64,1152]{1,0:T(8,128)(2,1)}, bf16[64,1152]{1,0:T(8,128)(2,1)S(1)}, u32[]{:S(2)}, u32[]{:S(2)}) collective-permute-start(bf16[64,1152]{1,0:T(8,128)(2,1)} %refs_0_.2), channel_id=1, source_target_pairs={{0,4},{2,6},{4,0},{6,2},{1,5},{3,7},{5,1},{7,3},{8,12},{10,14},{12... | collective-permute-start | bytes 442376 | tf_op jit(solution)/shard_map/ppermute | solution.py:279
  13.5 1.9 %collective-permute-start.7 = (bf16[64,1152]{1,0:T(8,128)(2,1)S(1)}, bf16[64,1152]{1,0:T(8,128)(2,1)S(1)}, u32[]{:S(2)}, u32[]{:S(2)}) collective-permute-start(bf16[64,1152]{1,0:T(8,128)(2,1)S(1)} %get-tuple-element.44.refs_0_.refs_2_), channel_id=1, source_target_pairs={{0,8},{8,0},{16,24},{24,16},{1,9},{9,1},{17,25},{25,17},{2,10},{10... | collective-permute-start | bytes 442376 | tf_op jit(solution)/shard_map/ppermute | solution.py:279
  15.4 1.5 %collective-permute-start.8 = (bf16[64,1152]{1,0:T(8,128)(2,1)S(1)}, bf16[64,1152]{1,0:T(8,128)(2,1)S(1)}, u32[]{:S(2)}, u32[]{:S(2)}) collective-permute-start(bf16[64,1152]{1,0:T(8,128)(2,1)S(1)} %get-tuple-element.44.refs_0_.refs_2_), channel_id=1, source_target_pairs={{0,16},{8,24},{16,0},{24,8},{1,17},{9,25},{17,1},{25,9},{2,18},{10... | collective-permute-start | bytes 442376 | tf_op jit(solution)/shard_map/ppermute | solution.py:279
  17.0 3.3 %collective-permute-done.4.refs_2_ = bf16[64,1152]{1,0:T(8,128)(2,1)S(1)} collective-permute-done((bf16[64,1152]{1,0:T(8,128)(2,1)}, bf16[64,1152]{1,0:T(8,128)(2,1)S(1)}, u32[]{:S(2)}, u32[]{:S(2)}) %collective-permute-start.4) | collective-permute-done | bytes 147488 | tf_op jit(solution)/shard_map/ppermute | solution.py:279
  24.0 1.7 %collective-permute-start.11 = (bf16[64,1152]{1,0:T(8,128)(2,1)S(1)}, bf16[64,1152]{1,0:T(8,128)(2,1)S(1)}, u32[]{:S(2)}, u32[]{:S(2)}) collective-permute-start(bf16[64,1152]{1,0:T(8,128)(2,1)S(1)} %shard_map.81), channel_id=1, source_target_pairs={{0,2},{2,0},{4,6},{6,4},{1,3},{3,1},{5,7},{7,5},{8,10},{10,8},{12,... | collective-permute-start | bytes 442376 | tf_op jit(solution)/shard_map/ppermute | solution.py:279
  25.6 1.9 %collective-permute-start.12 = (bf16[64,1152]{1,0:T(8,128)(2,1)S(1)}, bf16[64,1152]{1,0:T(8,128)(2,1)S(1)}, u32[]{:S(2)}, u32[]{:S(2)}) collective-permute-start(bf16[64,1152]{1,0:T(8,128)(2,1)S(1)} %get-tuple-element.52), channel_id=1, source_target_pairs={{0,4},{2,6},{4,0},{6,2},{1,5},{3,7},{5,1},{7,3},{8,12},{10,14},{12... | collective-permute-start | bytes 442376 | tf_op jit(solution)/shard_map/ppermute | solution.py:279
  28.5 1.6 %collective-permute-start.14 = (bf16[64,1152]{1,0:T(8,128)(2,1)S(1)}, bf16[64,1152]{1,0:T(8,128)(2,1)S(1)}, u32[]{:S(2)}, u32[]{:S(2)}) collective-permute-start(bf16[64,1152]{1,0:T(8,128)(2,1)S(1)} %get-tuple-element.49.refs_10_), channel_id=1, source_target_pairs={{0,8},{8,0},{16,24},{24,16},{1,9},{9,1},{17,25},{25,17},{2,10},{10... | collective-permute-start | bytes 442376 | tf_op jit(solution)/shard_map/ppermute | solution.py:279
  30.1 1.5 %collective-permute-start.15 = (bf16[64,1152]{1,0:T(8,128)(2,1)S(1)}, bf16[64,1152]{1,0:T(8,128)(2,1)S(1)}, u32[]{:S(2)}, u32[]{:S(2)}) collective-permute-start(bf16[64,1152]{1,0:T(8,128)(2,1)S(1)} %get-tuple-element.56), channel_id=1, source_target_pairs={{0,16},{8,24},{16,0},{24,8},{1,17},{9,25},{17,1},{25,9},{2,18},{10... | collective-permute-start | bytes 442376 | tf_op jit(solution)/shard_map/ppermute | solution.py:279
  32.9 2.5 %collective-permute-start.16 = (bf16[64,1152]{1,0:T(8,128)(2,1)S(1)}, bf16[64,1152]{1,0:T(8,128)(2,1)S(1)}, u32[]{:S(2)}, u32[]{:S(2)}) collective-permute-start(bf16[64,1152]{1,0:T(8,128)(2,1)S(1)} %get-tuple-element.57), channel_id=1, source_target_pairs={{0,24},{8,16},{16,8},{24,0},{1,25},{9,17},{17,9},{25,1},{2,26},{10... | collective-permute-start | bytes 442376 | tf_op jit(solution)/shard_map/ppermute | solution.py:279
  36.5 3.1 %collective-permute-done.12.refs_3_ = bf16[64,1152]{1,0:T(8,128)(2,1)S(1)} collective-permute-done((bf16[64,1152]{1,0:T(8,128)(2,1)S(1)}, bf16[64,1152]{1,0:T(8,128)(2,1)S(1)}, u32[]{:S(2)}, u32[]{:S(2)}) %collective-permute-start.12) | collective-permute-done | bytes 147488 | tf_op jit(solution)/shard_map/ppermute | solution.py:279
  40.0 2.5 %collective-permute-start.17 = (bf16[64,640]{1,0:T(8,128)(2,1)S(1)}, bf16[64,640]{1,0:T(8,128)(2,1)S(1)}, u32[]{:S(2)}, u32[]{:S(2)}) collective-permute-start(bf16[64,640]{1,0:T(8,128)(2,1)S(1)} %get-tuple-element.64), channel_id=1, source_target_pairs={{0,24},{8,16},{16,8},{24,0},{1,25},{9,17},{17,9},{25,1},{2,26},{10... | collective-permute-start | bytes 245768 | tf_op jit(solution)/shard_map/ppermute | solution.py:279
  43.6 2.4 %shard_map.83 = (bf16[64,1152]{1,0:T(8,128)(2,1)}, bf16[64,1152]{1,0:T(8,128)(2,1)}, f32[8,128]{1,0:T(8,128)S(1)}) custom-call(bf16[64,1152]{1,0:T(8,128)(2,1)S(1)} %get-tuple-element.58.refs_0_, bf16[1152,1152]{1,0:T(8,128)(2,1)S(1)} %copy-done.1, bf16[64,1152]{1,0:T(8,128)(2,1)S(1)} %get-tuple-element.59.refs_2_, bf16[1152,1152]{1,0:T(8,128)(2,1)S(1)} %copy-done, ...), custom_call_target="tpu_custom_call" | custom-call | flops 1000000000 | bytes 1000000000 | tf_op jit(solution)/shard_map/pallas_call | solution.py:44
  49.7 2.5 %collective-permute-start.23 = (bf16[144,384]{1,0:T(8,128)(2,1)S(1)}, bf16[144,384]{1,0:T(8,128)(2,1)S(1)}, u32[]{:S(2)}, u32[]{:S(2)}) collective-permute-start(bf16[144,384]{1,0:T(8,128)(2,1)S(1)} %get-tuple-element.74), channel_id=1, source_target_pairs={{0,6},{2,4},{4,2},{6,0},{1,7},{3,5},{5,3},{7,1},{8,14},{10,12},{12... | collective-permute-start | bytes 331784 | tf_op jit(solution)/shard_map/ppermute | solution.py:279
  52.3 2.0 %collective-permute-start.24 = (bf16[144,384]{1,0:T(8,128)(2,1)S(1)}, bf16[144,384]{1,0:T(8,128)(2,1)S(1)}, u32[]{:S(2)}, u32[]{:S(2)}) collective-permute-start(bf16[144,384]{1,0:T(8,128)(2,1)S(1)} %get-tuple-element.71.refs_6_), channel_id=1, source_target_pairs={{0,4},{2,6},{4,0},{6,2},{1,5},{3,7},{5,1},{7,3},{8,12},{10,14},{12... | collective-permute-start | bytes 331784 | tf_op jit(solution)/shard_map/ppermute | solution.py:279
  54.9 2.0 %collective-permute-start.22 = (bf16[216,384]{1,0:T(8,128)(2,1)S(1)}, bf16[216,384]{1,0:T(8,128)(2,1)S(1)}, u32[]{:S(2)}, u32[]{:S(2)}) collective-permute-start(bf16[216,384]{1,0:T(8,128)(2,1)S(1)} %get-tuple-element.73), channel_id=1, source_target_pairs={{0,2},{2,0},{4,6},{6,4},{1,3},{3,1},{5,7},{7,5},{8,10},{10,8},{12,... | collective-permute-start | bytes 497672 | tf_op jit(solution)/shard_map/ppermute | solution.py:279
  56.9 2.3 %collective-permute-done.28.refs_1_ = bf16[216,128]{1,0:T(8,128)(2,1)S(1)} collective-permute-done((bf16[216,128]{1,0:T(8,128)(2,1)S(1)}, bf16[216,128]{1,0:T(8,128)(2,1)S(1)}, u32[]{:S(2)}, u32[]{:S(2)}) %collective-permute-start.28) | collective-permute-done | bytes 55328 | tf_op jit(solution)/shard_map/ppermute | solution.py:279
  59.2 3.3 %collective-permute-start.29 = (bf16[216,128]{1,0:T(8,128)(2,1)S(1)}, bf16[216,128]{1,0:T(8,128)(2,1)S(1)}, u32[]{:S(2)}, u32[]{:S(2)}) collective-permute-start(bf16[216,128]{1,0:T(8,128)(2,1)S(1)} %shard_map.92), channel_id=1, source_target_pairs={{0,4},{2,6},{4,0},{6,2},{1,5},{3,7},{5,1},{7,3},{8,12},{10,14},{12... | collective-permute-start | bytes 165896 | tf_op jit(solution)/shard_map/ppermute | solution.py:279
  62.5 1.9 %collective-permute-done.24.refs_1_ = bf16[144,384]{1,0:T(8,128)(2,1)S(1)} collective-permute-done((bf16[144,384]{1,0:T(8,128)(2,1)S(1)}, bf16[144,384]{1,0:T(8,128)(2,1)S(1)}, u32[]{:S(2)}, u32[]{:S(2)}) %collective-permute-start.24) | collective-permute-done | bytes 110624 | tf_op jit(solution)/shard_map/ppermute | solution.py:279
  65.0 1.6 %collective-permute-start.26 = (bf16[144,384]{1,0:T(8,128)(2,1)S(1)}, bf16[144,384]{1,0:T(8,128)(2,1)S(1)}, u32[]{:S(2)}, u32[]{:S(2)}) collective-permute-start(bf16[144,384]{1,0:T(8,128)(2,1)S(1)} %shard_map.91.refs_0_), channel_id=1, source_target_pairs={{0,16},{8,24},{16,0},{24,8},{1,17},{9,25},{17,1},{25,9},{2,18},{10... | collective-permute-start | bytes 331784 | tf_op jit(solution)/shard_map/ppermute | solution.py:279
  66.6 1.4 %collective-permute-start.27 = (bf16[144,384]{1,0:T(8,128)(2,1)S(1)}, bf16[144,384]{1,0:T(8,128)(2,1)S(1)}, u32[]{:S(2)}, u32[]{:S(2)}) collective-permute-start(bf16[144,384]{1,0:T(8,128)(2,1)S(1)} %shard_map.91.refs_0_), channel_id=1, source_target_pairs={{0,24},{8,16},{16,8},{24,0},{1,25},{9,17},{17,9},{25,1},{2,26},{10... | collective-permute-start | bytes 331784 | tf_op jit(solution)/shard_map/ppermute | solution.py:279
  68.1 1.6 %collective-permute-start.31 = (bf16[216,128]{1,0:T(8,128)(2,1)S(1)}, bf16[216,128]{1,0:T(8,128)(2,1)S(1)}, u32[]{:S(2)}, u32[]{:S(2)}) collective-permute-start(bf16[216,128]{1,0:T(8,128)(2,1)S(1)} %shard_map.93.refs_0_.refs_4_), channel_id=1, source_target_pairs={{0,16},{8,24},{16,0},{24,8},{1,17},{9,25},{17,1},{25,9},{2,18},{10... | collective-permute-start | bytes 165896 | tf_op jit(solution)/shard_map/ppermute | solution.py:279
  (70 shorter events, 23.4 us)
Async XLA Ops:
  0.6 11.0 %collective-permute-start = (bf16[64,1152]{1,0:T(8,128)(2,1)}, bf16[64,1152]{1,0:T(8,128)(2,1)S(1)}, u32[]{:S(2)}, u32[]{:S(2)}) collective-permute-start(bf16[64,1152]{1,0:T(8,128)(2,1)} %refs_1_.3), channel_id=1, source_target_pairs={{0,8},{8,0},{16,24},{24,16},{1,9},{9,1},{17,25},{25,17},{2,10},{10... | collective-permute-start | bytes 442376 | tf_op jit(solution)/shard_map/ppermute | solution.py:279
  3.6 8.7 %collective-permute-start.1 = (bf16[64,1152]{1,0:T(8,128)(2,1)}, bf16[64,1152]{1,0:T(8,128)(2,1)S(1)}, u32[]{:S(2)}, u32[]{:S(2)}) collective-permute-start(bf16[64,1152]{1,0:T(8,128)(2,1)} %refs_1_.3), channel_id=1, source_target_pairs={{0,16},{8,24},{16,0},{24,8},{1,17},{9,25},{17,1},{25,9},{2,18},{10... | collective-permute-start | bytes 442376 | tf_op jit(solution)/shard_map/ppermute | solution.py:279
  5.2 7.2 %collective-permute-start.2 = (bf16[64,1152]{1,0:T(8,128)(2,1)}, bf16[64,1152]{1,0:T(8,128)(2,1)S(1)}, u32[]{:S(2)}, u32[]{:S(2)}) collective-permute-start(bf16[64,1152]{1,0:T(8,128)(2,1)} %refs_1_.3), channel_id=1, source_target_pairs={{0,24},{8,16},{16,8},{24,0},{1,25},{9,17},{17,9},{25,1},{2,26},{10... | collective-permute-start | bytes 442376 | tf_op jit(solution)/shard_map/ppermute | solution.py:279
  5.2 11.7 %collective-permute-start.3 = (bf16[64,1152]{1,0:T(8,128)(2,1)}, bf16[64,1152]{1,0:T(8,128)(2,1)S(1)}, u32[]{:S(2)}, u32[]{:S(2)}) collective-permute-start(bf16[64,1152]{1,0:T(8,128)(2,1)} %refs_0_.2), channel_id=1, source_target_pairs={{0,2},{2,0},{4,6},{6,4},{1,3},{3,1},{5,7},{7,5},{8,10},{10,8},{12,... | collective-permute-start | bytes 442376 | tf_op jit(solution)/shard_map/ppermute | solution.py:279
  7.2 13.1 %collective-permute-start.4 = (bf16[64,1152]{1,0:T(8,128)(2,1)}, bf16[64,1152]{1,0:T(8,128)(2,1)S(1)}, u32[]{:S(2)}, u32[]{:S(2)}) collective-permute-start(bf16[64,1152]{1,0:T(8,128)(2,1)} %refs_0_.2), channel_id=1, source_target_pairs={{0,4},{2,6},{4,0},{6,2},{1,5},{3,7},{5,1},{7,3},{8,12},{10,14},{12... | collective-permute-start | bytes 442376 | tf_op jit(solution)/shard_map/ppermute | solution.py:279
  11.7 8.7 %collective-permute-start.5 = (bf16[64,1152]{1,0:T(8,128)(2,1)}, bf16[64,1152]{1,0:T(8,128)(2,1)S(1)}, u32[]{:S(2)}, u32[]{:S(2)}) collective-permute-start(bf16[64,1152]{1,0:T(8,128)(2,1)} %refs_0_.2), channel_id=1, source_target_pairs={{0,6},{2,4},{4,2},{6,0},{1,7},{3,5},{5,3},{7,1},{8,14},{10,12},{12... | collective-permute-start | bytes 442376 | tf_op jit(solution)/shard_map/ppermute | solution.py:279
  13.5 10.5 %collective-permute-start.7 = (bf16[64,1152]{1,0:T(8,128)(2,1)S(1)}, bf16[64,1152]{1,0:T(8,128)(2,1)S(1)}, u32[]{:S(2)}, u32[]{:S(2)}) collective-permute-start(bf16[64,1152]{1,0:T(8,128)(2,1)S(1)} %get-tuple-element.44.refs_0_.refs_2_), channel_id=1, source_target_pairs={{0,8},{8,0},{16,24},{24,16},{1,9},{9,1},{17,25},{25,17},{2,10},{10... | collective-permute-start | bytes 442376 | tf_op jit(solution)/shard_map/ppermute | solution.py:279
  15.4 8.5 %collective-permute-start.8 = (bf16[64,1152]{1,0:T(8,128)(2,1)S(1)}, bf16[64,1152]{1,0:T(8,128)(2,1)S(1)}, u32[]{:S(2)}, u32[]{:S(2)}) collective-permute-start(bf16[64,1152]{1,0:T(8,128)(2,1)S(1)} %get-tuple-element.44.refs_0_.refs_2_), channel_id=1, source_target_pairs={{0,16},{8,24},{16,0},{24,8},{1,17},{9,25},{17,1},{25,9},{2,18},{10... | collective-permute-start | bytes 442376 | tf_op jit(solution)/shard_map/ppermute | solution.py:279
  16.9 7.0 %collective-permute-start.9 = (bf16[64,1152]{1,0:T(8,128)(2,1)S(1)}, bf16[64,1152]{1,0:T(8,128)(2,1)S(1)}, u32[]{:S(2)}, u32[]{:S(2)}) collective-permute-start(bf16[64,1152]{1,0:T(8,128)(2,1)S(1)} %get-tuple-element.44.refs_0_.refs_2_), channel_id=1, source_target_pairs={{0,24},{8,16},{16,8},{24,0},{1,25},{9,17},{17,9},{25,1},{2,26},{10... | collective-permute-start | bytes 442376 | tf_op jit(solution)/shard_map/ppermute | solution.py:279
  24.0 8.9 %collective-permute-start.11 = (bf16[64,1152]{1,0:T(8,128)(2,1)S(1)}, bf16[64,1152]{1,0:T(8,128)(2,1)S(1)}, u32[]{:S(2)}, u32[]{:S(2)}) collective-permute-start(bf16[64,1152]{1,0:T(8,128)(2,1)S(1)} %shard_map.81), channel_id=1, source_target_pairs={{0,2},{2,0},{4,6},{6,4},{1,3},{3,1},{5,7},{7,5},{8,10},{10,8},{12,... | collective-permute-start | bytes 442376 | tf_op jit(solution)/shard_map/ppermute | solution.py:279
  25.6 13.9 %collective-permute-start.12 = (bf16[64,1152]{1,0:T(8,128)(2,1)S(1)}, bf16[64,1152]{1,0:T(8,128)(2,1)S(1)}, u32[]{:S(2)}, u32[]{:S(2)}) collective-permute-start(bf16[64,1152]{1,0:T(8,128)(2,1)S(1)} %get-tuple-element.52), channel_id=1, source_target_pairs={{0,4},{2,6},{4,0},{6,2},{1,5},{3,7},{5,1},{7,3},{8,12},{10,14},{12... | collective-permute-start | bytes 442376 | tf_op jit(solution)/shard_map/ppermute | solution.py:279
  27.5 12.1 %collective-permute-start.13 = (bf16[64,1152]{1,0:T(8,128)(2,1)S(1)}, bf16[64,1152]{1,0:T(8,128)(2,1)S(1)}, u32[]{:S(2)}, u32[]{:S(2)}) collective-permute-start(bf16[64,1152]{1,0:T(8,128)(2,1)S(1)} %get-tuple-element.53), channel_id=1, source_target_pairs={{0,6},{2,4},{4,2},{6,0},{1,7},{3,5},{5,3},{7,1},{8,14},{10,12},{12... | collective-permute-start | bytes 442376 | tf_op jit(solution)/shard_map/ppermute | solution.py:279
  28.5 11.0 %collective-permute-start.14 = (bf16[64,1152]{1,0:T(8,128)(2,1)S(1)}, bf16[64,1152]{1,0:T(8,128)(2,1)S(1)}, u32[]{:S(2)}, u32[]{:S(2)}) collective-permute-start(bf16[64,1152]{1,0:T(8,128)(2,1)S(1)} %get-tuple-element.49.refs_10_), channel_id=1, source_target_pairs={{0,8},{8,0},{16,24},{24,16},{1,9},{9,1},{17,25},{25,17},{2,10},{10... | collective-permute-start | bytes 442376 | tf_op jit(solution)/shard_map/ppermute | solution.py:279
  30.1 9.5 %collective-permute-start.15 = (bf16[64,1152]{1,0:T(8,128)(2,1)S(1)}, bf16[64,1152]{1,0:T(8,128)(2,1)S(1)}, u32[]{:S(2)}, u32[]{:S(2)}) collective-permute-start(bf16[64,1152]{1,0:T(8,128)(2,1)S(1)} %get-tuple-element.56), channel_id=1, source_target_pairs={{0,16},{8,24},{16,0},{24,8},{1,17},{9,25},{17,1},{25,9},{2,18},{10... | collective-permute-start | bytes 442376 | tf_op jit(solution)/shard_map/ppermute | solution.py:279
  32.9 6.7 %collective-permute-start.16 = (bf16[64,1152]{1,0:T(8,128)(2,1)S(1)}, bf16[64,1152]{1,0:T(8,128)(2,1)S(1)}, u32[]{:S(2)}, u32[]{:S(2)}) collective-permute-start(bf16[64,1152]{1,0:T(8,128)(2,1)S(1)} %get-tuple-element.57), channel_id=1, source_target_pairs={{0,24},{8,16},{16,8},{24,0},{1,25},{9,17},{17,9},{25,1},{2,26},{10... | collective-permute-start | bytes 442376 | tf_op jit(solution)/shard_map/ppermute | solution.py:279
  40.0 6.0 %collective-permute-start.17 = (bf16[64,640]{1,0:T(8,128)(2,1)S(1)}, bf16[64,640]{1,0:T(8,128)(2,1)S(1)}, u32[]{:S(2)}, u32[]{:S(2)}) collective-permute-start(bf16[64,640]{1,0:T(8,128)(2,1)S(1)} %get-tuple-element.64), channel_id=1, source_target_pairs={{0,24},{8,16},{16,8},{24,0},{1,25},{9,17},{17,9},{25,1},{2,26},{10... | collective-permute-start | bytes 245768 | tf_op jit(solution)/shard_map/ppermute | solution.py:279
  48.4 6.4 %collective-permute-start.21 = (bf16[2,144,640]{2,1,0:T(8,128)(2,1)S(1)}, bf16[2,144,640]{2,1,0:T(8,128)(2,1)S(1)}, u32[]{:S(2)}, u32[]{:S(2)}) collective-permute-start(bf16[2,144,640]{2,1,0:T(8,128)(2,1)S(1)} %shard_map.85.refs_5_), channel_id=1, source_target_pairs={{0,1},{1,0},{2,3},{3,2},{4,5},{5,4},{6,7},{7,6},{8,9},{9,8},{10,11... | collective-permute-start | bytes 1105928 | tf_op jit(solution)/shard_map/ppermute | solution.py:279
  49.7 12.7 %collective-permute-start.23 = (bf16[144,384]{1,0:T(8,128)(2,1)S(1)}, bf16[144,384]{1,0:T(8,128)(2,1)S(1)}, u32[]{:S(2)}, u32[]{:S(2)}) collective-permute-start(bf16[144,384]{1,0:T(8,128)(2,1)S(1)} %get-tuple-element.74), channel_id=1, source_target_pairs={{0,6},{2,4},{4,2},{6,0},{1,7},{3,5},{5,3},{7,1},{8,14},{10,12},{12... | collective-permute-start | bytes 331784 | tf_op jit(solution)/shard_map/ppermute | solution.py:279
  52.3 12.1 %collective-permute-start.24 = (bf16[144,384]{1,0:T(8,128)(2,1)S(1)}, bf16[144,384]{1,0:T(8,128)(2,1)S(1)}, u32[]{:S(2)}, u32[]{:S(2)}) collective-permute-start(bf16[144,384]{1,0:T(8,128)(2,1)S(1)} %get-tuple-element.71.refs_6_), channel_id=1, source_target_pairs={{0,4},{2,6},{4,0},{6,2},{1,5},{3,7},{5,1},{7,3},{8,12},{10,14},{12... | collective-permute-start | bytes 331784 | tf_op jit(solution)/shard_map/ppermute | solution.py:279
  54.9 9.6 %collective-permute-start.22 = (bf16[216,384]{1,0:T(8,128)(2,1)S(1)}, bf16[216,384]{1,0:T(8,128)(2,1)S(1)}, u32[]{:S(2)}, u32[]{:S(2)}) collective-permute-start(bf16[216,384]{1,0:T(8,128)(2,1)S(1)} %get-tuple-element.73), channel_id=1, source_target_pairs={{0,2},{2,0},{4,6},{6,4},{1,3},{3,1},{5,7},{7,5},{8,10},{10,8},{12,... | collective-permute-start | bytes 497672 | tf_op jit(solution)/shard_map/ppermute | solution.py:279
  59.2 8.9 %collective-permute-start.29 = (bf16[216,128]{1,0:T(8,128)(2,1)S(1)}, bf16[216,128]{1,0:T(8,128)(2,1)S(1)}, u32[]{:S(2)}, u32[]{:S(2)}) collective-permute-start(bf16[216,128]{1,0:T(8,128)(2,1)S(1)} %shard_map.92), channel_id=1, source_target_pairs={{0,4},{2,6},{4,0},{6,2},{1,5},{3,7},{5,1},{7,3},{8,12},{10,14},{12... | collective-permute-start | bytes 165896 | tf_op jit(solution)/shard_map/ppermute | solution.py:279
  64.5 5.9 %collective-permute-start.25 = (bf16[144,384]{1,0:T(8,128)(2,1)S(1)}, bf16[144,384]{1,0:T(8,128)(2,1)S(1)}, u32[]{:S(2)}, u32[]{:S(2)}) collective-permute-start(bf16[144,384]{1,0:T(8,128)(2,1)S(1)} %shard_map.91.refs_0_), channel_id=1, source_target_pairs={{0,8},{8,0},{16,24},{24,16},{1,9},{9,1},{17,25},{25,17},{2,10},{10... | collective-permute-start | bytes 331784 | tf_op jit(solution)/shard_map/ppermute | solution.py:279
  65.0 7.4 %collective-permute-start.26 = (bf16[144,384]{1,0:T(8,128)(2,1)S(1)}, bf16[144,384]{1,0:T(8,128)(2,1)S(1)}, u32[]{:S(2)}, u32[]{:S(2)}) collective-permute-start(bf16[144,384]{1,0:T(8,128)(2,1)S(1)} %shard_map.91.refs_0_), channel_id=1, source_target_pairs={{0,16},{8,24},{16,0},{24,8},{1,17},{9,25},{17,1},{25,9},{2,18},{10... | collective-permute-start | bytes 331784 | tf_op jit(solution)/shard_map/ppermute | solution.py:279
  66.6 6.8 %collective-permute-start.27 = (bf16[144,384]{1,0:T(8,128)(2,1)S(1)}, bf16[144,384]{1,0:T(8,128)(2,1)S(1)}, u32[]{:S(2)}, u32[]{:S(2)}) collective-permute-start(bf16[144,384]{1,0:T(8,128)(2,1)S(1)} %shard_map.91.refs_0_), channel_id=1, source_target_pairs={{0,24},{8,16},{16,8},{24,0},{1,25},{9,17},{17,9},{25,1},{2,26},{10... | collective-permute-start | bytes 331784 | tf_op jit(solution)/shard_map/ppermute | solution.py:279
  (12 other events, 58.1 us)
